TPU v7x, 512 devices: a whole 4x4x16 slice. The times are simulated.
512 devices in a mesh: tile: 16 (over y, x_hi, core), mode: 32 (over x_lo, z).
Axes of the slice: x: 4 (x_hi: 2, x_lo: 2; x = x_hi * 2 + x_lo), y: 4, z: 16, core: 2. Of those that a mesh axis runs over, the one named last changes fastest.
Arguments:
- object_field: float32 [2, 8192, 512], P(None, ('tile', 'mode')), may hold values from -5 to 5
- probe_modes: float32 [32, 2, 256, 256], P('mode'), may hold values from -4 to 4
- measured_amplitude: float32 [16, 8, 256, 256], P('tile'), may hold values from 1 to 16
- row_offsets: int32 [16, 8], P('tile'), may hold values from 0 to 511
- col_offsets: int32 [16, 8], P('tile'), may hold values from 0 to 256
- position_counts: int32 [16], replicated, may hold values from 1 to 8, 96 in all
Outputs:
- updated_object: float32 [2, 8192, 512], P(None, ('tile', 'mode'))
Inputs may be any that keep to these rules, and one draw needn't show every extreme that they name: Tile t uses its first position_counts[t] slots; some tile uses all 8.
All inputs are finite; a program needn't handle non-finite values.
Results may differ from a plain program's by a relative error of at most 0.0021.
Values may be sent and summed in bfloat16 or wider, within the bound.
No kernel may reach another device: no remote copies, remote signals or barrier semaphores. Data moves between devices by JAX's collectives and lax.ppermute only.
A program may use at most 64 MiB of HBM per device.

v0:
```python
import math

import jax
import jax.numpy as jnp
from jax import lax
from jax.sharding import PartitionSpec as P

step_size = 0.05


def shifted(block, axis, distance):
    devices = range(lax.axis_size(axis))
    route = [(i - distance, i) for i in devices if i - distance in devices]
    return lax.ppermute(block, axis, route)


def dft_tables(length):
    freqs = jnp.arange(length, dtype=jnp.int32)
    turns = freqs[:, None] * freqs[None, :] % length
    phase = turns.astype(jnp.float32) * (2.0 * math.pi / length)
    norm_scale = 1.0 / math.sqrt(length)
    return (
        (jnp.cos(phase) * norm_scale).astype(jnp.bfloat16),
        (-jnp.sin(phase) * norm_scale).astype(jnp.bfloat16),
    )


def right_product(real_in, imag_in, cos_table, sin_table):

    def prod(left_side, right_side):
        return jnp.einsum("pij,jk->pik", left_side, right_side, preferred_element_type=jnp.float32)

    return (
        prod(real_in, cos_table) - prod(imag_in, sin_table),
        prod(real_in, sin_table) + prod(imag_in, cos_table),
    )


def left_product(real_in, imag_in, cos_table, sin_table):

    def prod(left_side, right_side):
        return jnp.einsum("ki,pij->pkj", left_side, right_side, preferred_element_type=jnp.float32)

    return (
        prod(cos_table, real_in) - prod(sin_table, imag_in),
        prod(sin_table, real_in) + prod(cos_table, imag_in),
    )


def on_device(
    object_field, probe_modes, measured_amplitude, row_offsets, col_offsets, position_counts
):
    window = probe_modes.shape[-1]
    slots = row_offsets.shape[1]
    tile_width = object_field.shape[2]
    cos_table, sin_table = dft_tables(window)
    back_sin = -sin_table
    half_object = object_field.astype(jnp.bfloat16)
    tile_half = lax.all_gather(half_object, "mode", axis=1, tiled=True)
    below = shifted(tile_half[:, :window], "tile", -1)
    extended = jnp.concatenate([tile_half, below], axis=1)
    row_starts = row_offsets[0]
    col_starts = col_offsets[0]
    zero_index = jnp.zeros((), jnp.int32)

    def cut_patch(row_start, col_start):
        return lax.dynamic_slice(extended, (zero_index, row_start, col_start), (2, window, window))

    patches = jax.vmap(cut_patch)(row_starts, col_starts).astype(jnp.float32)
    probe = probe_modes[0]
    exit_real = (probe[0] * patches[:, 0] - probe[1] * patches[:, 1]).astype(jnp.bfloat16)
    exit_imag = (probe[0] * patches[:, 1] + probe[1] * patches[:, 0]).astype(jnp.bfloat16)
    half_real, half_imag = right_product(exit_real, exit_imag, cos_table, sin_table)
    spec_real, spec_imag = left_product(
        half_real.astype(jnp.bfloat16), half_imag.astype(jnp.bfloat16), cos_table, sin_table
    )
    local_power = spec_real * spec_real + spec_imag * spec_imag
    amplitude = measured_amplitude[0]
    intensity = lax.psum(local_power, "mode")
    correction = 1.0 - amplitude / jnp.sqrt(intensity + 1.0)
    alive_mask = (
        jnp.arange(slots, dtype=jnp.int32) < position_counts[lax.axis_index("tile")]
    ).astype(jnp.float32)
    factor = alive_mask[:, None, None] * correction
    wave_real = (spec_real * factor).astype(jnp.bfloat16)
    wave_imag = (spec_imag * factor).astype(jnp.bfloat16)
    back_real, back_imag = right_product(wave_real, wave_imag, cos_table, back_sin)
    grad_real, grad_imag = left_product(
        back_real.astype(jnp.bfloat16), back_imag.astype(jnp.bfloat16), cos_table, back_sin
    )
    terms = jnp.stack(
        [probe[0] * grad_real + probe[1] * grad_imag, probe[0] * grad_imag - probe[1] * grad_real],
        axis=1,
    )

    def place_term(position, gradient):
        row_start = row_starts[position]
        col_start = col_starts[position]
        current = lax.dynamic_slice(
            gradient, (zero_index, row_start, col_start), (2, window, window)
        )
        return lax.dynamic_update_slice(
            gradient, current + terms[position], (zero_index, row_start, col_start)
        )

    start_grad = jnp.zeros((2, tile_width + window, tile_width), jnp.float32)
    gradient = lax.fori_loop(0, slots, place_term, start_grad)
    incoming = shifted(gradient[:, tile_width:], "tile", 1)
    tile_grad = jnp.concatenate(
        [gradient[:, :window] + incoming, gradient[:, window:tile_width]], axis=1
    )
    owned = lax.psum_scatter(tile_grad, "mode", scatter_dimension=1, tiled=True)
    return object_field - step_size * owned


def solution(mesh):
    placed = (
        P(None, ("tile", "mode"), None),
        P("mode", None, None, None),
        P("tile", None, None, None),
        P("tile", None),
        P("tile", None),
        P(),
    )
    return jax.shard_map(
        on_device,
        mesh=mesh,
        in_specs=placed,
        out_specs=P(None, ("tile", "mode"), None),
        check_vma=False,
    )
```

profile of v0, /device:TPU:16, one launch (start us, length us, event | category | flops | bytes accessed | tf_op | source)
XLA Modules:
  0.0 745.2 jit_solution(12373841539828667383)
XLA Ops:
  6.5 1.5 convert_element_type.104
  8.1 137.6 %all-gather.2.cloned.1.call-done = bf16[2,512,512]{2,1,0:T(8,128)(2,1)} async-done(((bf16[2,16,512]{2,1,0:T(8,128)(2,1)}), bf16[2,512,512]{2,1,0:T(8,128)(2,1)}) %all-gather.2.cloned.1.call-update) | async-done | bytes 1048592 | tf_op jit(solution)/shard_map/all_gather | solution.py:59
  145.7 1.2 slice.57
  146.9 1.9 collective-permute-start
  150.9 4.6 collective-permute-done
  155.5 1.1 pad_maximum_fusion.2
  156.6 23.8 %while.15 = (s32[]{:T(128)}, bf16[2,768,512]{2,1,0:T(8,128)(2,1)S(1)}, s32[8,3]{0,1:T(4,128)S(1)}, bf16[8,2,256,256]{2,3,0,1:T(8,128)(2,1)}, s32[]{:T(128)}) while((s32[]{:T(128)}, bf16[2,768,512]{2,1,0:T(8,128)(2,1)S(1)}, s32[8,3]{0,1:T(4,128)S(1)}, bf16[8,2,256,256]{2,3,0,1:T(8,128)(2,1)}, s32[]{:T(128)}) %tuple.50), condition=%wide.while_cond, body=%wide.while_body.sunk | while | flops 2 | bytes 1572989 | solution.py:67
  157.3 1.4 dynamic-slice_bitcast_fusion.2
  160.3 1.4 dynamic-slice_bitcast_fusion.2
  163.2 1.4 dynamic-slice_bitcast_fusion.2
  166.2 1.4 dynamic-slice_bitcast_fusion.2
  169.2 1.4 dynamic-slice_bitcast_fusion.2
  172.2 1.4 dynamic-slice_bitcast_fusion.2
  175.1 1.4 dynamic-slice_bitcast_fusion.2
  178.1 1.4 dynamic-slice_bitcast_fusion.2
  180.4 2.1 convert_element_type.105
  183.1 1.4 fusion.25
  184.5 1.4 fusion.38
  185.9 1.4 subtract_convert_fusion.1
  187.3 1.4 fusion.22
  188.7 1.4 fusion.36
  190.1 1.4 add_convert_fusion.1
  191.5 1.4 convolution_subtract_fusion.1
  192.9 3.7 fusion.4
  196.7 3.0 copy.16
  201.1 253.3 %all-reduce.2.cloned.1.call-done = f32[8,256,256]{1,2,0:T(8,128)} async-done(((f32[8,256,256]{1,2,0:T(8,128)}), f32[8,256,256]{1,2,0:T(8,128)}) %all-reduce.2.cloned.1.call-update) | async-done | bytes 2097168 | tf_op jit(solution)/shard_map/psum | solution.py:79
  454.3 3.6 fusion.5
  457.9 1.4 fusion.19
  459.4 1.4 fusion.32
  460.8 1.4 subtract_convert_fusion
  462.2 1.4 fusion.16
  463.6 1.4 fusion.30
  465.0 1.4 add_convert_fusion
  466.4 1.4 convolution_add_fusion
  467.8 2.0 fusion.1
  469.8 2.4 pad_maximum_fusion
  472.2 2.1 broadcast_in_dim.2
  474.3 110.0 %while.14 = (s32[]{:T(128)}, f32[2,768,512]{2,1,0:T(8,128)}, s32[8]{0:T(128)S(1)}, s32[8]{0:T(128)S(1)}, f32[8,2,256,256]{2,3,0,1:T(8,128)}, /*index=5*/s32[]{:T(128)}, s32[]{:T(128)}, s32[]{:T(128)}, s32[]{:T(128)}) while((s32[]{:T(128)}, f32[2,768,512]{2,1,0:T(8,128)}, s32[8]{0:T(128)S(1)}, s32[8]{0:T(128)S(1)}, ...), condition=%wide.region_2.3_spmd, body=%wide.region_1.2_spmd.sunk | while | flops 131080 | bytes 4718801 | solution.py:107
  478.8 1.1 constant_dynamic-slice_fusion.4
  480.1 1.4 bitcast_add_fusion.2
  481.5 6.5 dynamic_update_slice.8
  492.5 1.1 constant_dynamic-slice_fusion.4
  493.8 1.4 bitcast_add_fusion.2
  495.1 6.5 dynamic_update_slice.8
  506.2 1.1 constant_dynamic-slice_fusion.4
  507.4 1.4 bitcast_add_fusion.2
  508.8 6.6 dynamic_update_slice.8
  521.2 1.4 bitcast_add_fusion.2
  522.6 6.6 dynamic_update_slice.8
  535.0 1.4 bitcast_add_fusion.2
  536.3 6.8 dynamic_update_slice.8
  548.9 1.4 bitcast_add_fusion.2
  550.3 6.5 dynamic_update_slice.8
  562.6 1.4 bitcast_add_fusion.2
  564.0 6.6 dynamic_update_slice.8
  576.3 1.4 bitcast_add_fusion.2
  577.7 6.6 dynamic_update_slice.8
  584.3 1.3 slice.40
  585.6 1.9 collective-permute-start.1
  587.5 16.6 %collective-permute-done.1 = f32[2,256,512]{2,1,0:T(8,128)S(1)} collective-permute-done((f32[2,256,512]{2,1,0:T(8,128)S(1)}, f32[2,256,512]{2,1,0:T(8,128)S(1)}, u32[]{:S(2)}, u32[]{:S(2)}) %collective-permute-start.1) | collective-permute-done | bytes 1048608 | tf_op jit(solution)/shard_map/ppermute | solution.py:14
  604.1 1.9 slice_add_fusion
  606.0 1.5 pad_maximum_fusion.1
  607.5 129.7 %reduce-scatter.2.cloned.1.call-done = f32[2,16,512]{2,1,0:T(8,128)} async-done(((f32[2,512,512]{2,1,0:T(8,128)}), f32[2,16,512]{2,1,0:T(8,128)}) %reduce-scatter.2.cloned.1.call-update) | async-done | bytes 65552 | tf_op jit(solution)/shard_map/reduce_scatter | solution.py:112
  737.2 1.5 multiply_subtract_fusion
  (89 shorter events, 32.4 us)
Async XLA Ops:
  6.5 144.3 %copy-start.3 = (s32[1,8]{1,0:T(1,128)S(1)}, s32[1,8]{1,0:T(1,128)}, u32[]{:S(2)}) copy-start(s32[1,8]{1,0:T(1,128)} %param.12) | copy-start | bytes 100
  6.5 144.3 %copy-start.4 = (s32[1,8]{1,0:T(1,128)S(1)}, s32[1,8]{1,0:T(1,128)}, u32[]{:S(2)}) copy-start(s32[1,8]{1,0:T(1,128)} %param.11) | copy-start | bytes 100
  6.5 139.2 %all-gather.2.cloned.1.call-start = ((), (), s32[]{:S(2)}) async-start(), calls=%async_computation.1 | async-start | bytes 1081344 | tf_op jit(solution)/shard_map/all_gather | solution.py:59
  8.0 446.3 %all-reduce.2.cloned.1.call-start = ((), (), s32[]{:S(2)}) async-start(), calls=%async_computation.2 | async-start | bytes 4194304 | tf_op jit(solution)/shard_map/psum | solution.py:79
  145.7 9.8 %copy-start = (bf16[2,512,512]{2,1,0:T(8,128)(2,1)S(1)}, bf16[2,512,512]{2,1,0:T(8,128)(2,1)}, u32[]{:S(2)}) copy-start(bf16[2,512,512]{2,1,0:T(8,128)(2,1)} %all-gather.2.cloned.1.call-done) | copy-start | bytes 3145732
  146.9 8.6 %collective-permute-start = (bf16[2,256,512]{2,1,0:T(8,128)(2,1)S(1)}, bf16[2,256,512]{2,1,0:T(8,128)(2,1)}, u32[]{:S(2)}, u32[]{:S(2)}) collective-permute-start(bf16[2,256,512]{2,1,0:T(8,128)(2,1)S(1)} %slice.57), channel_id=1, source_target_pairs={{32,0},{64,32},{96,64},{128,96},{160,128},{192,160},{224,192},{256... | collective-permute-start | bytes 1572872 | tf_op jit(solution)/shard_map/ppermute | solution.py:14
  180.4 2.1 copy-start.1
  196.7 540.5 %reduce-scatter.2.cloned.1.call-start = ((), (), s32[]{:S(2)}) async-start(), calls=%async_computation.3 | async-start | bytes 2162688 | tf_op jit(solution)/shard_map/reduce_scatter | solution.py:112
  196.7 3.0 copy-start.5
  585.6 18.5 %collective-permute-start.1 = (f32[2,256,512]{2,1,0:T(8,128)S(1)}, f32[2,256,512]{2,1,0:T(8,128)S(1)}, u32[]{:S(2)}, u32[]{:S(2)}) collective-permute-start(f32[2,256,512]{2,1,0:T(8,128)S(1)} %slice.40), channel_id=1, source_target_pairs={{0,32},{32,64},{64,96},{96,128},{128,160},{160,192},{192,224},{224... | collective-permute-start | bytes 3145736 | tf_op jit(solution)/shard_map/ppermute | solution.py:14
  607.5 129.8 %copy-start.2 = (f32[2,16,512]{2,1,0:T(8,128)S(1)}, f32[2,16,512]{2,1,0:T(8,128)}, u32[]{:S(2)}) copy-start(f32[2,16,512]{2,1,0:T(8,128)} %param.8) | copy-start | bytes 196612
Sparse Core Ops, SparseCore 0:
  9.4 136.1 all-gather.1
  196.8 257.4 all-reduce.1
  607.6 129.5 reduce-scatter.1
where the time goes:
time: 749 us; the launch traced here: 745 us
  waiting for transfers between devices  542 us (72%)
  local copies, waits for them, and re-layouts  106 us (14%)
  other arithmetic  27.7 us (4%)
  loops' own time  27.1 us (4%)
  matrix products  25.4 us (3%)
  between operations  13.3 us (2%)
    psum x1, waiting for transfers between devices, on_device(): intensity = lax.psum(local_power, 'mode')  253 us
    all_gather x1, waiting for transfers between devices, on_device(): tile_half = lax.all_gather(half_object, 'mode', axis=1, tiled=True)  138 us
    reduce_scatter x1, waiting for transfers between devices, on_device(): owned = lax.psum_scatter(tile_grad, 'mode', scatter_dimension=1, tiled=True)  130 us
    dynamic_update_slice x8, local copies, waits for them, and re-layouts, place_term(): lax.dynamic_update_slice(gradient, current + terms[position], (zero_index...  52.5 us
    another operation x1, loops' own time, on_device(): gradient = lax.fori_loop(0, slots, place_term, start_grad)  27 us
    gather x40, local copies, waits for them, and re-layouts  23.6 us
    ppermute x2, waiting for transfers between devices, shifted(): return lax.ppermute(block, axis, route)  21.2 us
  transfers between devices with their start and end apart: 5, of which 5 were waited for; matrix products, arithmetic and copies ran while one was open for 1% of the time, Pallas kernels for 0%

commit v1 on v0

v1 whole, which is shorter than its diff:
```python
import functools
import math

import jax
import jax.numpy as jnp
import numpy as np
from jax import lax
from jax.experimental import pallas as pl
from jax.experimental.pallas import tpu as pltpu
from jax.sharding import Mesh, PartitionSpec as P

step_size = 0.05
f32 = jnp.float32
bf16 = jnp.bfloat16
TILE_AXES = ("y", "xh", "c")
SPARE = 16
VMEM_LIMIT = 48 * 1024 * 1024


def dft_blocks(length):
    freqs = np.arange(length, dtype=np.int32)
    turns = freqs[:, None] * freqs[None, :] % length
    phase = turns.astype(np.float32) * np.float32(2.0 * math.pi / length)
    norm_scale = np.float32(1.0 / math.sqrt(length))
    cos_table = (np.cos(phase) * norm_scale).astype(jnp.bfloat16)
    sin_table = (-np.sin(phase) * norm_scale).astype(jnp.bfloat16)
    right = np.block([[cos_table, sin_table], [-sin_table, cos_table]])
    left = np.block([[cos_table, -sin_table], [sin_table, cos_table]])
    return right, left


def dot(left_side, right_side):
    return jnp.dot(left_side, right_side, preferred_element_type=f32)


def side_by_side(stacked):
    size = stacked.shape[0] // 2
    return jnp.concatenate([stacked[:size], stacked[size:]], axis=1)


def on_top(beside):
    size = beside.shape[1] // 2
    return jnp.concatenate([beside[:, :size], beside[:, size:]], axis=0)


def forward_kernel(
    rows_ref, cols_ref, lane_ref, mine_ref, other_ref, below_ref, probe_ref, right_ref, left_ref,
    spec_ref, power_ref, extended,
):
    slot = pl.program_id(0)
    chunks, _, chunk_rows, width = mine_ref.shape
    modes, _, window, _ = probe_ref.shape
    half = chunks * chunk_rows
    lane = lane_ref[0]

    @pl.when(slot == 0)
    def _():
        extended[:, pl.ds(3 * half, SPARE), :] = jnp.zeros((2, SPARE, width), f32)
        for source, base in (
            (mine_ref, lane * half), (other_ref, (1 - lane) * half), (below_ref, 2 * half)
        ):
            for chunk in range(chunks):
                start = base + chunk * chunk_rows
                if not isinstance(start, int):
                    start = pl.multiple_of(start, chunk_rows)
                for part in range(2):
                    extended[part, pl.ds(start, chunk_rows), :] = source[chunk, part].astype(f32)

    place = lane * pl.num_programs(0) + slot
    row_start = rows_ref[place]
    col_start = cols_ref[place]
    source_col = lax.broadcasted_iota(jnp.int32, (width, window), 0)
    target_col = lax.broadcasted_iota(jnp.int32, (width, window), 1)
    pick = (source_col == target_col + col_start).astype(f32).astype(bf16)
    aligned = pl.multiple_of(row_start // 8 * 8, 8)
    taken = window + SPARE
    back_turn = (taken - row_start % 8) % taken

    def cut_patch(part):
        columns = dot(extended[part, pl.ds(aligned, taken), :].astype(bf16), pick)
        return pltpu.roll(columns, back_turn, 0)[:window]

    patch_real, patch_imag = cut_patch(0), cut_patch(1)
    power = None
    for mode in range(modes):
        probe_real, probe_imag = probe_ref[mode, 0], probe_ref[mode, 1]
        exit_real = (probe_real * patch_real - probe_imag * patch_imag).astype(bf16)
        exit_imag = (probe_real * patch_imag + probe_imag * patch_real).astype(bf16)
        half_spectrum = dot(jnp.concatenate([exit_real, exit_imag], axis=1), right_ref[...])
        spectrum = dot(left_ref[...], on_top(half_spectrum.astype(bf16)))
        spec_ref[0, mode] = spectrum
        squares = spectrum * spectrum
        term = squares[:window] + squares[window:]
        power = term if power is None else power + term
    power_ref[0] = power.astype(bf16)


def backward_kernel(
    rows_ref, cols_ref, lane_ref, spec_ref, factor_ref, probe_ref, right_ref, left_ref,
    mine_ref, other_ref, below_ref, gradient,
):
    slot = pl.program_id(0)
    chunks, _, chunk_rows, width = mine_ref.shape
    modes, _, window, _ = probe_ref.shape
    half = chunks * chunk_rows
    lane = lane_ref[0]

    @pl.when(slot == 0)
    def _():
        gradient[...] = jnp.zeros_like(gradient)

    factor = factor_ref[0].astype(f32)
    factor = jnp.concatenate([factor, factor], axis=0)
    sum_real, sum_imag = None, None
    for mode in range(modes):
        wave = (spec_ref[0, mode] * factor).astype(bf16)
        back_half = dot(side_by_side(wave), left_ref[...])
        back_wave = dot(right_ref[...], on_top(back_half.astype(bf16)))
        back_real, back_imag = back_wave[:window], back_wave[window:]
        probe_real, probe_imag = probe_ref[mode, 0], probe_ref[mode, 1]
        term_real = probe_real * back_real + probe_imag * back_imag
        term_imag = probe_real * back_imag - probe_imag * back_real
        sum_real = term_real if sum_real is None else sum_real + term_real
        sum_imag = term_imag if sum_imag is None else sum_imag + term_imag

    place = lane * pl.num_programs(0) + slot
    row_start = rows_ref[place]
    col_start = cols_ref[place]
    source_col = lax.broadcasted_iota(jnp.int32, (window, width), 0)
    target_col = lax.broadcasted_iota(jnp.int32, (window, width), 1)
    spread = (target_col == source_col + col_start).astype(f32).astype(bf16)
    aligned = pl.multiple_of(row_start // 8 * 8, 8)
    spare = jnp.zeros((SPARE, window), f32)
    for part, term in enumerate((sum_real, sum_imag)):
        moved = pltpu.roll(jnp.concatenate([term, spare], axis=0), row_start % 8, 0)
        high = moved.astype(bf16)
        low = (moved - high.astype(f32)).astype(bf16)
        at_rows = pl.ds(aligned, window + SPARE)
        gradient[part, at_rows, :] = gradient[part, at_rows, :] + (dot(high, spread) + dot(low, spread))

    @pl.when(slot == pl.num_programs(0) - 1)
    def _():
        for target, base in (
            (mine_ref, lane * half), (other_ref, (1 - lane) * half), (below_ref, 2 * half)
        ):
            for chunk in range(chunks):
                start = base + chunk * chunk_rows
                if not isinstance(start, int):
                    start = pl.multiple_of(start, chunk_rows)
                for part in range(2):
                    target[chunk, part] = gradient[part, pl.ds(start, chunk_rows), :].astype(target.dtype)


def whole(shape):
    return pl.BlockSpec(shape, lambda slot, *_: (0,) * len(shape))


def per_slot(shape):
    return pl.BlockSpec((1,) + shape, lambda slot, *_: (slot,) + (0,) * len(shape))


def to_all(block, axis):
    copies = jnp.broadcast_to(block[None], (lax.axis_size(axis),) + block.shape)
    return lax.all_to_all(copies, axis, 0, 0, tiled=True)


def on_device(
    object_field, probe_modes, measured_amplitude, row_offsets, col_offsets, position_counts
):
    window = probe_modes.shape[-1]
    slots = row_offsets.shape[1]
    width = object_field.shape[2]
    depth = lax.axis_size("z")
    tiles = lax.axis_size(TILE_AXES)
    chunk_rows = object_field.shape[1]
    lane = lax.axis_index("xl")
    here = lax.axis_index("z")
    right, left = (jnp.asarray(table) for table in dft_blocks(window))
    own_slots = slots // lax.axis_size("xl")
    swap = [(0, 1), (1, 0)]
    upwards = [(i, i - 1) for i in range(1, tiles)]
    downwards = [(i - 1, i) for i in range(1, tiles)]

    other_probe = lax.ppermute(probe_modes, "xl", swap)
    mine = to_all(object_field.astype(bf16), "z")
    other = lax.ppermute(mine, "xl", swap)
    top = jnp.where(lane == 0, mine, other)
    below = lax.ppermute(top, TILE_AXES, upwards)
    probes = jnp.concatenate([probe_modes, other_probe], axis=0)

    scalars = (row_offsets[0], col_offsets[0], lane.astype(jnp.int32)[None])
    chunked = (depth, 2, chunk_rows, width)
    modes = probes.shape[0]
    product_flops = own_slots * modes * 2 * 2 * (2 * window) ** 2 * window
    spectrum, power = pl.pallas_call(
        forward_kernel,
        grid_spec=pltpu.PrefetchScalarGridSpec(
            num_scalar_prefetch=3,
            grid=(own_slots,),
            in_specs=[whole(chunked)] * 3
            + [whole(probes.shape), whole(right.shape), whole(left.shape)],
            out_specs=[per_slot((modes, 2 * window, window)), per_slot((window, window))],
            scratch_shapes=[pltpu.VMEM((2, 3 * depth * chunk_rows + SPARE, width), f32)],
        ),
        out_shape=[
            jax.ShapeDtypeStruct((own_slots, modes, 2 * window, window), f32),
            jax.ShapeDtypeStruct((own_slots, window, window), bf16),
        ],
        compiler_params=pltpu.CompilerParams(vmem_limit_bytes=VMEM_LIMIT),
        cost_estimate=pl.CostEstimate(
            flops=product_flops, bytes_accessed=8 * 1024 * 1024, transcendentals=0
        ),
        name="forward",
    )(*scalars, mine, other, below, probes, right, left)

    pieces = lax.all_to_all(
        power.reshape(depth, own_slots * window // depth, window), "z", 0, 0, tiled=True
    )
    intensity = jnp.sum(pieces.astype(f32), axis=0)
    piece_rows = intensity.shape[0]
    per_window = window // piece_rows
    slot = lane * own_slots + here // per_window
    amplitude = lax.dynamic_slice(
        measured_amplitude[0],
        (slot, here % per_window * piece_rows, jnp.zeros((), slot.dtype)),
        (1, piece_rows, window),
    )[0]
    alive = (slot < position_counts[lax.axis_index(TILE_AXES)]).astype(f32)
    factor_piece = (alive * (1.0 - amplitude / jnp.sqrt(intensity + 1.0))).astype(bf16)
    factor = to_all(factor_piece, "z").reshape(own_slots, window, window)

    kept, sent, beneath = pl.pallas_call(
        backward_kernel,
        grid_spec=pltpu.PrefetchScalarGridSpec(
            num_scalar_prefetch=3,
            grid=(own_slots,),
            in_specs=[per_slot((modes, 2 * window, window)), per_slot((window, window))]
            + [whole(probes.shape), whole(right.shape), whole(left.shape)],
            out_specs=[whole(chunked)] * 3,
            scratch_shapes=[pltpu.VMEM((2, 3 * depth * chunk_rows + SPARE, width), f32)],
        ),
        out_shape=[
            jax.ShapeDtypeStruct(chunked, f32),
            jax.ShapeDtypeStruct(chunked, f32),
            jax.ShapeDtypeStruct(chunked, bf16),
        ],
        compiler_params=pltpu.CompilerParams(vmem_limit_bytes=VMEM_LIMIT),
        cost_estimate=pl.CostEstimate(
            flops=product_flops, bytes_accessed=8 * 1024 * 1024, transcendentals=0
        ),
        name="backward",
    )(*scalars, spectrum, factor, probes, right, left)

    from_above = lax.ppermute(beneath, TILE_AXES, downwards).astype(f32)
    zero = jnp.zeros((), f32)
    outgoing = (sent + jnp.where(lane == 1, from_above, zero)).astype(bf16)
    incoming = lax.ppermute(outgoing, "xl", swap).astype(f32)
    own_half = kept + jnp.where(lane == 0, from_above, zero) + incoming
    terms = lax.all_to_all(own_half.astype(bf16), "z", 0, 0, tiled=True)
    return object_field - step_size * jnp.sum(terms.astype(f32), axis=0)


def solution(mesh):
    tiles, modes = mesh.devices.shape
    parts = Mesh(mesh.devices.reshape(tiles // 4, 2, 2, 2, modes // 2), TILE_AXES + ("xl", "z"))
    placed = (
        P(None, TILE_AXES + ("xl", "z"), None),
        P(("xl", "z"), None, None, None),
        P(TILE_AXES, None, None, None),
        P(TILE_AXES, None),
        P(TILE_AXES, None),
        P(),
    )
    return jax.shard_map(
        on_device,
        mesh=parts,
        in_specs=placed,
        out_specs=P(None, TILE_AXES + ("xl", "z"), None),
        check_vma=False,
    )
```

time: 749 us -> 231 us (0.31)
  waiting for transfers between devices: 542 us -> 60.6 us
  blocking collectives: 0 us -> 117 us
  local copies, waits for them, and re-layouts: 106 us -> 4.91 us
  loops' own time: 27.1 us -> 0 us
  matrix products: 25.4 us -> 0 us
  other arithmetic: 27.7 us -> 3.02 us
  starting transfers between devices: 3.93 us -> 25.1 us
  Pallas kernels: 0 us -> 18.4 us
  between operations: 13.3 us -> 0.74 us
    psum x1 -> x0, waiting for transfers between devices: 253 us -> none  [on_device(): intensity = lax.psum(local_power, 'mode')]
    all_gather x1 -> x0, waiting for transfers between devices: 138 us -> none  [on_device(): tile_half = lax.all_gather(half_object, 'mode', axis=1, tiled=True)]
    reduce_scatter x1 -> x0, waiting for transfers between devices: 130 us -> none  [on_device(): owned = lax.psum_scatter(tile_grad, 'mode', scatter_dimension=1, tiled=True)]
    all_to_all x0 -> x3, blocking collectives: none -> 117 us  [the longest x2 85.5 us: to_all(): return lax.all_to_all(copies, axis, 0, 0, tiled=True)]
    dynamic_update_slice x8 -> x0, local copies, waits for them, and re-layouts: 52.5 us -> none  [place_term(): lax.dynamic_update_slice(gradient, current + terms[position], (zero_index...]
    another operation x2 -> x0, loops' own time: 27.1 us -> none  [the longest x1 27 us: on_device(): gradient = lax.fori_loop(0, slots, place_term, start_grad)]
    dot_general x16 -> x0, matrix products: 25.4 us -> none  [the longest x8 14.1 us: prod(): jnp.einsum('ki,pij->pkj', left_side, right_side, preferred_element_type=j...]
    gather x40 -> x0, local copies, waits for them, and re-layouts: 23.6 us -> none
  transfers between devices with their start and end apart: 5 -> 6, of which waited for: 5 -> 6; matrix products, arithmetic and copies ran while one was open for 1% -> 1% of each run, Pallas kernels for 0% -> 0%
where the time goes in v1:
time: 231 us; the launch traced here: 230 us
  blocking collectives  117 us (51%)
  waiting for transfers between devices  60.6 us (26%)
  starting transfers between devices  25.1 us (11%)
  Pallas kernels  18.4 us (8%)
  local copies, waits for them, and re-layouts  4.91 us (2%)
  other arithmetic  3.02 us (1%)
    all_to_all x2, blocking collectives, to_all(): return lax.all_to_all(copies, axis, 0, 0, tiled=True)  85.5 us
    all_to_all x1, blocking collectives, on_device(): terms = lax.all_to_all(own_half.astype(bf16), 'z', 0, 0, tiled=True)  31.9 us
    all_to_all x1, waiting for transfers between devices, on_device(): lax.all_to_all(power.reshape(depth, own_slots * window // depth, window),...  23.1 us
    all_to_all x1, starting transfers between devices, on_device(): lax.all_to_all(power.reshape(depth, own_slots * window // depth, window),...  12.9 us
    ppermute x1, waiting for transfers between devices, on_device(): incoming = lax.ppermute(outgoing, 'xl', swap).astype(f32)  11.5 us
    ppermute x1, waiting for transfers between devices, on_device(): from_above = lax.ppermute(beneath, TILE_AXES, downwards).astype(f32)  11.2 us
    pallas_call x1, Pallas kernels, on_device(): pl.pallas_call(backward_kernel, grid_spec=pltpu.PrefetchScalarGridSpec(nu...  10.4 us
    ppermute x1, waiting for transfers between devices, on_device(): other = lax.ppermute(mine, 'xl', swap)  8.76 us
  transfers between devices with their start and end apart: 6, of which 6 were waited for; matrix products, arithmetic and copies ran while one was open for 1% of the time, Pallas kernels for 0%

profile of v1, /device:TPU:16, one launch (start us, length us, event | category | flops | bytes accessed | tf_op | source)
XLA Modules:
  0.0 230.2 jit_solution(16287854344126355246)
XLA Ops:
  0.0 0.8 convert_element_type.31
  0.8 0.1 broadcast_in_dim.21
  0.9 44.1 %all_to_all.20.mine_ref = bf16[16,2,16,512]{3,2,1,0:T(8,128)(2,1)S(1)} all-to-all(bf16[16,2,16,512]{3,2,1,0:T(8,128)(2,1)S(1)} %broadcast_in_dim.21), channel_id=1, replica_groups=mesh['y'=4,'xh'=2,'c'=2,'xl'=2,'z'=16] {'z'}, dimensions={0} | all-to-all | bytes 1048576 | tf_op jit(solution)/shard_map/all_to_all | solution.py:164
  45.0 0.0 copy-start
  45.0 0.0 copy-start.1
  45.0 0.0 copy-start.2
  45.0 0.0 copy-start.4
  45.0 3.5 %collective-permute-start = (bf16[16,2,16,512]{3,2,1,0:T(8,128)(2,1)S(1)}, bf16[16,2,16,512]{3,2,1,0:T(8,128)(2,1)S(1)}, u32[]{:S(2)}, u32[]{:S(2)}) collective-permute-start(bf16[16,2,16,512]{3,2,1,0:T(8,128)(2,1)S(1)} %all_to_all.20.mine_ref), channel_id=1, source_target_pairs={{0,16},{16,0},{1,17},{17,1},{2,18},{18,2},{3,19},{19,3},{4,20},{20... | collective-permute-start | bytes 1572872 | tf_op jit(solution)/shard_map/ppermute | solution.py:186
  48.5 2.4 %collective-permute-start.2 = (f32[1,2,256,256]{3,2,1,0:T(8,128)}, f32[1,2,256,256]{3,2,1,0:T(8,128)}, u32[]{:S(2)}, u32[]{:S(2)}) collective-permute-start(f32[1,2,256,256]{3,2,1,0:T(8,128)} %param.9), channel_id=1, source_target_pairs={{0,16},{16,0},{1,17},{17,1},{2,18},{18,2},{3,19},{19,3},{4,20},{20... | collective-permute-start | bytes 1572872 | tf_op jit(solution)/shard_map/ppermute | solution.py:184
  51.0 8.8 %collective-permute-done.other_ref = bf16[16,2,16,512]{3,2,1,0:T(8,128)(2,1)S(1)} collective-permute-done((bf16[16,2,16,512]{3,2,1,0:T(8,128)(2,1)S(1)}, bf16[16,2,16,512]{3,2,1,0:T(8,128)(2,1)S(1)}, u32[]{:S(2)}, u32[]{:S(2)}) %collective-permute-start) | collective-permute-done | bytes 524320 | tf_op jit(solution)/shard_map/ppermute | solution.py:186
  59.8 0.1 broadcast_select_fusion
  59.8 1.9 collective-permute-start.1
  61.8 1.1 constant_dynamic-update-slice_fusion.1
  62.8 2.7 %collective-permute-done.2 = f32[1,2,256,256]{3,2,1,0:T(8,128)} collective-permute-done((f32[1,2,256,256]{3,2,1,0:T(8,128)}, f32[1,2,256,256]{3,2,1,0:T(8,128)}, u32[]{:S(2)}, u32[]{:S(2)}) %collective-permute-start.2) | collective-permute-done | bytes 524320 | tf_op jit(solution)/shard_map/ppermute | solution.py:184
  65.5 1.1 constant_dynamic-update-slice_fusion.probe_ref
  66.6 3.4 %collective-permute-done.1.below_ref = bf16[16,2,16,512]{3,2,1,0:T(8,128)(2,1)S(1)} collective-permute-done((bf16[16,2,16,512]{3,2,1,0:T(8,128)(2,1)S(1)}, bf16[16,2,16,512]{3,2,1,0:T(8,128)(2,1)S(1)}, u32[]{:S(2)}, u32[]{:S(2)}) %collective-permute-start.1) | collective-permute-done | bytes 524320 | tf_op jit(solution)/shard_map/ppermute | solution.py:188
  70.0 0.0 copy-done
  70.0 0.0 copy-done.1
  70.0 0.0 copy-done.2
  70.0 0.0 copy-done.4
  70.0 0.0 copy-start.7
  70.0 8.0 %forward.1 = (f32[4,2,512,256]{3,2,1,0:T(8,128)}, bf16[4,256,256]{2,1,0:T(8,128)(2,1)}) custom-call(s32[8]{0:T(128)S(1)} %bitcast.15, s32[8]{0:T(128)S(1)} %bitcast.17, s32[1]{0:T(128)} %bitcast.2.lane_ref, bf16[16,2,16,512]{3,2,1,0:T(8,128)(2,1)S(1)} %all_to_all.20.mine_ref, bf16[16,2,16,512]{3,2,1,0:T(8,128)(2,1)S(1)} %collective-permute-done.other_ref, ...), custom_call_target="tpu_custom_call" | custom-call | flops 2147483648 | bytes 8388608 | tf_op jit(solution)/shard_map/forward/pallas_call | solution.py:195
  78.0 12.9 %all-to-all-start.1 = ((bf16[16,64,256]{2,1,0:T(8,128)(2,1)}), bf16[16,64,256]{2,1,0:T(8,128)(2,1)S(1)}, u32[]{:S(2)}, u32[]{:S(2)}) async-start(bf16[16,64,256]{2,1,0:T(8,128)(2,1)} %bitcast.5), calls=%async_computation.1 | async-start | bytes 1048576 | tf_op jit(solution)/shard_map/all_to_all | solution.py:216
  91.0 0.0 copy-done.7
  91.0 0.6 dynamic_slice.6
  92.1 23.1 %all-to-all-done.1 = bf16[16,64,256]{2,1,0:T(8,128)(2,1)S(1)} async-done(((bf16[16,64,256]{2,1,0:T(8,128)(2,1)}), bf16[16,64,256]{2,1,0:T(8,128)(2,1)S(1)}, u32[]{:S(2)}, u32[]{:S(2)}) %all-to-all-start.1) | async-done | bytes 524320 | tf_op jit(solution)/shard_map/all_to_all | solution.py:216
  115.1 0.1 convert_reduce_fusion.1
  115.2 0.9 fusion.7
  116.1 41.4 %all_to_all.21 = bf16[16,64,256]{2,1,0:T(8,128)(2,1)S(1)} all-to-all(bf16[16,64,256]{2,1,0:T(8,128)(2,1)S(1)} %broadcast_in_dim.22), channel_id=1, replica_groups=mesh['y'=4,'xh'=2,'c'=2,'xl'=2,'z'=16] {'z'}, dimensions={0} | all-to-all | bytes 1048576 | tf_op jit(solution)/shard_map/all_to_all | solution.py:164
  157.5 0.0 copy-start.3
  157.5 1.0 copy-done.3
  158.6 0.0 copy-start.5
  158.6 1.0 copy-done.5
  159.6 10.4 %backward.1 = (f32[16,2,16,512]{3,2,1,0:T(8,128)S(1)}, f32[16,2,16,512]{3,2,1,0:T(8,128)S(1)}, bf16[16,2,16,512]{3,2,1,0:T(8,128)(2,1)}) custom-call(s32[8]{0:T(128)S(1)} %bitcast.16, s32[8]{0:T(128)S(1)} %bitcast.18, s32[1]{0:T(128)} %bitcast.2.lane_ref, f32[4,2,512,256]{3,2,1,0:T(8,128)} %get-tuple-element.10.spec_ref, bf16[4,256,256]{2,1,0:T(8,128)(2,1)S(1)} %bitcast.14, ...), custom_call_target="tpu_custom_call" | custom-call | flops 2147483648 | bytes 8388608 | tf_op jit(solution)/shard_map/backward/pallas_call | solution.py:232
  170.0 1.9 collective-permute-start.3
  171.9 11.2 %collective-permute-done.3 = bf16[16,2,16,512]{3,2,1,0:T(8,128)(2,1)S(1)} collective-permute-done((bf16[16,2,16,512]{3,2,1,0:T(8,128)(2,1)}, bf16[16,2,16,512]{3,2,1,0:T(8,128)(2,1)S(1)}, u32[]{:S(2)}, u32[]{:S(2)}) %collective-permute-start.3) | collective-permute-done | bytes 524320 | tf_op jit(solution)/shard_map/ppermute | solution.py:254
  183.1 0.2 fusion.4
  183.3 2.4 %collective-permute-start.4 = (bf16[16,2,16,512]{3,2,1,0:T(8,128)(2,1)S(1)}, bf16[16,2,16,512]{3,2,1,0:T(8,128)(2,1)S(1)}, u32[]{:S(2)}, u32[]{:S(2)}) collective-permute-start(bf16[16,2,16,512]{3,2,1,0:T(8,128)(2,1)S(1)} %fusion.4), channel_id=1, source_target_pairs={{0,16},{16,0},{1,17},{17,1},{2,18},{18,2},{3,19},{19,3},{4,20},{20... | collective-permute-start | bytes 1572872 | tf_op jit(solution)/shard_map/ppermute | solution.py:257
  185.7 11.5 %collective-permute-done.4 = bf16[16,2,16,512]{3,2,1,0:T(8,128)(2,1)S(1)} collective-permute-done((bf16[16,2,16,512]{3,2,1,0:T(8,128)(2,1)S(1)}, bf16[16,2,16,512]{3,2,1,0:T(8,128)(2,1)S(1)}, u32[]{:S(2)}, u32[]{:S(2)}) %collective-permute-start.4) | collective-permute-done | bytes 524320 | tf_op jit(solution)/shard_map/ppermute | solution.py:257
  197.3 0.0 copy-start.6
  197.3 0.3 fusion.2
  197.5 31.9 %all_to_all.22 = bf16[16,2,16,512]{3,2,1,0:T(8,128)(2,1)S(1)} all-to-all(bf16[16,2,16,512]{3,2,1,0:T(8,128)(2,1)S(1)} %fusion.2), channel_id=1, replica_groups=mesh['y'=4,'xh'=2,'c'=2,'xl'=2,'z'=16] {'z'}, dimensions={0} | all-to-all | bytes 1048576 | tf_op jit(solution)/shard_map/all_to_all | solution.py:259
  229.5 0.1 convert_reduce_fusion
  229.6 0.0 copy-done.6
  229.6 0.6 multiply_subtract_fusion
  (1 shorter events, 0.0 us)
Async XLA Ops:
  45.0 25.0 %copy-start = (s32[1,8]{1,0:T(1,128)S(1)}, s32[1,8]{1,0:T(1,128)}, u32[]{:S(2)}) copy-start(s32[1,8]{1,0:T(1,128)} %param.11) | copy-start | bytes 100
  45.0 25.0 %copy-start.1 = (s32[1,8]{1,0:T(1,128)S(1)}, s32[1,8]{1,0:T(1,128)}, u32[]{:S(2)}) copy-start(s32[1,8]{1,0:T(1,128)} %param.12) | copy-start | bytes 100
  45.0 25.0 %copy-start.2 = (bf16[512,512]{1,0:T(8,128)(2,1)S(1)}, bf16[512,512]{1,0:T(8,128)(2,1)}, u32[]{:S(2)}) copy-start(bf16[512,512]{1,0:T(8,128)(2,1)} %constant.71.clone.right_ref) | copy-start | bytes 1572868
  45.0 25.0 %copy-start.4 = (bf16[512,512]{1,0:T(8,128)(2,1)S(1)}, bf16[512,512]{1,0:T(8,128)(2,1)}, u32[]{:S(2)}) copy-start(bf16[512,512]{1,0:T(8,128)(2,1)} %constant.72.clone.left_ref) | copy-start | bytes 1572868
  45.0 14.8 %collective-permute-start = (bf16[16,2,16,512]{3,2,1,0:T(8,128)(2,1)S(1)}, bf16[16,2,16,512]{3,2,1,0:T(8,128)(2,1)S(1)}, u32[]{:S(2)}, u32[]{:S(2)}) collective-permute-start(bf16[16,2,16,512]{3,2,1,0:T(8,128)(2,1)S(1)} %all_to_all.20.mine_ref), channel_id=1, source_target_pairs={{0,16},{16,0},{1,17},{17,1},{2,18},{18,2},{3,19},{19,3},{4,20},{20... | collective-permute-start | bytes 1572872 | tf_op jit(solution)/shard_map/ppermute | solution.py:186
  48.5 16.9 %collective-permute-start.2 = (f32[1,2,256,256]{3,2,1,0:T(8,128)}, f32[1,2,256,256]{3,2,1,0:T(8,128)}, u32[]{:S(2)}, u32[]{:S(2)}) collective-permute-start(f32[1,2,256,256]{3,2,1,0:T(8,128)} %param.9), channel_id=1, source_target_pairs={{0,16},{16,0},{1,17},{17,1},{2,18},{18,2},{3,19},{19,3},{4,20},{20... | collective-permute-start | bytes 1572872 | tf_op jit(solution)/shard_map/ppermute | solution.py:184
  59.8 10.2 %collective-permute-start.1 = (bf16[16,2,16,512]{3,2,1,0:T(8,128)(2,1)S(1)}, bf16[16,2,16,512]{3,2,1,0:T(8,128)(2,1)S(1)}, u32[]{:S(2)}, u32[]{:S(2)}) collective-permute-start(bf16[16,2,16,512]{3,2,1,0:T(8,128)(2,1)S(1)} %broadcast_select_fusion), channel_id=1, source_target_pairs={{32,0},{64,32},{96,64},{128,96},{160,128},{192,160},{224,192},{256... | collective-permute-start | bytes 1572872 | tf_op jit(solution)/shard_map/ppermute | solution.py:188
  70.0 20.9 %copy-start.7 = (s32[16]{0:T(128)S(1)}, s32[16]{0:T(128)}, u32[]{:S(2)}) copy-start(s32[16]{0:T(128)} %param.13) | copy-start | bytes 196
  78.0 37.1 %all-to-all-start.1 = ((bf16[16,64,256]{2,1,0:T(8,128)(2,1)}), bf16[16,64,256]{2,1,0:T(8,128)(2,1)S(1)}, u32[]{:S(2)}, u32[]{:S(2)}) async-start(bf16[16,64,256]{2,1,0:T(8,128)(2,1)} %bitcast.5), calls=%async_computation.1 | async-start | bytes 1048576 | tf_op jit(solution)/shard_map/all_to_all | solution.py:216
  157.5 1.0 copy-start.3
  158.6 1.0 copy-start.5
  170.0 13.1 %collective-permute-start.3 = (bf16[16,2,16,512]{3,2,1,0:T(8,128)(2,1)}, bf16[16,2,16,512]{3,2,1,0:T(8,128)(2,1)S(1)}, u32[]{:S(2)}, u32[]{:S(2)}) collective-permute-start(bf16[16,2,16,512]{3,2,1,0:T(8,128)(2,1)} %get-tuple-element.13), channel_id=1, source_target_pairs={{0,32},{32,64},{64,96},{96,128},{128,160},{160,192},{192,224},{224... | collective-permute-start | bytes 1572872 | tf_op jit(solution)/shard_map/ppermute | solution.py:254
  183.3 14.0 %collective-permute-start.4 = (bf16[16,2,16,512]{3,2,1,0:T(8,128)(2,1)S(1)}, bf16[16,2,16,512]{3,2,1,0:T(8,128)(2,1)S(1)}, u32[]{:S(2)}, u32[]{:S(2)}) collective-permute-start(bf16[16,2,16,512]{3,2,1,0:T(8,128)(2,1)S(1)} %fusion.4), channel_id=1, source_target_pairs={{0,16},{16,0},{1,17},{17,1},{2,18},{18,2},{3,19},{19,3},{4,20},{20... | collective-permute-start | bytes 1572872 | tf_op jit(solution)/shard_map/ppermute | solution.py:257
  197.3 32.3 %copy-start.6 = (f32[2,16,512]{2,1,0:T(8,128)S(1)}, f32[2,16,512]{2,1,0:T(8,128)}, u32[]{:S(2)}) copy-start(f32[2,16,512]{2,1,0:T(8,128)} %param.8) | copy-start | bytes 196612

commit v2 on v0

v2 whole, which is shorter than its diff:
```python
import math

import jax
import jax.numpy as jnp
import numpy as np
from jax import lax
from jax.experimental import pallas as pl
from jax.experimental.pallas import tpu as pltpu
from jax.sharding import Mesh, PartitionSpec as P

step_size = 0.05
f32 = jnp.float32
bf16 = jnp.bfloat16
TILE_AXES = ("y", "xh", "c")
DEPTH_AXES = ("zq", "zr")
VMEM_LIMIT = 48 * 1024 * 1024


def dft_blocks(length):
    freqs = np.arange(length, dtype=np.int32)
    turns = freqs[:, None] * freqs[None, :] % length
    phase = turns.astype(np.float32) * np.float32(2.0 * math.pi / length)
    norm_scale = np.float32(1.0 / math.sqrt(length))
    cos_table = (np.cos(phase) * norm_scale).astype(jnp.bfloat16)
    sin_table = (-np.sin(phase) * norm_scale).astype(jnp.bfloat16)
    right = np.block([[cos_table, sin_table], [-sin_table, cos_table]])
    left = np.block([[cos_table, -sin_table], [sin_table, cos_table]])
    return right, left


def dot(left_side, right_side):
    return jnp.dot(left_side, right_side, preferred_element_type=f32)


def on_top(beside):
    size = beside.shape[1] // 2
    return jnp.concatenate([beside[:, :size], beside[:, size:]], axis=0)


def one_hot(rows, columns, offset):
    row = lax.broadcasted_iota(jnp.int32, (rows, columns), 0)
    column = lax.broadcasted_iota(jnp.int32, (rows, columns), 1)
    return (column == row + offset).astype(f32).astype(bf16)


def one_hot_down(rows, columns, offset):
    row = lax.broadcasted_iota(jnp.int32, (rows, columns), 0)
    column = lax.broadcasted_iota(jnp.int32, (rows, columns), 1)
    return (row == column + offset).astype(f32).astype(bf16)


def cut_kernel(
    meta_ref, cols_ref, above_ref, half_ref, pair_ref, near_ref, far_ref, last_ref,
    own_ref, partner_ref, upper_ref, lower_ref, probe_ref,
):
    chunks, _, _, width = half_ref.shape
    window = own_ref.shape[-1]
    slots = cols_ref.shape[0]
    lane, quarter = meta_ref[0], meta_ref[1]
    quarters = slots // 2
    starts = (
        cols_ref[lane * quarters + quarter],
        cols_ref[(1 - lane) * quarters + quarter],
        above_ref[slots + quarter],
        above_ref[slots + quarters + quarter],
    )
    for part in range(2):
        rows = jnp.concatenate([half_ref[chunk, part] for chunk in range(chunks)], axis=0)
        for target, start in zip((own_ref, partner_ref, upper_ref, lower_ref), starts):
            target[part] = dot(rows, one_hot_down(width, window, start)).astype(bf16)
    for index, source in enumerate((pair_ref, near_ref, far_ref, last_ref)):
        probe_ref[index] = source[...]


def full_probe(here_ref, there_ref, core, mode):
    def rows(part):
        here, there = here_ref[0, mode, part].astype(f32), there_ref[0, mode, part].astype(f32)
        first = jnp.where(core == 0, here, there)
        second = jnp.where(core == 0, there, here)
        return jnp.concatenate([first, second], axis=0)

    return rows(0), rows(1)


def forward_kernel(
    meta_ref, rows_ref, own_ref, other_ref, below0_ref, below1_ref, here_ref, there_ref,
    right_ref, left_ref, spec_ref, power_ref, patch, total,
):
    step = pl.program_id(0)
    lane, quarter, core = meta_ref[0], meta_ref[1], meta_ref[2]
    window = own_ref.shape[-1]
    height = own_ref.shape[1]
    row_start = rows_ref[lane * (rows_ref.shape[0] // 2) + quarter]

    @pl.when(step == 0)
    def _():
        pick = jnp.concatenate(
            [
                one_hot(window, height, row_start - lane * height),
                one_hot(window, height, row_start - (1 - lane) * height),
                one_hot(window, height, row_start - 2 * height),
            ],
            axis=1,
        )
        for part in range(2):
            below = below0_ref[part] + below1_ref[part]
            patch[part] = dot(pick, jnp.concatenate([own_ref[part], other_ref[part], below], axis=0))
        total[...] = jnp.zeros_like(total)

    for mode in range(here_ref.shape[1]):
        probe_real, probe_imag = full_probe(here_ref, there_ref, core, mode)
        exit_real = (probe_real * patch[0] - probe_imag * patch[1]).astype(bf16)
        exit_imag = (probe_real * patch[1] + probe_imag * patch[0]).astype(bf16)
        half_spectrum = dot(jnp.concatenate([exit_real, exit_imag], axis=1), right_ref[...])
        spectrum = dot(left_ref[...], on_top(half_spectrum.astype(bf16)))
        spec_ref[0, mode] = spectrum
        squares = spectrum * spectrum
        total[...] = total[...] + (squares[:window] + squares[window:])

    @pl.when(step == pl.num_programs(0) - 1)
    def _():
        power_ref[...] = total[...].astype(bf16)


def backward_kernel(
    meta_ref, spec_ref, powers_ref, amplitude_ref, here_ref, there_ref, right_ref, left_ref,
    window_ref, factor, sums,
):
    step = pl.program_id(0)
    core, alive = meta_ref[2], meta_ref[3]
    window = window_ref.shape[-1]

    @pl.when(step == 0)
    def _():
        intensity = powers_ref[0].astype(f32)
        for member in range(1, powers_ref.shape[0]):
            intensity = intensity + powers_ref[member].astype(f32)
        correction = 1.0 - amplitude_ref[0] / jnp.sqrt(intensity + 1.0)
        factor[...] = alive.astype(f32) * correction
        sums[...] = jnp.zeros_like(sums)

    for mode in range(here_ref.shape[1]):
        wave_real = (spec_ref[0, mode, :window] * factor[...]).astype(bf16)
        wave_imag = (spec_ref[0, mode, window:] * factor[...]).astype(bf16)
        back_half = dot(jnp.concatenate([wave_real, wave_imag], axis=1), left_ref[...])
        back_wave = dot(right_ref[...], on_top(back_half.astype(bf16)))
        back_real, back_imag = back_wave[:window], back_wave[window:]
        probe_real, probe_imag = full_probe(here_ref, there_ref, core, mode)
        sums[0] = sums[0] + (probe_real * back_real + probe_imag * back_imag)
        sums[1] = sums[1] + (probe_real * back_imag - probe_imag * back_real)

    @pl.when(step == pl.num_programs(0) - 1)
    def _():
        window_ref[...] = sums[...].astype(bf16)


def place_kernel(
    meta_ref, rows_ref, cols_ref, above_ref, own_ref, partner_ref, upper_ref, lower_ref, half_ref
):
    chunks, _, chunk_rows, width = half_ref.shape
    height = chunks * chunk_rows
    window = own_ref.shape[-1]
    slots = rows_ref.shape[0]
    quarters = slots // 2
    lane, quarter = meta_ref[0], meta_ref[1]
    mine, partners = lane * quarters + quarter, (1 - lane) * quarters + quarter
    first, second = quarter, quarters + quarter
    row_starts = (
        rows_ref[mine] - lane * height,
        rows_ref[partners] - lane * height,
        above_ref[first] - 2 * height,
        above_ref[second] - 2 * height,
    )
    col_starts = (
        cols_ref[mine], cols_ref[partners], above_ref[slots + first], above_ref[slots + second]
    )
    spread = jnp.concatenate([one_hot(window, width, start) for start in col_starts], axis=0)
    sources = (own_ref, partner_ref, upper_ref, lower_ref)
    shifts = [one_hot_down(height, window, start) for start in row_starts]
    for part in range(2):
        moved = [dot(shift, source[part]).astype(bf16) for shift, source in zip(shifts, sources)]
        placed = dot(jnp.concatenate(moved, axis=1), spread).astype(bf16)
        for chunk in range(chunks):
            half_ref[chunk, part] = placed[chunk * chunk_rows : (chunk + 1) * chunk_rows]


def whole(shape):
    return pl.BlockSpec(shape, lambda step, *_: (0,) * len(shape))


def per_step(shape):
    return pl.BlockSpec((1,) + shape, lambda step, *_: (step,) + (0,) * len(shape))


def call(kernel, name, scalars, operands, in_specs, results, out_specs, steps=1, scratch=(), flops=0):
    return pl.pallas_call(
        kernel,
        grid_spec=pltpu.PrefetchScalarGridSpec(
            num_scalar_prefetch=len(scalars),
            grid=(steps,),
            in_specs=in_specs,
            out_specs=out_specs,
            scratch_shapes=scratch,
        ),
        out_shape=results,
        compiler_params=pltpu.CompilerParams(vmem_limit_bytes=VMEM_LIMIT),
        cost_estimate=pl.CostEstimate(
            flops=flops, bytes_accessed=4 * 1024 * 1024, transcendentals=0
        ),
        name=name,
    )(*scalars, *operands)


def to_all(block, axis):
    size = lax.axis_size(axis)
    return lax.all_to_all(jnp.broadcast_to(block[None], (size,) + block.shape), axis, 0, 0, tiled=True)


def on_device(
    object_field, probe_modes, measured_amplitude, row_offsets, col_offsets, position_counts
):
    window = probe_modes.shape[-1]
    slots = row_offsets.shape[1]
    width = object_field.shape[2]
    chunk_rows = object_field.shape[1]
    depth = lax.axis_size(DEPTH_AXES)
    quarters = lax.axis_size("zq")
    tiles = lax.axis_size(TILE_AXES)
    lane, quarter, core = lax.axis_index("xl"), lax.axis_index("zq"), lax.axis_index("c")
    right, left = (jnp.asarray(table) for table in dft_blocks(window))
    swap = [(0, 1), (1, 0)]
    axes = TILE_AXES + ("xl",)
    up_first = [(2 * (t + 1), 2 * t) for t in range(tiles - 1)]
    up_second = [(2 * (t + 1), 2 * t + 1) for t in range(tiles - 1)]
    down_first = [(2 * t, 2 * (t + 1)) for t in range(tiles - 1)]
    down_second = [(2 * t + 1, 2 * (t + 1)) for t in range(tiles - 1)]
    downwards = [(t, t + 1) for t in range(tiles - 1)]

    count = position_counts[lax.axis_index(TILE_AXES)]
    alive = (lane * quarters + quarter < count).astype(jnp.int32)
    meta = jnp.stack([lane, quarter, core, alive]).astype(jnp.int32)
    rows, cols = row_offsets[0], col_offsets[0]
    above = lax.ppermute(jnp.concatenate([rows, cols]), TILE_AXES, downwards)

    part_rows = window // 2
    probe_part = lax.dynamic_slice_in_dim(
        probe_modes.astype(bf16), core * part_rows, part_rows, axis=2
    )
    pair = jnp.concatenate([probe_part, lax.ppermute(probe_part, "xl", swap)], axis=0)
    brought = [
        lax.ppermute(pair, "zq", [(i, (i + d) % quarters) for i in range(quarters)])
        for d in range(1, quarters)
    ]
    half = to_all(object_field.astype(bf16), DEPTH_AXES)

    patch_shape = (2, half.shape[0] * chunk_rows, window)
    window_shape = (2, window, window)
    probes_shape = (quarters,) + pair.shape
    own, partner, upper, lower, here = call(
        cut_kernel, "cut", (meta, cols, above), (half, pair, *brought),
        [whole(half.shape)] + [whole(pair.shape)] * 4,
        [jax.ShapeDtypeStruct(patch_shape, bf16)] * 4 + [jax.ShapeDtypeStruct(probes_shape, bf16)],
        [whole(patch_shape)] * 4 + [whole(probes_shape)],
    )
    there = lax.ppermute(here, "c", swap)
    other = lax.ppermute(partner, "xl", swap)
    below0 = lax.ppermute(upper, axes, up_first)
    below1 = lax.ppermute(lower, axes, up_second)

    modes = quarters * pair.shape[0]
    product_flops = modes * 2 * 2 * (2 * window) ** 2 * window
    probe_block = per_step(pair.shape)
    spec_shape = (pair.shape[0], 2 * window, window)
    spectrum, power = call(
        forward_kernel, "forward", (meta, rows),
        (own, other, below0, below1, here, there, right, left),
        [whole(patch_shape)] * 4 + [probe_block] * 2 + [whole(right.shape), whole(left.shape)],
        [
            jax.ShapeDtypeStruct((quarters,) + spec_shape, f32),
            jax.ShapeDtypeStruct((window, window), bf16),
        ],
        [per_step(spec_shape), whole((window, window))],
        steps=quarters,
        scratch=[pltpu.VMEM(window_shape, f32), pltpu.VMEM((window, window), f32)],
        flops=product_flops,
    )
    powers = lax.all_gather(power, "zr", axis=0)

    slot_block = pl.BlockSpec(
        (1, window, window), lambda step, meta_ref: (meta_ref[0] * quarters + meta_ref[1], 0, 0)
    )
    term = call(
        backward_kernel, "backward", (meta,),
        (spectrum, powers, measured_amplitude[0], here, there, right, left),
        [per_step(spec_shape), whole(powers.shape), slot_block]
        + [probe_block] * 2 + [whole(right.shape), whole(left.shape)],
        jax.ShapeDtypeStruct(window_shape, bf16),
        whole(window_shape),
        steps=quarters,
        scratch=[pltpu.VMEM((window, window), f32), pltpu.VMEM(window_shape, f32)],
        flops=product_flops,
    )

    partners = lax.ppermute(term, "xl", swap)
    above0 = lax.ppermute(term, axes, down_first)
    above1 = lax.ppermute(term, axes, down_second)
    half_sum = call(
        place_kernel, "place", (meta, rows, cols, above), (term, partners, above0, above1),
        [whole(window_shape)] * 4,
        jax.ShapeDtypeStruct(half.shape, bf16),
        whole(half.shape),
    )
    terms = lax.all_to_all(half_sum, DEPTH_AXES, 0, 0, tiled=True)
    return object_field - step_size * jnp.sum(terms.astype(f32), axis=0)


def solution(mesh):
    tiles, modes = mesh.devices.shape
    parts = Mesh(
        mesh.devices.reshape(tiles // 4, 2, 2, 2, 4, modes // 8), TILE_AXES + ("xl",) + DEPTH_AXES
    )
    tile, mode = TILE_AXES, ("xl",) + DEPTH_AXES
    placed = (
        P(None, tile + mode, None),
        P(mode, None, None, None),
        P(tile, None, None, None),
        P(tile, None),
        P(tile, None),
        P(),
    )
    return jax.shard_map(
        on_device,
        mesh=parts,
        in_specs=placed,
        out_specs=P(None, tile + mode, None),
        check_vma=False,
    )
```

time: 749 us -> 196 us (0.26)
  the two profiles are of different devices: /device:TPU:16 before, /device:TPU:1 now
where the time goes in v2:
time: 196 us; the launch traced here: 195 us
  starting transfers between devices  65.2 us (33%)
  blocking collectives  55 us (28%)
  waiting for transfers between devices  49.3 us (25%)
  Pallas kernels  16.5 us (8%)
  local copies, waits for them, and re-layouts  5.58 us (3%)
  other arithmetic  2.48 us (1%)
    all_to_all x1, blocking collectives, on_device(): terms = lax.all_to_all(half_sum, DEPTH_AXES, 0, 0, tiled=True)  32.9 us
    ppermute x3, waiting for transfers between devices, on_device(): lax.ppermute(pair, 'zq', [(i, (i + d) % quarters) for i in range(quarters)])  28.7 us
    all_gather x1, blocking collectives, on_device(): powers = lax.all_gather(power, 'zr', axis=0)  22.1 us
    ppermute x3, starting transfers between devices, on_device(): lax.ppermute(pair, 'zq', [(i, (i + d) % quarters) for i in range(quarters)])  21.5 us
    pallas_call x4, Pallas kernels, call(): pl.pallas_call(kernel, grid_spec=pltpu.PrefetchScalarGridSpec(num_scalar_...  16.5 us
    all_to_all x1, starting transfers between devices, to_all(): lax.all_to_all(jnp.broadcast_to(block[None], (size,) + block.shape), axis...  15.7 us
    ppermute x1, waiting for transfers between devices, on_device(): below0 = lax.ppermute(upper, axes, up_first)  7.92 us
    ppermute x1, starting transfers between devices, on_device(): above = lax.ppermute(jnp.concatenate([rows, cols]), TILE_AXES, downwards)  7.46 us
  transfers between devices with their start and end apart: 13, of which 9 were waited for; matrix products, arithmetic and copies ran while one was open for 1% of the time, Pallas kernels for 0%

profile of v2, /device:TPU:1, one launch (start us, length us, event | category | flops | bytes accessed | tf_op | source)
XLA Modules:
  0.0 195.0 jit_solution(3614176334105826421)
XLA Ops:
  0.0 0.0 copy-start
  0.0 0.9 convert_element_type.10
  0.9 0.9 broadcast_in_dim.2
  1.8 15.7 %all-to-all-start = ((bf16[16,2,16,512]{3,2,1,0:T(8,128)(2,1)}), bf16[16,2,16,512]{3,2,1,0:T(8,128)(2,1)S(1)}, u32[]{:S(2)}, u32[]{:S(2)}) async-start(bf16[16,2,16,512]{3,2,1,0:T(8,128)(2,1)} %broadcast_in_dim.2), calls=%async_computation | async-start | bytes 1048576 | tf_op jit(solution)/shard_map/all_to_all | solution.py:216
  17.5 0.0 copy-done
  17.6 3.1 %collective-permute-start.1 = (bf16[1,2,128,256]{3,2,1,0:T(8,128)(2,1)S(1)}, bf16[1,2,128,256]{3,2,1,0:T(8,128)(2,1)S(1)}, u32[]{:S(2)}, u32[]{:S(2)}) collective-permute-start(bf16[1,2,128,256]{3,2,1,0:T(8,128)(2,1)S(1)} %dynamic-slice_convert_fusion), channel_id=1, source_target_pairs={{0,16},{16,0},{1,17},{17,1},{2,18},{18,2},{3,19},{19,3},{4,20},{20... | collective-permute-start | bytes 393224 | tf_op jit(solution)/shard_map/ppermute | solution.py:249
  20.7 2.6 %collective-permute-done.1 = bf16[1,2,128,256]{3,2,1,0:T(8,128)(2,1)S(1)} collective-permute-done((bf16[1,2,128,256]{3,2,1,0:T(8,128)(2,1)S(1)}, bf16[1,2,128,256]{3,2,1,0:T(8,128)(2,1)S(1)}, u32[]{:S(2)}, u32[]{:S(2)}) %collective-permute-start.1) | collective-permute-done | bytes 131104 | tf_op jit(solution)/shard_map/ppermute | solution.py:249
  23.3 7.2 %collective-permute-start.4 = (bf16[2,2,128,256]{3,2,1,0:T(8,128)(2,1)S(1)}, bf16[2,2,128,256]{3,2,1,0:T(8,128)(2,1)S(1)}, u32[]{:S(2)}, u32[]{:S(2)}) collective-permute-start(bf16[2,2,128,256]{3,2,1,0:T(8,128)(2,1)S(1)} %pad_maximum_fusion.pair_ref), channel_id=1, source_target_pairs={{0,12},{4,0},{8,4},{12,8},{1,13},{5,1},{9,5},{13,9},{2,14},{6,2},{... | collective-permute-start | bytes 786440 | tf_op jit(solution)/shard_map/ppermute | solution.py:251
  30.5 7.0 %collective-permute-start.3 = (bf16[2,2,128,256]{3,2,1,0:T(8,128)(2,1)S(1)}, bf16[2,2,128,256]{3,2,1,0:T(8,128)(2,1)S(1)}, u32[]{:S(2)}, u32[]{:S(2)}) collective-permute-start(bf16[2,2,128,256]{3,2,1,0:T(8,128)(2,1)S(1)} %pad_maximum_fusion.pair_ref), channel_id=1, source_target_pairs={{0,8},{4,12},{8,0},{12,4},{1,9},{5,13},{9,1},{13,5},{2,10},{6,14},... | collective-permute-start | bytes 786440 | tf_op jit(solution)/shard_map/ppermute | solution.py:251
  37.5 7.3 %collective-permute-start.2 = (bf16[2,2,128,256]{3,2,1,0:T(8,128)(2,1)S(1)}, bf16[2,2,128,256]{3,2,1,0:T(8,128)(2,1)S(1)}, u32[]{:S(2)}, u32[]{:S(2)}) collective-permute-start(bf16[2,2,128,256]{3,2,1,0:T(8,128)(2,1)S(1)} %pad_maximum_fusion.pair_ref), channel_id=1, source_target_pairs={{0,4},{4,8},{8,12},{12,0},{1,5},{5,9},{9,13},{13,1},{2,6},{6,10},{... | collective-permute-start | bytes 786440 | tf_op jit(solution)/shard_map/ppermute | solution.py:251
  44.8 0.7 pad_add_fusion.1
  45.5 7.5 %collective-permute-start = (s32[16]{0:T(128)S(1)}, s32[16]{0:T(128)S(1)}, u32[]{:S(2)}, u32[]{:S(2)}) collective-permute-start(s32[16]{0:T(128)S(1)} %pad_add_fusion.1), channel_id=1, source_target_pairs={{0,32},{32,64},{64,96},{96,128},{128,160},{160,192},{192,224},{224... | collective-permute-start | bytes 200 | tf_op jit(solution)/shard_map/ppermute | solution.py:243
  53.0 1.3 dynamic_slice.6
  55.0 0.1 pad_add_fusion.meta_ref
  55.1 0.0 collective-permute-done.above_ref
  55.1 11.1 %collective-permute-done.4.last_ref = bf16[2,2,128,256]{3,2,1,0:T(8,128)(2,1)S(1)} collective-permute-done((bf16[2,2,128,256]{3,2,1,0:T(8,128)(2,1)S(1)}, bf16[2,2,128,256]{3,2,1,0:T(8,128)(2,1)S(1)}, u32[]{:S(2)}, u32[]{:S(2)}) %collective-permute-start.4) | collective-permute-done | bytes 262176 | tf_op jit(solution)/shard_map/ppermute | solution.py:251
  66.2 4.9 %collective-permute-done.3.far_ref = bf16[2,2,128,256]{3,2,1,0:T(8,128)(2,1)S(1)} collective-permute-done((bf16[2,2,128,256]{3,2,1,0:T(8,128)(2,1)S(1)}, bf16[2,2,128,256]{3,2,1,0:T(8,128)(2,1)S(1)}, u32[]{:S(2)}, u32[]{:S(2)}) %collective-permute-start.3) | collective-permute-done | bytes 262176 | tf_op jit(solution)/shard_map/ppermute | solution.py:251
  71.2 12.6 %collective-permute-done.2.near_ref = bf16[2,2,128,256]{3,2,1,0:T(8,128)(2,1)S(1)} collective-permute-done((bf16[2,2,128,256]{3,2,1,0:T(8,128)(2,1)S(1)}, bf16[2,2,128,256]{3,2,1,0:T(8,128)(2,1)S(1)}, u32[]{:S(2)}, u32[]{:S(2)}) %collective-permute-start.2) | collective-permute-done | bytes 262176 | tf_op jit(solution)/shard_map/ppermute | solution.py:251
  83.8 0.0 all-to-all-done.half_ref
  83.8 0.0 copy-start.4
  83.8 0.7 copy-done.4
  84.4 1.4 cut.1
  85.8 3.3 %collective-permute-start.8 = (bf16[4,2,2,128,256]{4,3,2,1,0:T(8,128)(2,1)S(1)}, bf16[4,2,2,128,256]{4,3,2,1,0:T(8,128)(2,1)S(1)}, u32[]{:S(2)}, u32[]{:S(2)}) collective-permute-start(bf16[4,2,2,128,256]{4,3,2,1,0:T(8,128)(2,1)S(1)} %get-tuple-element.16.here_ref), channel_id=1, source_target_pairs={{0,32},{32,0},{1,33},{33,1},{2,34},{34,2},{3,35},{35,3},{4,36},{36... | collective-permute-start | bytes 3145736 | tf_op jit(solution)/shard_map/ppermute | solution.py:265
  89.1 3.1 %collective-permute-start.5 = (bf16[2,256,256]{2,1,0:T(8,128)(2,1)S(1)}, bf16[2,256,256]{2,1,0:T(8,128)(2,1)S(1)}, u32[]{:S(2)}, u32[]{:S(2)}) collective-permute-start(bf16[2,256,256]{2,1,0:T(8,128)(2,1)S(1)} %get-tuple-element.13), channel_id=1, source_target_pairs={{0,16},{16,0},{1,17},{17,1},{2,18},{18,2},{3,19},{19,3},{4,20},{20... | collective-permute-start | bytes 786440 | tf_op jit(solution)/shard_map/ppermute | solution.py:266
  92.2 2.2 %collective-permute-start.6 = (bf16[2,256,256]{2,1,0:T(8,128)(2,1)S(1)}, bf16[2,256,256]{2,1,0:T(8,128)(2,1)S(1)}, u32[]{:S(2)}, u32[]{:S(2)}) collective-permute-start(bf16[2,256,256]{2,1,0:T(8,128)(2,1)S(1)} %get-tuple-element.14), channel_id=1, source_target_pairs={{32,0},{64,32},{96,64},{128,96},{160,128},{192,160},{224,192},{256... | collective-permute-start | bytes 786440 | tf_op jit(solution)/shard_map/ppermute | solution.py:267
  94.5 1.3 collective-permute-start.7
  95.8 3.2 %collective-permute-done.5.other_ref = bf16[2,256,256]{2,1,0:T(8,128)(2,1)S(1)} collective-permute-done((bf16[2,256,256]{2,1,0:T(8,128)(2,1)S(1)}, bf16[2,256,256]{2,1,0:T(8,128)(2,1)S(1)}, u32[]{:S(2)}, u32[]{:S(2)}) %collective-permute-start.5) | collective-permute-done | bytes 262176 | tf_op jit(solution)/shard_map/ppermute | solution.py:266
  98.9 7.9 %collective-permute-done.6.below0_ref = bf16[2,256,256]{2,1,0:T(8,128)(2,1)S(1)} collective-permute-done((bf16[2,256,256]{2,1,0:T(8,128)(2,1)S(1)}, bf16[2,256,256]{2,1,0:T(8,128)(2,1)S(1)}, u32[]{:S(2)}, u32[]{:S(2)}) %collective-permute-start.6) | collective-permute-done | bytes 262176 | tf_op jit(solution)/shard_map/ppermute | solution.py:267
  106.9 0.0 collective-permute-done.7.below1_ref
  106.9 0.0 collective-permute-done.8.there_ref
  106.9 0.0 copy-start.2
  106.9 1.0 copy-done.2
  107.9 0.0 copy-start.3
  107.9 1.0 copy-done.3
  109.0 0.0 copy-start.5
  109.0 0.7 copy-done.5
  109.6 0.0 copy-start.1
  109.6 6.6 %forward.1 = (f32[4,2,512,256]{3,2,1,0:T(8,128)}, bf16[256,256]{1,0:T(8,128)(2,1)S(1)}) custom-call(s32[4]{0:T(128)S(1)} %pad_add_fusion.meta_ref, s32[8]{0:T(128)S(1)} %bitcast.15, bf16[2,256,256]{2,1,0:T(8,128)(2,1)S(1)} %get-tuple-element.12.own_ref, bf16[2,256,256]{2,1,0:T(8,128)(2,1)S(1)} %collective-permute-done.5.other_ref, ...), custom_call_target="tpu_custom_call" | custom-call | flops 2147483648 | bytes 4194304 | tf_op jit(solution)/shard_map/forward/pallas_call | solution.py:196
  116.2 22.1 %all-gather = bf16[1024,256]{1,0:T(8,128)(2,1)S(1)} all-gather(bf16[256,256]{1,0:T(8,128)(2,1)S(1)} %get-tuple-element.18), channel_id=2, replica_groups=mesh['y'=4,'xh'=2,'c'=2,'xl'=2,'zq'=4,'zr'=4] {'zr'}, dimensions={0}, use_global_device_ids=true | all-gather | bytes 655360 | tf_op jit(solution)/shard_map/all_gather | solution.py:287
  138.3 0.0 copy-done.1
  138.3 0.0 copy-start.6
  138.3 6.8 %backward.1.own_ref = bf16[2,256,256]{2,1,0:T(8,128)(2,1)S(1)} custom-call(s32[4]{0:T(128)S(1)} %pad_add_fusion.meta_ref, f32[4,2,512,256]{3,2,1,0:T(8,128)} %get-tuple-element.17.spec_ref, bf16[4,256,256]{2,1,0:T(8,128)(2,1)S(1)} %bitcast.10, f32[8,256,256]{2,1,0:T(8,128)S(1)} %bitcast.9, bf16[4,2,2,128,256]{4,3,2,1,0:T(8,128)(2,1)S(1)} %get-tuple-element.16.here_ref, ...), custom_call_target="tpu_custom_call" | custom-call | flops 2147483648 | bytes 4194304 | tf_op jit(solution)/shard_map/backward/pallas_call | solution.py:196
  145.1 1.3 collective-permute-start.11
  146.4 4.3 %collective-permute-start.10 = (bf16[2,256,256]{2,1,0:T(8,128)(2,1)S(1)}, bf16[2,256,256]{2,1,0:T(8,128)(2,1)S(1)}, u32[]{:S(2)}, u32[]{:S(2)}) collective-permute-start(bf16[2,256,256]{2,1,0:T(8,128)(2,1)S(1)} %backward.1.own_ref), channel_id=1, source_target_pairs={{0,32},{32,64},{64,96},{96,128},{128,160},{160,192},{192,224},{224... | collective-permute-start | bytes 786440 | tf_op jit(solution)/shard_map/ppermute | solution.py:305
  150.7 1.9 collective-permute-start.9
  152.6 0.2 collective-permute-done.11.lower_ref
  152.8 2.7 %collective-permute-done.10.upper_ref = bf16[2,256,256]{2,1,0:T(8,128)(2,1)S(1)} collective-permute-done((bf16[2,256,256]{2,1,0:T(8,128)(2,1)S(1)}, bf16[2,256,256]{2,1,0:T(8,128)(2,1)S(1)}, u32[]{:S(2)}, u32[]{:S(2)}) %collective-permute-start.10) | collective-permute-done | bytes 262176 | tf_op jit(solution)/shard_map/ppermute | solution.py:305
  155.5 4.1 %collective-permute-done.9.partner_ref = bf16[2,256,256]{2,1,0:T(8,128)(2,1)S(1)} collective-permute-done((bf16[2,256,256]{2,1,0:T(8,128)(2,1)S(1)}, bf16[2,256,256]{2,1,0:T(8,128)(2,1)S(1)}, u32[]{:S(2)}, u32[]{:S(2)}) %collective-permute-start.9) | collective-permute-done | bytes 262176 | tf_op jit(solution)/shard_map/ppermute | solution.py:304
  159.6 1.7 place.1
  161.3 32.9 %all_to_all.10 = bf16[16,2,16,512]{3,2,1,0:T(8,128)(2,1)S(1)} all-to-all(bf16[16,2,16,512]{3,2,1,0:T(8,128)(2,1)S(1)} %place.1), channel_id=1, replica_groups=mesh['y'=4,'xh'=2,'c'=2,'xl'=2,'zq'=4,'zr'=4] {'zq','zr'}, dimensions={0} | all-to-all | bytes 1048576 | tf_op jit(solution)/shard_map/all_to_all | solution.py:313
  194.3 0.1 convert_reduce_fusion
  194.4 0.0 copy-done.6
  194.4 0.6 multiply_subtract_fusion
  (2 shorter events, 0.0 us)
Async XLA Ops:
  0.0 17.5 %copy-start = (f32[1,2,256,256]{3,2,1,0:T(8,128)S(1)}, f32[1,2,256,256]{3,2,1,0:T(8,128)}, u32[]{:S(2)}) copy-start(f32[1,2,256,256]{3,2,1,0:T(8,128)} %param.9) | copy-start | bytes 1572868
  1.8 82.0 %all-to-all-start = ((bf16[16,2,16,512]{3,2,1,0:T(8,128)(2,1)}), bf16[16,2,16,512]{3,2,1,0:T(8,128)(2,1)S(1)}, u32[]{:S(2)}, u32[]{:S(2)}) async-start(bf16[16,2,16,512]{3,2,1,0:T(8,128)(2,1)} %broadcast_in_dim.2), calls=%async_computation | async-start | bytes 1048576 | tf_op jit(solution)/shard_map/all_to_all | solution.py:216
  17.6 5.7 %collective-permute-start.1 = (bf16[1,2,128,256]{3,2,1,0:T(8,128)(2,1)S(1)}, bf16[1,2,128,256]{3,2,1,0:T(8,128)(2,1)S(1)}, u32[]{:S(2)}, u32[]{:S(2)}) collective-permute-start(bf16[1,2,128,256]{3,2,1,0:T(8,128)(2,1)S(1)} %dynamic-slice_convert_fusion), channel_id=1, source_target_pairs={{0,16},{16,0},{1,17},{17,1},{2,18},{18,2},{3,19},{19,3},{4,20},{20... | collective-permute-start | bytes 393224 | tf_op jit(solution)/shard_map/ppermute | solution.py:249
  23.3 42.9 %collective-permute-start.4 = (bf16[2,2,128,256]{3,2,1,0:T(8,128)(2,1)S(1)}, bf16[2,2,128,256]{3,2,1,0:T(8,128)(2,1)S(1)}, u32[]{:S(2)}, u32[]{:S(2)}) collective-permute-start(bf16[2,2,128,256]{3,2,1,0:T(8,128)(2,1)S(1)} %pad_maximum_fusion.pair_ref), channel_id=1, source_target_pairs={{0,12},{4,0},{8,4},{12,8},{1,13},{5,1},{9,5},{13,9},{2,14},{6,2},{... | collective-permute-start | bytes 786440 | tf_op jit(solution)/shard_map/ppermute | solution.py:251
  30.5 40.7 %collective-permute-start.3 = (bf16[2,2,128,256]{3,2,1,0:T(8,128)(2,1)S(1)}, bf16[2,2,128,256]{3,2,1,0:T(8,128)(2,1)S(1)}, u32[]{:S(2)}, u32[]{:S(2)}) collective-permute-start(bf16[2,2,128,256]{3,2,1,0:T(8,128)(2,1)S(1)} %pad_maximum_fusion.pair_ref), channel_id=1, source_target_pairs={{0,8},{4,12},{8,0},{12,4},{1,9},{5,13},{9,1},{13,5},{2,10},{6,14},... | collective-permute-start | bytes 786440 | tf_op jit(solution)/shard_map/ppermute | solution.py:251
  37.5 46.2 %collective-permute-start.2 = (bf16[2,2,128,256]{3,2,1,0:T(8,128)(2,1)S(1)}, bf16[2,2,128,256]{3,2,1,0:T(8,128)(2,1)S(1)}, u32[]{:S(2)}, u32[]{:S(2)}) collective-permute-start(bf16[2,2,128,256]{3,2,1,0:T(8,128)(2,1)S(1)} %pad_maximum_fusion.pair_ref), channel_id=1, source_target_pairs={{0,4},{4,8},{8,12},{12,0},{1,5},{5,9},{9,13},{13,1},{2,6},{6,10},{... | collective-permute-start | bytes 786440 | tf_op jit(solution)/shard_map/ppermute | solution.py:251
  45.5 9.5 %collective-permute-start = (s32[16]{0:T(128)S(1)}, s32[16]{0:T(128)S(1)}, u32[]{:S(2)}, u32[]{:S(2)}) collective-permute-start(s32[16]{0:T(128)S(1)} %pad_add_fusion.1), channel_id=1, source_target_pairs={{0,32},{32,64},{64,96},{96,128},{128,160},{160,192},{192,224},{224... | collective-permute-start | bytes 200 | tf_op jit(solution)/shard_map/ppermute | solution.py:243
  83.8 0.7 copy-start.4
  85.8 21.1 %collective-permute-start.8 = (bf16[4,2,2,128,256]{4,3,2,1,0:T(8,128)(2,1)S(1)}, bf16[4,2,2,128,256]{4,3,2,1,0:T(8,128)(2,1)S(1)}, u32[]{:S(2)}, u32[]{:S(2)}) collective-permute-start(bf16[4,2,2,128,256]{4,3,2,1,0:T(8,128)(2,1)S(1)} %get-tuple-element.16.here_ref), channel_id=1, source_target_pairs={{0,32},{32,0},{1,33},{33,1},{2,34},{34,2},{3,35},{35,3},{4,36},{36... | collective-permute-start | bytes 3145736 | tf_op jit(solution)/shard_map/ppermute | solution.py:265
  89.1 9.8 %collective-permute-start.5 = (bf16[2,256,256]{2,1,0:T(8,128)(2,1)S(1)}, bf16[2,256,256]{2,1,0:T(8,128)(2,1)S(1)}, u32[]{:S(2)}, u32[]{:S(2)}) collective-permute-start(bf16[2,256,256]{2,1,0:T(8,128)(2,1)S(1)} %get-tuple-element.13), channel_id=1, source_target_pairs={{0,16},{16,0},{1,17},{17,1},{2,18},{18,2},{3,19},{19,3},{4,20},{20... | collective-permute-start | bytes 786440 | tf_op jit(solution)/shard_map/ppermute | solution.py:266
  92.2 14.6 %collective-permute-start.6 = (bf16[2,256,256]{2,1,0:T(8,128)(2,1)S(1)}, bf16[2,256,256]{2,1,0:T(8,128)(2,1)S(1)}, u32[]{:S(2)}, u32[]{:S(2)}) collective-permute-start(bf16[2,256,256]{2,1,0:T(8,128)(2,1)S(1)} %get-tuple-element.14), channel_id=1, source_target_pairs={{32,0},{64,32},{96,64},{128,96},{160,128},{192,160},{224,192},{256... | collective-permute-start | bytes 786440 | tf_op jit(solution)/shard_map/ppermute | solution.py:267
  94.5 12.4 %collective-permute-start.7 = (bf16[2,256,256]{2,1,0:T(8,128)(2,1)S(1)}, bf16[2,256,256]{2,1,0:T(8,128)(2,1)S(1)}, u32[]{:S(2)}, u32[]{:S(2)}) collective-permute-start(bf16[2,256,256]{2,1,0:T(8,128)(2,1)S(1)} %get-tuple-element.15), channel_id=1, source_target_pairs={{32,16},{64,48},{96,80},{128,112},{160,144},{192,176},{224,208},{2... | collective-permute-start | bytes 786440 | tf_op jit(solution)/shard_map/ppermute | solution.py:268
  106.9 1.0 copy-start.2
  107.9 1.0 copy-start.3
  109.0 0.7 copy-start.5
  109.6 28.7 %copy-start.1 = (f32[1,8,256,256]{3,2,1,0:T(8,128)S(1)}, f32[1,8,256,256]{3,2,1,0:T(8,128)}, u32[]{:S(2)}) copy-start(f32[1,8,256,256]{3,2,1,0:T(8,128)} %param.10) | copy-start | bytes 6291460
  138.3 56.1 %copy-start.6 = (f32[2,16,512]{2,1,0:T(8,128)S(1)}, f32[2,16,512]{2,1,0:T(8,128)}, u32[]{:S(2)}) copy-start(f32[2,16,512]{2,1,0:T(8,128)} %param.8) | copy-start | bytes 196612
  145.1 7.7 %collective-permute-start.11 = (bf16[2,256,256]{2,1,0:T(8,128)(2,1)S(1)}, bf16[2,256,256]{2,1,0:T(8,128)(2,1)S(1)}, u32[]{:S(2)}, u32[]{:S(2)}) collective-permute-start(bf16[2,256,256]{2,1,0:T(8,128)(2,1)S(1)} %backward.1.own_ref), channel_id=1, source_target_pairs={{16,32},{48,64},{80,96},{112,128},{144,160},{176,192},{208,224},{2... | collective-permute-start | bytes 786440 | tf_op jit(solution)/shard_map/ppermute | solution.py:306
  146.4 9.1 %collective-permute-start.10 = (bf16[2,256,256]{2,1,0:T(8,128)(2,1)S(1)}, bf16[2,256,256]{2,1,0:T(8,128)(2,1)S(1)}, u32[]{:S(2)}, u32[]{:S(2)}) collective-permute-start(bf16[2,256,256]{2,1,0:T(8,128)(2,1)S(1)} %backward.1.own_ref), channel_id=1, source_target_pairs={{0,32},{32,64},{64,96},{96,128},{128,160},{160,192},{192,224},{224... | collective-permute-start | bytes 786440 | tf_op jit(solution)/shard_map/ppermute | solution.py:305
  150.7 8.9 %collective-permute-start.9 = (bf16[2,256,256]{2,1,0:T(8,128)(2,1)S(1)}, bf16[2,256,256]{2,1,0:T(8,128)(2,1)S(1)}, u32[]{:S(2)}, u32[]{:S(2)}) collective-permute-start(bf16[2,256,256]{2,1,0:T(8,128)(2,1)S(1)} %backward.1.own_ref), channel_id=1, source_target_pairs={{0,16},{16,0},{1,17},{17,1},{2,18},{18,2},{3,19},{19,3},{4,20},{20... | collective-permute-start | bytes 786440 | tf_op jit(solution)/shard_map/ppermute | solution.py:304

commit v3 on v2

v3 whole, which is shorter than its diff:
```python
import math

import jax
import jax.numpy as jnp
import numpy as np
from jax import lax
from jax.experimental import pallas as pl
from jax.experimental.pallas import tpu as pltpu
from jax.sharding import Mesh, PartitionSpec as P

step_size = 0.05
f32 = jnp.float32
bf16 = jnp.bfloat16
TILE_AXES = ("y", "xh", "c")
DEPTH_AXES = ("zq", "zr")
STEPS = 2
CHUNK = 16
QUARTERS = 4
RUN = 4
VMEM_LIMIT = 48 * 1024 * 1024


def dft_blocks(length):
    freqs = np.arange(length, dtype=np.int32)
    turns = freqs[:, None] * freqs[None, :] % length
    phase = turns.astype(np.float32) * np.float32(2.0 * math.pi / length)
    norm_scale = np.float32(1.0 / math.sqrt(length))
    cos_table = (np.cos(phase) * norm_scale).astype(jnp.bfloat16)
    sin_table = (-np.sin(phase) * norm_scale).astype(jnp.bfloat16)
    right = np.block([[cos_table, sin_table], [-sin_table, cos_table]])
    left = np.block([[cos_table, -sin_table], [sin_table, cos_table]])
    return right, left


def dot(left_side, right_side):
    return jnp.dot(left_side, right_side, preferred_element_type=f32)


def on_top(beside):
    size = beside.shape[1] // 2
    return jnp.concatenate([beside[:, :size], beside[:, size:]], axis=0)


def one_hot(rows, columns, offset):
    row = lax.broadcasted_iota(jnp.int32, (rows, columns), 0)
    column = lax.broadcasted_iota(jnp.int32, (rows, columns), 1)
    return (column == row + offset).astype(f32).astype(bf16)


def one_hot_down(rows, columns, offset):
    row = lax.broadcasted_iota(jnp.int32, (rows, columns), 0)
    column = lax.broadcasted_iota(jnp.int32, (rows, columns), 1)
    return (row == column + offset).astype(f32).astype(bf16)


def first_row(row_start, member):
    return (row_start // CHUNK - member + RUN - 1) // RUN * CHUNK


def class_rows(touched, window, row_start, across):
    blocks = []
    for member in range(RUN):
        shape = (window, touched) if across else (touched, window)
        spot = lax.broadcasted_iota(jnp.int32, shape, 1 if across else 0)
        row = lax.broadcasted_iota(jnp.int32, shape, 0 if across else 1)
        chunk = (first_row(row_start, member) // CHUNK + spot // CHUNK) * RUN + member
        blocks.append((chunk * CHUNK + spot % CHUNK == row + row_start).astype(f32).astype(bf16))
    return jnp.concatenate(blocks, axis=1 if across else 0)


def cut_kernel(
    meta_ref, scan_ref, above_ref, packed_ref, own_ref, partner_ref, upper_ref, lower_ref, probe_ref
):
    chunks, _, _, width = packed_ref.shape
    window = own_ref.shape[-1]
    quarters = chunks
    slots = 2 * quarters
    lane, quarter = meta_ref[0], meta_ref[1]
    starts = (
        scan_ref[slots + lane * quarters + quarter],
        scan_ref[slots + (1 - lane) * quarters + quarter],
        above_ref[slots + quarter],
        above_ref[slots + quarters + quarter],
    )
    pick = jnp.concatenate([one_hot_down(width, window, start) for start in starts], axis=1)
    for part in range(2):
        rows = jnp.concatenate([packed_ref[chunk, part, :CHUNK] for chunk in range(chunks)], axis=0)
        columns = dot(rows, pick).astype(bf16)
        for index, target in enumerate((own_ref, partner_ref, upper_ref, lower_ref)):
            target[part] = columns[:, index * window : (index + 1) * window]
        for chunk in range(chunks):
            probe_ref[chunk, part] = packed_ref[chunk, part, CHUNK:]


def touch_kernel(
    meta_ref, scan_ref, own_ref, other_ref, below0_ref, below1_ref, touched_ref
):
    lane, quarter, member = meta_ref[0], meta_ref[1], meta_ref[5]
    height = own_ref.shape[1]
    touched = touched_ref.shape[1]
    row_start = scan_ref[lane * QUARTERS + quarter]
    first = first_row(row_start, member)
    pick = jnp.concatenate(
        [
            one_hot(touched, height, first - lane * height),
            one_hot(touched, height, first - (1 - lane) * height),
            one_hot(touched, height, first - 2 * height),
        ],
        axis=1,
    )
    for part in range(2):
        below = below0_ref[part] + below1_ref[part]
        stack = jnp.concatenate([own_ref[part], other_ref[part], below], axis=0)
        touched_ref[part] = dot(pick, stack).astype(bf16)


def full_probe(here_ref, there_ref, meta_ref, mode):
    core, up = meta_ref[2], meta_ref[6]
    count = here_ref.shape[0]
    window = here_ref.shape[-1] // 2

    def rows(part):
        pieces = []
        for row in range(count):
            place = lax.rem(up - row + count, count)
            here = here_ref[place, mode, part].astype(f32)
            there = there_ref[place, mode, part].astype(f32)
            for piece in (jnp.where(core == 0, here, there), jnp.where(core == 0, there, here)):
                pieces += [piece[:, :window], piece[:, window:]]
        return jnp.concatenate(pieces, axis=0)

    return rows(0), rows(1)


def forward_kernel(
    meta_ref, scan_ref, touched_ref, here_ref, there_ref,
    right_ref, left_ref, spec_ref, power_ref, patch, total,
):
    step = pl.program_id(0)
    lane, quarter = meta_ref[0], meta_ref[1]
    window = power_ref.shape[-1]
    row_start = scan_ref[lane * QUARTERS + quarter]

    @pl.when(step == 0)
    def _():
        pick = class_rows(touched_ref.shape[2], window, row_start, True)
        for part in range(2):
            stack = jnp.concatenate([touched_ref[member, part] for member in range(RUN)], axis=0)
            patch[part] = dot(pick, stack)
        total[...] = jnp.zeros_like(total)

    for mode in range(here_ref.shape[1]):
        probe_real, probe_imag = full_probe(here_ref, there_ref, meta_ref, mode)
        exit_real = (probe_real * patch[0] - probe_imag * patch[1]).astype(bf16)
        exit_imag = (probe_real * patch[1] + probe_imag * patch[0]).astype(bf16)
        half_spectrum = dot(jnp.concatenate([exit_real, exit_imag], axis=1), right_ref[...])
        spectrum = dot(left_ref[...], on_top(half_spectrum.astype(bf16)))
        spec_ref[0, mode] = spectrum
        squares = spectrum * spectrum
        total[...] = total[...] + (squares[:window] + squares[window:])

    @pl.when(step == pl.num_programs(0) - 1)
    def _():
        power_ref[...] = total[...].astype(bf16)


def backward_kernel(
    meta_ref, scan_ref, spec_ref, powers_ref, amplitude_ref, here_ref, there_ref, right_ref, left_ref,
    pieces_ref, factor, sums,
):
    step = pl.program_id(0)
    slot = meta_ref[0] * QUARTERS + meta_ref[1]
    alive = slot < scan_ref[4 * QUARTERS + meta_ref[3]]
    window = pieces_ref.shape[-1]

    @pl.when(step == 0)
    def _():
        intensity = powers_ref[0].astype(f32)
        for member in range(1, powers_ref.shape[0]):
            intensity = intensity + powers_ref[member].astype(f32)
        correction = 1.0 - amplitude_ref[0] / jnp.sqrt(intensity + 1.0)
        factor[...] = jnp.where(alive, correction, 0.0)
        sums[...] = jnp.zeros_like(sums)

    for mode in range(here_ref.shape[1]):
        wave_real = (spec_ref[0, mode, :window] * factor[...]).astype(bf16)
        wave_imag = (spec_ref[0, mode, window:] * factor[...]).astype(bf16)
        back_half = dot(jnp.concatenate([wave_real, wave_imag], axis=1), left_ref[...])
        back_wave = dot(right_ref[...], on_top(back_half.astype(bf16)))
        back_real, back_imag = back_wave[:window], back_wave[window:]
        probe_real, probe_imag = full_probe(here_ref, there_ref, meta_ref, mode)
        sums[0] = sums[0] + (probe_real * back_real + probe_imag * back_imag)
        sums[1] = sums[1] + (probe_real * back_imag - probe_imag * back_real)

    @pl.when(step == pl.num_programs(0) - 1)
    def _():
        row_start = scan_ref[slot]
        touched = pieces_ref.shape[2]
        deal = class_rows(touched, window, row_start, False)
        for part in range(2):
            dealt = dot(deal, sums[part].astype(bf16)).astype(bf16)
            for member in range(RUN):
                pieces_ref[member, part] = dealt[member * touched : (member + 1) * touched]


def place_kernel(
    meta_ref, scan_ref, above_ref, own_ref, partner_ref, upper_ref, lower_ref, half_ref
):
    chunks, _, chunk_rows, width = half_ref.shape
    height = chunks * chunk_rows
    _, touched, window = own_ref.shape
    quarters = chunks
    slots = 2 * quarters
    lane, quarter, member = meta_ref[0], meta_ref[1], meta_ref[5]
    mine, partners = lane * quarters + quarter, (1 - lane) * quarters + quarter
    first, second = quarter, quarters + quarter
    row_starts = (
        first_row(scan_ref[mine], member) - lane * height,
        first_row(scan_ref[partners], member) - lane * height,
        first_row(above_ref[first], member) - 2 * height,
        first_row(above_ref[second], member) - 2 * height,
    )
    col_starts = (
        scan_ref[slots + mine], scan_ref[slots + partners], above_ref[slots + first], above_ref[slots + second]
    )
    spread = jnp.concatenate([one_hot(window, width, start) for start in col_starts], axis=0)
    sources = (own_ref, partner_ref, upper_ref, lower_ref)
    shifts = [one_hot_down(height, touched, start) for start in row_starts]
    for part in range(2):
        moved = [dot(shift, source[part]).astype(bf16) for shift, source in zip(shifts, sources)]
        placed = dot(jnp.concatenate(moved, axis=1), spread).astype(bf16)
        for chunk in range(chunks):
            half_ref[chunk, part] = placed[chunk * chunk_rows : (chunk + 1) * chunk_rows]


def whole(shape):
    return pl.BlockSpec(shape, lambda step, *_: (0,) * len(shape))


def per_step(shape):
    return pl.BlockSpec((1,) + shape, lambda step, *_: (step,) + (0,) * len(shape))


def call(kernel, name, scalars, operands, in_specs, results, out_specs, steps=1, scratch=(), flops=0):
    return pl.pallas_call(
        kernel,
        grid_spec=pltpu.PrefetchScalarGridSpec(
            num_scalar_prefetch=len(scalars),
            grid=(steps,),
            in_specs=in_specs,
            out_specs=out_specs,
            scratch_shapes=scratch,
        ),
        out_shape=results,
        compiler_params=pltpu.CompilerParams(vmem_limit_bytes=VMEM_LIMIT),
        cost_estimate=pl.CostEstimate(
            flops=flops, bytes_accessed=4 * 1024 * 1024, transcendentals=0
        ),
        name=name,
    )(*scalars, *operands)


def on_device(
    object_field, probe_modes, measured_amplitude, row_offsets, col_offsets, position_counts
):
    window = probe_modes.shape[-1]
    slots = row_offsets.shape[1]
    width = object_field.shape[2]
    chunk_rows = object_field.shape[1]
    quarters = lax.axis_size("zq")
    tiles = lax.axis_size(TILE_AXES)
    lane, quarter, core = lax.axis_index("xl"), lax.axis_index("zq"), lax.axis_index("c")
    right, left = (jnp.asarray(table) for table in dft_blocks(window))
    swap = [(0, 1), (1, 0)]
    axes = TILE_AXES + ("xl",)
    up_first = [(2 * (t + 1), 2 * t) for t in range(tiles - 1)]
    up_second = [(2 * (t + 1), 2 * t + 1) for t in range(tiles - 1)]
    down_first = [(2 * t, 2 * (t + 1)) for t in range(tiles - 1)]
    down_second = [(2 * t + 1, 2 * (t + 1)) for t in range(tiles - 1)]
    downwards = [(t, t + 1) for t in range(tiles - 1)]

    up = lax.axis_index("y")
    member, tile = lax.axis_index("zr"), lax.axis_index(TILE_AXES)
    meta = jnp.stack([lane, quarter, core, tile, up * 2 + core, member, up]).astype(jnp.int32)
    scan = jnp.concatenate([row_offsets[0], col_offsets[0], position_counts])
    above = lax.ppermute(scan, TILE_AXES, downwards)

    ups = lax.axis_size("y")
    piece_rows = 2 * chunk_rows
    piece = lax.dynamic_slice_in_dim(probe_modes[0], (up * 2 + core) * piece_rows, piece_rows, axis=1)
    piece = jnp.concatenate([piece[:, :chunk_rows], piece[:, chunk_rows:]], axis=2)
    packed = jnp.concatenate([object_field, piece], axis=1).astype(bf16)
    packed = jnp.broadcast_to(packed[None], (quarters,) + packed.shape)
    packed = lax.all_to_all(packed, "zq", 0, 0, tiled=True)
    cut_shape = (2, quarters * chunk_rows, window)
    lane_shape = (quarters, 2, chunk_rows, width)
    own, partner, upper, lower, lane_modes = call(
        cut_kernel, "cut", (meta, scan, above), (packed,), [whole(packed.shape)],
        [jax.ShapeDtypeStruct(cut_shape, bf16)] * 4 + [jax.ShapeDtypeStruct(lane_shape, bf16)],
        [whole(cut_shape)] * 4 + [whole(lane_shape)],
    )
    other_modes = lax.ppermute(lane_modes, "xl", swap)
    other = lax.ppermute(partner, "xl", swap)
    below0 = lax.ppermute(upper, axes, up_first)
    below1 = lax.ppermute(lower, axes, up_second)
    lane_modes, other_modes, other, below0, below1 = lax.optimization_barrier(
        (lane_modes, other_modes, other, below0, below1)
    )
    part_modes = jnp.concatenate([lane_modes, other_modes], axis=0)
    shared = [
        lax.ppermute(part_modes, "y", [(i, (i + d) % ups) for i in range(ups)]) for d in range(1, ups)
    ]
    touched_shape = (2, window // RUN + CHUNK, window)
    touched = call(
        touch_kernel, "touch", (meta, scan), (own, other, below0, below1), [whole(cut_shape)] * 4,
        jax.ShapeDtypeStruct(touched_shape, bf16), whole(touched_shape),
    )
    touched = lax.all_gather(touched, "zr", axis=0)
    *shared, touched = lax.optimization_barrier((*shared, touched))
    here = jnp.stack([part_modes, *shared])
    there = lax.ppermute(here, "c", swap)
    window_shape = (2, window, window)

    modes = here.shape[1]
    at_once = modes // STEPS
    product_flops = modes * 2 * 2 * (2 * window) ** 2 * window
    probe_block = pl.BlockSpec(
        here.shape[:1] + (at_once,) + here.shape[2:], lambda step, *_: (0, step, 0, 0, 0)
    )
    spec_shape = (at_once, 2 * window, window)
    spectrum, power = call(
        forward_kernel, "forward", (meta, scan),
        (touched, here, there, right, left),
        [whole(touched.shape)] + [probe_block] * 2 + [whole(right.shape), whole(left.shape)],
        [
            jax.ShapeDtypeStruct((STEPS,) + spec_shape, f32),
            jax.ShapeDtypeStruct((window, window), bf16),
        ],
        [per_step(spec_shape), whole((window, window))],
        steps=STEPS,
        scratch=[pltpu.VMEM(window_shape, f32), pltpu.VMEM((window, window), f32)],
        flops=product_flops,
    )
    powers = lax.all_gather(power, "zr", axis=0)

    slot_block = pl.BlockSpec(
        (1, window, window), lambda step, meta_ref, *_: (meta_ref[0] * quarters + meta_ref[1], 0, 0)
    )
    pieces = call(
        backward_kernel, "backward", (meta, scan),
        (spectrum, powers, measured_amplitude[0], here, there, right, left),
        [per_step(spec_shape), whole(powers.shape), slot_block]
        + [probe_block] * 2 + [whole(right.shape), whole(left.shape)],
        jax.ShapeDtypeStruct(touched.shape, bf16),
        whole(touched.shape),
        steps=STEPS,
        scratch=[pltpu.VMEM((window, window), f32), pltpu.VMEM(window_shape, f32)],
        flops=product_flops,
    )
    pieces = lax.all_to_all(pieces, "zr", 0, 0, tiled=True)
    term = jnp.sum(pieces.astype(f32), axis=0).astype(bf16)
    partners = lax.ppermute(term, "xl", swap)
    above0 = lax.ppermute(term, axes, down_first)
    above1 = lax.ppermute(term, axes, down_second)
    half_sum = call(
        place_kernel, "place", (meta, scan, above), (term, partners, above0, above1),
        [whole(touched_shape)] * 4,
        jax.ShapeDtypeStruct(lane_shape, bf16), whole(lane_shape),
    )
    terms = lax.all_to_all(half_sum, "zq", 0, 0, tiled=True)
    return object_field - step_size * jnp.sum(terms.astype(f32), axis=0)


def solution(mesh):
    tiles, modes = mesh.devices.shape
    parts = Mesh(
        mesh.devices.reshape(tiles // 4, 2, 2, 2, 4, modes // 8), TILE_AXES + ("xl",) + DEPTH_AXES
    )
    tile, mode = TILE_AXES, ("xl",) + DEPTH_AXES
    placed = (
        P(None, tile + mode, None),
        P(mode, None, None, None),
        P(tile, None, None, None),
        P(tile, None),
        P(tile, None),
        P(),
    )
    return jax.shard_map(
        on_device,
        mesh=parts,
        in_specs=placed,
        out_specs=P(None, tile + mode, None),
        check_vma=False,
    )
```

time: 196 us -> 153 us (0.78)
  waiting for transfers between devices: 49.3 us -> 15.7 us
  starting transfers between devices: 65.2 us -> 61.3 us
  local copies, waits for them, and re-layouts: 5.58 us -> 1.87 us
    ppermute x5, waiting for transfers between devices: 31.3 us -> 0.61 us  [the longest x1 0.6 us: on_device(): above = lax.ppermute(scan, TILE_AXES, downwards)]
    ppermute x5, starting transfers between devices: 32 us -> 18.1 us  [the longest x3 9.5 us: on_device(): lax.ppermute(part_modes, 'y', [(i, (i + d) % ups) for i in range(ups)])]
    all_gather x0 -> x1, blocking collectives: none -> 13.8 us  [on_device(): touched = lax.all_gather(touched, 'zr', axis=0)]
    all_gather x1, blocking collectives: 22.1 us -> 13.1 us  [on_device(): powers = lax.all_gather(power, 'zr', axis=0)]
    all_to_all x1, waiting for transfers between devices: 0.01 us -> 6.82 us  [on_device(): packed = lax.all_to_all(packed, 'zq', 0, 0, tiled=True)]
    ppermute x1, starting transfers between devices: 2.2 us -> 8.22 us  [on_device(): below0 = lax.ppermute(upper, axes, up_first)]
    ppermute x1, waiting for transfers between devices: 7.92 us -> 2.79 us  [on_device(): below0 = lax.ppermute(upper, axes, up_first)]
    all_to_all x1 -> x2, blocking collectives: 32.9 us -> 28.6 us  [the longest x1 18.6 us: on_device(): terms = lax.all_to_all(half_sum, 'zq', 0, 0, tiled=True)]
  transfers between devices with their start and end apart: 13 -> 13, of which waited for: 9 -> 5; matrix products, arithmetic and copies ran while one was open for 1% -> 1% of each run, Pallas kernels for 0% -> 1%
where the time goes in v3:
time: 153 us; the launch traced here: 152 us
  starting transfers between devices  61.3 us (40%)
  blocking collectives  55.4 us (36%)
  waiting for transfers between devices  15.7 us (10%)
  Pallas kernels  15.4 us (10%)
  other arithmetic  2.46 us (2%)
  local copies, waits for them, and re-layouts  1.87 us (1%)
    all_to_all x1, blocking collectives, on_device(): terms = lax.all_to_all(half_sum, 'zq', 0, 0, tiled=True)  18.6 us
    all_to_all x1, starting transfers between devices, on_device(): packed = lax.all_to_all(packed, 'zq', 0, 0, tiled=True)  15.6 us
    pallas_call x5, Pallas kernels, call(): pl.pallas_call(kernel, grid_spec=pltpu.PrefetchScalarGridSpec(num_scalar_...  15.4 us
    all_gather x1, blocking collectives, on_device(): touched = lax.all_gather(touched, 'zr', axis=0)  13.8 us
    all_gather x1, blocking collectives, on_device(): powers = lax.all_gather(power, 'zr', axis=0)  13.1 us
    all_to_all x1, blocking collectives, on_device(): pieces = lax.all_to_all(pieces, 'zr', 0, 0, tiled=True)  9.96 us
    ppermute x3, starting transfers between devices, on_device(): lax.ppermute(part_modes, 'y', [(i, (i + d) % ups) for i in range(ups)])  9.5 us
    ppermute x1, starting transfers between devices, on_device(): below0 = lax.ppermute(upper, axes, up_first)  8.22 us
  transfers between devices with their start and end apart: 13, of which 5 were waited for; matrix products, arithmetic and copies ran while one was open for 1% of the time, Pallas kernels for 1%

profile of v3, /device:TPU:1, one launch (start us, length us, event | category | flops | bytes accessed | tf_op | source)
XLA Modules:
  0.0 152.4 jit_solution(5449517254564978025)
XLA Ops:
  0.0 0.0 copy-start
  0.0 0.0 copy-start.2
  0.0 0.0 copy-start.3
  0.0 1.0 copy-done
  1.1 0.8 convert.11
  1.9 0.7 broadcast_in_dim.2
  2.6 15.6 %all-to-all-start = ((bf16[4,2,32,512]{3,2,1,0:T(8,128)(2,1)}), bf16[4,2,32,512]{3,2,1,0:T(8,128)(2,1)S(1)}, u32[]{:S(2)}, u32[]{:S(2)}) async-start(bf16[4,2,32,512]{3,2,1,0:T(8,128)(2,1)} %broadcast_in_dim.2), calls=%async_computation | async-start | bytes 524288 | tf_op jit(solution)/shard_map/all_to_all | solution.py:294
  18.3 0.8 pad_add_fusion.scan_ref
  19.0 5.5 %collective-permute-start = (s32[32]{0:T(128)S(1)}, s32[32]{0:T(128)S(1)}, u32[]{:S(2)}, u32[]{:S(2)}) collective-permute-start(s32[32]{0:T(128)S(1)} %pad_add_fusion.scan_ref), channel_id=1, source_target_pairs={{0,32},{32,64},{64,96},{96,128},{128,160},{160,192},{192,224},{224... | collective-permute-start | bytes 392 | tf_op jit(solution)/shard_map/ppermute | solution.py:286
  24.5 0.1 stack.46.meta_ref
  24.6 0.6 collective-permute-done.above_ref
  25.2 6.8 %all-to-all-done.packed_ref = bf16[4,2,32,512]{3,2,1,0:T(8,128)(2,1)S(1)} async-done(((bf16[4,2,32,512]{3,2,1,0:T(8,128)(2,1)}), bf16[4,2,32,512]{3,2,1,0:T(8,128)(2,1)S(1)}, u32[]{:S(2)}, u32[]{:S(2)}) %all-to-all-start) | async-done | bytes 262176 | tf_op jit(solution)/shard_map/all_to_all | solution.py:294
  32.0 1.1 cut.1
  33.2 3.1 %collective-permute-start.1 = (bf16[4,2,16,512]{3,2,1,0:T(8,128)(2,1)S(1)}, bf16[4,2,16,512]{3,2,1,0:T(8,128)(2,1)S(1)}, u32[]{:S(2)}, u32[]{:S(2)}) collective-permute-start(bf16[4,2,16,512]{3,2,1,0:T(8,128)(2,1)S(1)} %get-tuple-element.25), channel_id=1, source_target_pairs={{0,16},{16,0},{1,17},{17,1},{2,18},{18,2},{3,19},{19,3},{4,20},{20... | collective-permute-start | bytes 393224 | tf_op jit(solution)/shard_map/ppermute | solution.py:302
  36.3 2.2 %collective-permute-start.2 = (bf16[2,64,256]{2,1,0:T(8,128)(2,1)S(1)}, bf16[2,64,256]{2,1,0:T(8,128)(2,1)S(1)}, u32[]{:S(2)}, u32[]{:S(2)}) collective-permute-start(bf16[2,64,256]{2,1,0:T(8,128)(2,1)S(1)} %get-tuple-element.22), channel_id=1, source_target_pairs={{0,16},{16,0},{1,17},{17,1},{2,18},{18,2},{3,19},{19,3},{4,20},{20... | collective-permute-start | bytes 196616 | tf_op jit(solution)/shard_map/ppermute | solution.py:303
  38.5 8.2 %collective-permute-start.3 = (bf16[2,64,256]{2,1,0:T(8,128)(2,1)S(1)}, bf16[2,64,256]{2,1,0:T(8,128)(2,1)S(1)}, u32[]{:S(2)}, u32[]{:S(2)}) collective-permute-start(bf16[2,64,256]{2,1,0:T(8,128)(2,1)S(1)} %get-tuple-element.23), channel_id=1, source_target_pairs={{32,0},{64,32},{96,64},{128,96},{160,128},{192,160},{224,192},{256... | collective-permute-start | bytes 196616 | tf_op jit(solution)/shard_map/ppermute | solution.py:304
  46.7 1.8 %collective-permute-start.4 = (bf16[2,64,256]{2,1,0:T(8,128)(2,1)S(1)}, bf16[2,64,256]{2,1,0:T(8,128)(2,1)S(1)}, u32[]{:S(2)}, u32[]{:S(2)}) collective-permute-start(bf16[2,64,256]{2,1,0:T(8,128)(2,1)S(1)} %get-tuple-element.24), channel_id=1, source_target_pairs={{32,16},{64,48},{96,80},{128,112},{160,144},{192,176},{224,208},{2... | collective-permute-start | bytes 196616 | tf_op jit(solution)/shard_map/ppermute | solution.py:305
  48.5 0.0 collective-permute-done.2.other_ref
  48.5 2.8 %collective-permute-done.3.below0_ref = bf16[2,64,256]{2,1,0:T(8,128)(2,1)S(1)} collective-permute-done((bf16[2,64,256]{2,1,0:T(8,128)(2,1)S(1)}, bf16[2,64,256]{2,1,0:T(8,128)(2,1)S(1)}, u32[]{:S(2)}, u32[]{:S(2)}) %collective-permute-start.3) | collective-permute-done | bytes 65568 | tf_op jit(solution)/shard_map/ppermute | solution.py:304
  51.3 0.0 collective-permute-done.4.below1_ref
  51.3 0.0 collective-permute-done.1
  51.3 4.6 %collective-permute-start.7 = (bf16[8,2,16,512]{3,2,1,0:T(8,128)(2,1)S(1)}, bf16[8,2,16,512]{3,2,1,0:T(8,128)(2,1)S(1)}, u32[]{:S(2)}, u32[]{:S(2)}) collective-permute-start(bf16[8,2,16,512]{3,2,1,0:T(8,128)(2,1)S(1)} %constant_dynamic-update-slice_fusion), channel_id=1, source_target_pairs={{0,384},{128,0},{256,128},{384,256},{1,385},{129,1},{257,129},{385... | collective-permute-start | bytes 786440 | tf_op jit(solution)/shard_map/ppermute | solution.py:311
  56.0 2.3 %collective-permute-start.6 = (bf16[8,2,16,512]{3,2,1,0:T(8,128)(2,1)S(1)}, bf16[8,2,16,512]{3,2,1,0:T(8,128)(2,1)S(1)}, u32[]{:S(2)}, u32[]{:S(2)}) collective-permute-start(bf16[8,2,16,512]{3,2,1,0:T(8,128)(2,1)S(1)} %constant_dynamic-update-slice_fusion), channel_id=1, source_target_pairs={{0,256},{128,384},{256,0},{384,128},{1,257},{129,385},{257,1},{385... | collective-permute-start | bytes 786440 | tf_op jit(solution)/shard_map/ppermute | solution.py:311
  58.2 2.6 %collective-permute-start.5 = (bf16[8,2,16,512]{3,2,1,0:T(8,128)(2,1)S(1)}, bf16[8,2,16,512]{3,2,1,0:T(8,128)(2,1)S(1)}, u32[]{:S(2)}, u32[]{:S(2)}) collective-permute-start(bf16[8,2,16,512]{3,2,1,0:T(8,128)(2,1)S(1)} %constant_dynamic-update-slice_fusion), channel_id=1, source_target_pairs={{0,128},{128,256},{256,384},{384,0},{1,129},{129,257},{257,385},{3... | collective-permute-start | bytes 786440 | tf_op jit(solution)/shard_map/ppermute | solution.py:311
  60.8 0.8 touch.1
  61.6 13.8 %all-gather = bf16[8,80,256]{2,1,0:T(8,128)(2,1)S(1)} all-gather(bf16[2,80,256]{2,1,0:T(8,128)(2,1)S(1)} %touch.1), channel_id=2, replica_groups=mesh['y'=4,'xh'=2,'c'=2,'xl'=2,'zq'=4,'zr'=4] {'zr'}, dimensions={0}, use_global_device_ids=true | all-gather | bytes 409600 | tf_op jit(solution)/shard_map/all_gather | solution.py:318
  75.4 0.0 collective-permute-done.7
  75.4 0.0 collective-permute-done.6
  75.4 0.0 collective-permute-done.5
  75.4 0.1 pad_maximum_fusion.here_ref
  75.5 0.0 copy-start.1
  75.5 4.1 %collective-permute-start.8 = (bf16[4,8,2,16,512]{4,3,2,1,0:T(8,128)(2,1)S(1)}, bf16[4,8,2,16,512]{4,3,2,1,0:T(8,128)(2,1)S(1)}, u32[]{:S(2)}, u32[]{:S(2)}) collective-permute-start(bf16[4,8,2,16,512]{4,3,2,1,0:T(8,128)(2,1)S(1)} %pad_maximum_fusion.here_ref), channel_id=1, source_target_pairs={{0,32},{32,0},{1,33},{33,1},{2,34},{34,2},{3,35},{35,3},{4,36},{36... | collective-permute-start | bytes 3145736 | tf_op jit(solution)/shard_map/ppermute | solution.py:321
  79.6 2.3 %collective-permute-done.8.there_ref = bf16[4,8,2,16,512]{4,3,2,1,0:T(8,128)(2,1)S(1)} collective-permute-done((bf16[4,8,2,16,512]{4,3,2,1,0:T(8,128)(2,1)S(1)}, bf16[4,8,2,16,512]{4,3,2,1,0:T(8,128)(2,1)S(1)}, u32[]{:S(2)}, u32[]{:S(2)}) %collective-permute-start.8) | collective-permute-done | bytes 1048608 | tf_op jit(solution)/shard_map/ppermute | solution.py:321
  81.9 0.0 copy-done.2
  81.9 0.0 copy-done.3
  81.9 5.9 %forward.1 = (f32[2,4,512,256]{3,2,1,0:T(8,128)}, bf16[256,256]{1,0:T(8,128)(2,1)S(1)}) custom-call(s32[7]{0:T(128)S(1)} %stack.46.meta_ref, s32[32]{0:T(128)S(1)} %pad_add_fusion.scan_ref, bf16[4,2,80,256]{3,2,1,0:T(8,128)(2,1)S(1)} %bitcast.20, bf16[4,8,2,16,512]{4,3,2,1,0:T(8,128)(2,1)S(1)} %pad_maximum_fusion.here_ref, ...), custom_call_target="tpu_custom_call" | custom-call | flops 2147483648 | bytes 4194304 | tf_op jit(solution)/shard_map/forward/pallas_call | solution.py:245
  87.8 13.1 %all-gather.1 = bf16[1024,256]{1,0:T(8,128)(2,1)S(1)} all-gather(bf16[256,256]{1,0:T(8,128)(2,1)S(1)} %get-tuple-element.36), channel_id=3, replica_groups=mesh['y'=4,'xh'=2,'c'=2,'xl'=2,'zq'=4,'zr'=4] {'zr'}, dimensions={0}, use_global_device_ids=true | all-gather | bytes 655360 | tf_op jit(solution)/shard_map/all_gather | solution.py:344
  100.9 0.0 copy-done.1
  100.9 0.0 copy-start.4
  100.9 6.3 %backward.1 = bf16[4,2,80,256]{3,2,1,0:T(8,128)(2,1)S(1)} custom-call(s32[7]{0:T(128)S(1)} %stack.46.meta_ref, s32[32]{0:T(128)S(1)} %pad_add_fusion.scan_ref, f32[2,4,512,256]{3,2,1,0:T(8,128)} %get-tuple-element.35.spec_ref, bf16[4,256,256]{2,1,0:T(8,128)(2,1)S(1)} %bitcast.19, f32[8,256,256]{2,1,0:T(8,128)S(1)} %bitcast.18, ...), custom_call_target="tpu_custom_call" | custom-call | flops 2147483648 | bytes 4194304 | tf_op jit(solution)/shard_map/backward/pallas_call | solution.py:245
  107.2 10.0 %all_to_all.15 = bf16[4,2,80,256]{3,2,1,0:T(8,128)(2,1)S(1)} all-to-all(bf16[4,2,80,256]{3,2,1,0:T(8,128)(2,1)S(1)} %backward.1), channel_id=1, replica_groups=mesh['y'=4,'xh'=2,'c'=2,'xl'=2,'zq'=4,'zr'=4] {'zr'}, dimensions={0} | all-to-all | bytes 655360 | tf_op jit(solution)/shard_map/all_to_all | solution.py:360
  117.2 1.3 collective-permute-start.11
  118.5 8.1 %collective-permute-start.10 = (bf16[2,80,256]{2,1,0:T(8,128)(2,1)S(1)}, bf16[2,80,256]{2,1,0:T(8,128)(2,1)S(1)}, u32[]{:S(2)}, u32[]{:S(2)}) collective-permute-start(bf16[2,80,256]{2,1,0:T(8,128)(2,1)S(1)} %reduce_sum.21.own_ref), channel_id=1, source_target_pairs={{0,32},{32,64},{64,96},{96,128},{128,160},{160,192},{192,224},{224... | collective-permute-start | bytes 245768 | tf_op jit(solution)/shard_map/ppermute | solution.py:363
  126.6 1.9 %collective-permute-start.9 = (bf16[2,80,256]{2,1,0:T(8,128)(2,1)S(1)}, bf16[2,80,256]{2,1,0:T(8,128)(2,1)S(1)}, u32[]{:S(2)}, u32[]{:S(2)}) collective-permute-start(bf16[2,80,256]{2,1,0:T(8,128)(2,1)S(1)} %reduce_sum.21.own_ref), channel_id=1, source_target_pairs={{0,16},{16,0},{1,17},{17,1},{2,18},{18,2},{3,19},{19,3},{4,20},{20... | collective-permute-start | bytes 245768 | tf_op jit(solution)/shard_map/ppermute | solution.py:362
  128.5 0.0 collective-permute-done.11.lower_ref
  128.6 0.0 collective-permute-done.10.upper_ref
  128.6 3.2 %collective-permute-done.9.partner_ref = bf16[2,80,256]{2,1,0:T(8,128)(2,1)S(1)} collective-permute-done((bf16[2,80,256]{2,1,0:T(8,128)(2,1)S(1)}, bf16[2,80,256]{2,1,0:T(8,128)(2,1)S(1)}, u32[]{:S(2)}, u32[]{:S(2)}) %collective-permute-start.9) | collective-permute-done | bytes 81952 | tf_op jit(solution)/shard_map/ppermute | solution.py:362
  131.8 1.3 place.1
  133.1 18.6 %all_to_all.16 = bf16[4,2,16,512]{3,2,1,0:T(8,128)(2,1)S(1)} all-to-all(bf16[4,2,16,512]{3,2,1,0:T(8,128)(2,1)S(1)} %place.1), channel_id=1, replica_groups=mesh['y'=4,'xh'=2,'c'=2,'xl'=2,'zq'=4,'zr'=4] {'zq'}, dimensions={0} | all-to-all | bytes 262144 | tf_op jit(solution)/shard_map/all_to_all | solution.py:370
  151.8 0.0 copy-done.4
  151.8 0.6 multiply_subtract_fusion
  (7 shorter events, 0.1 us)
Async XLA Ops:
  0.0 1.0 copy-start
  0.0 81.9 %copy-start.2 = (bf16[512,512]{1,0:T(8,128)(2,1)S(1)}, bf16[512,512]{1,0:T(8,128)(2,1)}, u32[]{:S(2)}) copy-start(bf16[512,512]{1,0:T(8,128)(2,1)} %constant.47.clone.left_ref) | copy-start | bytes 1572868
  0.0 81.9 %copy-start.3 = (bf16[512,512]{1,0:T(8,128)(2,1)S(1)}, bf16[512,512]{1,0:T(8,128)(2,1)}, u32[]{:S(2)}) copy-start(bf16[512,512]{1,0:T(8,128)(2,1)} %constant.46.clone.right_ref) | copy-start | bytes 1572868
  2.6 29.4 %all-to-all-start = ((bf16[4,2,32,512]{3,2,1,0:T(8,128)(2,1)}), bf16[4,2,32,512]{3,2,1,0:T(8,128)(2,1)S(1)}, u32[]{:S(2)}, u32[]{:S(2)}) async-start(bf16[4,2,32,512]{3,2,1,0:T(8,128)(2,1)} %broadcast_in_dim.2), calls=%async_computation | async-start | bytes 524288 | tf_op jit(solution)/shard_map/all_to_all | solution.py:294
  19.0 6.2 %collective-permute-start = (s32[32]{0:T(128)S(1)}, s32[32]{0:T(128)S(1)}, u32[]{:S(2)}, u32[]{:S(2)}) collective-permute-start(s32[32]{0:T(128)S(1)} %pad_add_fusion.scan_ref), channel_id=1, source_target_pairs={{0,32},{32,64},{64,96},{96,128},{128,160},{160,192},{192,224},{224... | collective-permute-start | bytes 392 | tf_op jit(solution)/shard_map/ppermute | solution.py:286
  33.2 18.1 %collective-permute-start.1 = (bf16[4,2,16,512]{3,2,1,0:T(8,128)(2,1)S(1)}, bf16[4,2,16,512]{3,2,1,0:T(8,128)(2,1)S(1)}, u32[]{:S(2)}, u32[]{:S(2)}) collective-permute-start(bf16[4,2,16,512]{3,2,1,0:T(8,128)(2,1)S(1)} %get-tuple-element.25), channel_id=1, source_target_pairs={{0,16},{16,0},{1,17},{17,1},{2,18},{18,2},{3,19},{19,3},{4,20},{20... | collective-permute-start | bytes 393224 | tf_op jit(solution)/shard_map/ppermute | solution.py:302
  36.3 12.2 %collective-permute-start.2 = (bf16[2,64,256]{2,1,0:T(8,128)(2,1)S(1)}, bf16[2,64,256]{2,1,0:T(8,128)(2,1)S(1)}, u32[]{:S(2)}, u32[]{:S(2)}) collective-permute-start(bf16[2,64,256]{2,1,0:T(8,128)(2,1)S(1)} %get-tuple-element.22), channel_id=1, source_target_pairs={{0,16},{16,0},{1,17},{17,1},{2,18},{18,2},{3,19},{19,3},{4,20},{20... | collective-permute-start | bytes 196616 | tf_op jit(solution)/shard_map/ppermute | solution.py:303
  38.5 12.8 %collective-permute-start.3 = (bf16[2,64,256]{2,1,0:T(8,128)(2,1)S(1)}, bf16[2,64,256]{2,1,0:T(8,128)(2,1)S(1)}, u32[]{:S(2)}, u32[]{:S(2)}) collective-permute-start(bf16[2,64,256]{2,1,0:T(8,128)(2,1)S(1)} %get-tuple-element.23), channel_id=1, source_target_pairs={{32,0},{64,32},{96,64},{128,96},{160,128},{192,160},{224,192},{256... | collective-permute-start | bytes 196616 | tf_op jit(solution)/shard_map/ppermute | solution.py:304
  46.7 4.6 %collective-permute-start.4 = (bf16[2,64,256]{2,1,0:T(8,128)(2,1)S(1)}, bf16[2,64,256]{2,1,0:T(8,128)(2,1)S(1)}, u32[]{:S(2)}, u32[]{:S(2)}) collective-permute-start(bf16[2,64,256]{2,1,0:T(8,128)(2,1)S(1)} %get-tuple-element.24), channel_id=1, source_target_pairs={{32,16},{64,48},{96,80},{128,112},{160,144},{192,176},{224,208},{2... | collective-permute-start | bytes 196616 | tf_op jit(solution)/shard_map/ppermute | solution.py:305
  51.3 24.1 %collective-permute-start.7 = (bf16[8,2,16,512]{3,2,1,0:T(8,128)(2,1)S(1)}, bf16[8,2,16,512]{3,2,1,0:T(8,128)(2,1)S(1)}, u32[]{:S(2)}, u32[]{:S(2)}) collective-permute-start(bf16[8,2,16,512]{3,2,1,0:T(8,128)(2,1)S(1)} %constant_dynamic-update-slice_fusion), channel_id=1, source_target_pairs={{0,384},{128,0},{256,128},{384,256},{1,385},{129,1},{257,129},{385... | collective-permute-start | bytes 786440 | tf_op jit(solution)/shard_map/ppermute | solution.py:311
  56.0 19.4 %collective-permute-start.6 = (bf16[8,2,16,512]{3,2,1,0:T(8,128)(2,1)S(1)}, bf16[8,2,16,512]{3,2,1,0:T(8,128)(2,1)S(1)}, u32[]{:S(2)}, u32[]{:S(2)}) collective-permute-start(bf16[8,2,16,512]{3,2,1,0:T(8,128)(2,1)S(1)} %constant_dynamic-update-slice_fusion), channel_id=1, source_target_pairs={{0,256},{128,384},{256,0},{384,128},{1,257},{129,385},{257,1},{385... | collective-permute-start | bytes 786440 | tf_op jit(solution)/shard_map/ppermute | solution.py:311
  58.2 17.2 %collective-permute-start.5 = (bf16[8,2,16,512]{3,2,1,0:T(8,128)(2,1)S(1)}, bf16[8,2,16,512]{3,2,1,0:T(8,128)(2,1)S(1)}, u32[]{:S(2)}, u32[]{:S(2)}) collective-permute-start(bf16[8,2,16,512]{3,2,1,0:T(8,128)(2,1)S(1)} %constant_dynamic-update-slice_fusion), channel_id=1, source_target_pairs={{0,128},{128,256},{256,384},{384,0},{1,129},{129,257},{257,385},{3... | collective-permute-start | bytes 786440 | tf_op jit(solution)/shard_map/ppermute | solution.py:311
  75.5 25.4 %copy-start.1 = (f32[1,8,256,256]{3,2,1,0:T(8,128)S(1)}, f32[1,8,256,256]{3,2,1,0:T(8,128)}, u32[]{:S(2)}) copy-start(f32[1,8,256,256]{3,2,1,0:T(8,128)} %param.10) | copy-start | bytes 6291460
  75.5 6.3 %collective-permute-start.8 = (bf16[4,8,2,16,512]{4,3,2,1,0:T(8,128)(2,1)S(1)}, bf16[4,8,2,16,512]{4,3,2,1,0:T(8,128)(2,1)S(1)}, u32[]{:S(2)}, u32[]{:S(2)}) collective-permute-start(bf16[4,8,2,16,512]{4,3,2,1,0:T(8,128)(2,1)S(1)} %pad_maximum_fusion.here_ref), channel_id=1, source_target_pairs={{0,32},{32,0},{1,33},{33,1},{2,34},{34,2},{3,35},{35,3},{4,36},{36... | collective-permute-start | bytes 3145736 | tf_op jit(solution)/shard_map/ppermute | solution.py:321
  100.9 50.9 %copy-start.4 = (f32[2,16,512]{2,1,0:T(8,128)S(1)}, f32[2,16,512]{2,1,0:T(8,128)}, u32[]{:S(2)}) copy-start(f32[2,16,512]{2,1,0:T(8,128)} %param.8) | copy-start | bytes 196612
  117.2 11.4 %collective-permute-start.11 = (bf16[2,80,256]{2,1,0:T(8,128)(2,1)S(1)}, bf16[2,80,256]{2,1,0:T(8,128)(2,1)S(1)}, u32[]{:S(2)}, u32[]{:S(2)}) collective-permute-start(bf16[2,80,256]{2,1,0:T(8,128)(2,1)S(1)} %reduce_sum.21.own_ref), channel_id=1, source_target_pairs={{16,32},{48,64},{80,96},{112,128},{144,160},{176,192},{208,224},{2... | collective-permute-start | bytes 245768 | tf_op jit(solution)/shard_map/ppermute | solution.py:364
  118.5 10.1 %collective-permute-start.10 = (bf16[2,80,256]{2,1,0:T(8,128)(2,1)S(1)}, bf16[2,80,256]{2,1,0:T(8,128)(2,1)S(1)}, u32[]{:S(2)}, u32[]{:S(2)}) collective-permute-start(bf16[2,80,256]{2,1,0:T(8,128)(2,1)S(1)} %reduce_sum.21.own_ref), channel_id=1, source_target_pairs={{0,32},{32,64},{64,96},{96,128},{128,160},{160,192},{192,224},{224... | collective-permute-start | bytes 245768 | tf_op jit(solution)/shard_map/ppermute | solution.py:363
  126.6 5.2 %collective-permute-start.9 = (bf16[2,80,256]{2,1,0:T(8,128)(2,1)S(1)}, bf16[2,80,256]{2,1,0:T(8,128)(2,1)S(1)}, u32[]{:S(2)}, u32[]{:S(2)}) collective-permute-start(bf16[2,80,256]{2,1,0:T(8,128)(2,1)S(1)} %reduce_sum.21.own_ref), channel_id=1, source_target_pairs={{0,16},{16,0},{1,17},{17,1},{2,18},{18,2},{3,19},{19,3},{4,20},{20... | collective-permute-start | bytes 245768 | tf_op jit(solution)/shard_map/ppermute | solution.py:362

commit v4 on v3

--- a/solution.py
+++ b/solution.py
@@ -13,11 +13,11 @@
 bf16 = jnp.bfloat16
 TILE_AXES = ("y", "xh", "c")
 DEPTH_AXES = ("zq", "zr")
-STEPS = 2
 CHUNK = 16
+AT_ONCE = 2
 QUARTERS = 4
 RUN = 4
-VMEM_LIMIT = 48 * 1024 * 1024
+VMEM_LIMIT = 20 * 1024 * 1024
 
 
 def dft_blocks(length):
@@ -60,11 +60,12 @@
 def class_rows(touched, window, row_start, across):
     blocks = []
     for member in range(RUN):
-        shape = (window, touched) if across else (touched, window)
-        spot = lax.broadcasted_iota(jnp.int32, shape, 1 if across else 0)
-        row = lax.broadcasted_iota(jnp.int32, shape, 0 if across else 1)
-        chunk = (first_row(row_start, member) // CHUNK + spot // CHUNK) * RUN + member
-        blocks.append((chunk * CHUNK + spot % CHUNK == row + row_start).astype(f32).astype(bf16))
+        spots, rows = ((1, touched), (window, 1)) if across else ((touched, 1), (1, window))
+        spot = lax.broadcasted_iota(jnp.int32, spots, 1 if across else 0)
+        row = lax.broadcasted_iota(jnp.int32, rows, 0 if across else 1)
+        target = spot + spot // CHUNK * (CHUNK * (RUN - 1))
+        first = first_row(row_start, member) * RUN + member * CHUNK - row_start
+        blocks.append((target + first == row).astype(f32).astype(bf16))
     return jnp.concatenate(blocks, axis=1 if across else 0)
 
 
@@ -123,84 +124,79 @@
         pieces = []
         for row in range(count):
             place = lax.rem(up - row + count, count)
-            here = here_ref[place, mode, part].astype(f32)
-            there = there_ref[place, mode, part].astype(f32)
+            here, there = here_ref[place, mode, part], there_ref[place, mode, part]
             for piece in (jnp.where(core == 0, here, there), jnp.where(core == 0, there, here)):
                 pieces += [piece[:, :window], piece[:, window:]]
-        return jnp.concatenate(pieces, axis=0)
+        return jnp.concatenate(pieces, axis=0).astype(f32)
 
     return rows(0), rows(1)
 
 
 def forward_kernel(
-    meta_ref, scan_ref, touched_ref, here_ref, there_ref,
-    right_ref, left_ref, spec_ref, power_ref, patch, total,
-):
-    step = pl.program_id(0)
+    meta_ref, scan_ref, touched_ref, here_ref, there_ref, right_ref, left_ref,
+    spec_ref, power_ref,
+):
     lane, quarter = meta_ref[0], meta_ref[1]
     window = power_ref.shape[-1]
     row_start = scan_ref[lane * QUARTERS + quarter]
-
-    @pl.when(step == 0)
-    def _():
-        pick = class_rows(touched_ref.shape[2], window, row_start, True)
-        for part in range(2):
-            stack = jnp.concatenate([touched_ref[member, part] for member in range(RUN)], axis=0)
-            patch[part] = dot(pick, stack)
-        total[...] = jnp.zeros_like(total)
-
-    for mode in range(here_ref.shape[1]):
-        probe_real, probe_imag = full_probe(here_ref, there_ref, meta_ref, mode)
-        exit_real = (probe_real * patch[0] - probe_imag * patch[1]).astype(bf16)
-        exit_imag = (probe_real * patch[1] + probe_imag * patch[0]).astype(bf16)
-        half_spectrum = dot(jnp.concatenate([exit_real, exit_imag], axis=1), right_ref[...])
-        spectrum = dot(left_ref[...], on_top(half_spectrum.astype(bf16)))
-        spec_ref[0, mode] = spectrum
-        squares = spectrum * spectrum
-        total[...] = total[...] + (squares[:window] + squares[window:])
-
-    @pl.when(step == pl.num_programs(0) - 1)
-    def _():
-        power_ref[...] = total[...].astype(bf16)
+    pick = class_rows(touched_ref.shape[2], window, row_start, True)
+    patch = [
+        dot(pick, jnp.concatenate([touched_ref[member, part] for member in range(RUN)], axis=0))
+        for part in range(2)
+    ]
+    total = jnp.zeros((window, window), f32)
+    for start in range(0, spec_ref.shape[0], AT_ONCE):
+        exits = []
+        for mode in range(start, start + AT_ONCE):
+            probe_real, probe_imag = full_probe(here_ref, there_ref, meta_ref, mode)
+            exit_real = (probe_real * patch[0] - probe_imag * patch[1]).astype(bf16)
+            exit_imag = (probe_real * patch[1] + probe_imag * patch[0]).astype(bf16)
+            exits.append(jnp.concatenate([exit_real, exit_imag], axis=1))
+        half_spectrum = dot(jnp.concatenate(exits, axis=0), right_ref[...]).astype(bf16)
+        stacks = [on_top(half_spectrum[i * window : (i + 1) * window]) for i in range(AT_ONCE)]
+        spectra = dot(left_ref[...], jnp.concatenate(stacks, axis=1))
+        for i in range(AT_ONCE):
+            spectrum = spectra[:, i * window : (i + 1) * window]
+            spec_ref[start + i] = spectrum
+            squares = spectrum * spectrum
+            total = total + (squares[:window] + squares[window:])
+    power_ref[...] = total.astype(bf16)
 
 
 def backward_kernel(
     meta_ref, scan_ref, spec_ref, powers_ref, amplitude_ref, here_ref, there_ref, right_ref, left_ref,
-    pieces_ref, factor, sums,
-):
-    step = pl.program_id(0)
+    pieces_ref,
+):
     slot = meta_ref[0] * QUARTERS + meta_ref[1]
     alive = slot < scan_ref[4 * QUARTERS + meta_ref[3]]
     window = pieces_ref.shape[-1]
-
-    @pl.when(step == 0)
-    def _():
-        intensity = powers_ref[0].astype(f32)
-        for member in range(1, powers_ref.shape[0]):
-            intensity = intensity + powers_ref[member].astype(f32)
-        correction = 1.0 - amplitude_ref[0] / jnp.sqrt(intensity + 1.0)
-        factor[...] = jnp.where(alive, correction, 0.0)
-        sums[...] = jnp.zeros_like(sums)
-
-    for mode in range(here_ref.shape[1]):
-        wave_real = (spec_ref[0, mode, :window] * factor[...]).astype(bf16)
-        wave_imag = (spec_ref[0, mode, window:] * factor[...]).astype(bf16)
-        back_half = dot(jnp.concatenate([wave_real, wave_imag], axis=1), left_ref[...])
-        back_wave = dot(right_ref[...], on_top(back_half.astype(bf16)))
-        back_real, back_imag = back_wave[:window], back_wave[window:]
-        probe_real, probe_imag = full_probe(here_ref, there_ref, meta_ref, mode)
-        sums[0] = sums[0] + (probe_real * back_real + probe_imag * back_imag)
-        sums[1] = sums[1] + (probe_real * back_imag - probe_imag * back_real)
-
-    @pl.when(step == pl.num_programs(0) - 1)
-    def _():
-        row_start = scan_ref[slot]
-        touched = pieces_ref.shape[2]
-        deal = class_rows(touched, window, row_start, False)
-        for part in range(2):
-            dealt = dot(deal, sums[part].astype(bf16)).astype(bf16)
-            for member in range(RUN):
-                pieces_ref[member, part] = dealt[member * touched : (member + 1) * touched]
+    intensity = powers_ref[0].astype(f32)
+    for member in range(1, powers_ref.shape[0]):
+        intensity = intensity + powers_ref[member].astype(f32)
+    correction = 1.0 - amplitude_ref[0, slot] / jnp.sqrt(intensity + 1.0)
+    factor = jnp.where(alive, correction, 0.0)
+    sums = [jnp.zeros((window, window), f32)] * 2
+    for start in range(0, spec_ref.shape[0], AT_ONCE):
+        waves = []
+        for mode in range(start, start + AT_ONCE):
+            wave_real = (spec_ref[mode, :window] * factor).astype(bf16)
+            wave_imag = (spec_ref[mode, window:] * factor).astype(bf16)
+            waves.append(jnp.concatenate([wave_real, wave_imag], axis=1))
+        back_half = dot(jnp.concatenate(waves, axis=0), left_ref[...]).astype(bf16)
+        stacks = [on_top(back_half[i * window : (i + 1) * window]) for i in range(AT_ONCE)]
+        back_waves = dot(right_ref[...], jnp.concatenate(stacks, axis=1))
+        for i in range(AT_ONCE):
+            back_wave = back_waves[:, i * window : (i + 1) * window]
+            back_real, back_imag = back_wave[:window], back_wave[window:]
+            probe_real, probe_imag = full_probe(here_ref, there_ref, meta_ref, start + i)
+            sums[0] = sums[0] + (probe_real * back_real + probe_imag * back_imag)
+            sums[1] = sums[1] + (probe_real * back_imag - probe_imag * back_real)
+    touched = pieces_ref.shape[2]
+    deal = class_rows(touched, window, scan_ref[slot], False)
+    for part in range(2):
+        dealt = dot(deal, sums[part].astype(bf16)).astype(bf16)
+        for member in range(RUN):
+            pieces_ref[member, part] = dealt[member * touched : (member + 1) * touched]
 
 
 def place_kernel(
@@ -233,21 +229,17 @@
             half_ref[chunk, part] = placed[chunk * chunk_rows : (chunk + 1) * chunk_rows]
 
 
-def whole(shape):
-    return pl.BlockSpec(shape, lambda step, *_: (0,) * len(shape))
-
-
-def per_step(shape):
-    return pl.BlockSpec((1,) + shape, lambda step, *_: (step,) + (0,) * len(shape))
-
-
-def call(kernel, name, scalars, operands, in_specs, results, out_specs, steps=1, scratch=(), flops=0):
+def call(kernel, name, scalars, operands, results, away=(), away_results=(), scratch=(), flops=0):
+    held, far = pl.BlockSpec(memory_space=pltpu.VMEM), pl.BlockSpec(memory_space=pltpu.HBM)
+    out_specs = held
+    if isinstance(results, list):
+        out_specs = [far if i in away_results else held for i in range(len(results))]
     return pl.pallas_call(
         kernel,
         grid_spec=pltpu.PrefetchScalarGridSpec(
             num_scalar_prefetch=len(scalars),
-            grid=(steps,),
-            in_specs=in_specs,
+            grid=(1,),
+            in_specs=[far if i in away else held for i in range(len(operands))],
             out_specs=out_specs,
             scratch_shapes=scratch,
         ),
@@ -295,9 +287,8 @@
     cut_shape = (2, quarters * chunk_rows, window)
     lane_shape = (quarters, 2, chunk_rows, width)
     own, partner, upper, lower, lane_modes = call(
-        cut_kernel, "cut", (meta, scan, above), (packed,), [whole(packed.shape)],
+        cut_kernel, "cut", (meta, scan, above), (packed,),
         [jax.ShapeDtypeStruct(cut_shape, bf16)] * 4 + [jax.ShapeDtypeStruct(lane_shape, bf16)],
-        [whole(cut_shape)] * 4 + [whole(lane_shape)],
     )
     other_modes = lax.ppermute(lane_modes, "xl", swap)
     other = lax.ppermute(partner, "xl", swap)
@@ -312,60 +303,39 @@
     ]
     touched_shape = (2, window // RUN + CHUNK, window)
     touched = call(
-        touch_kernel, "touch", (meta, scan), (own, other, below0, below1), [whole(cut_shape)] * 4,
-        jax.ShapeDtypeStruct(touched_shape, bf16), whole(touched_shape),
+        touch_kernel, "touch", (meta, scan), (own, other, below0, below1),
+        jax.ShapeDtypeStruct(touched_shape, bf16),
     )
     touched = lax.all_gather(touched, "zr", axis=0)
     *shared, touched = lax.optimization_barrier((*shared, touched))
     here = jnp.stack([part_modes, *shared])
     there = lax.ppermute(here, "c", swap)
-    window_shape = (2, window, window)
-
     modes = here.shape[1]
-    at_once = modes // STEPS
     product_flops = modes * 2 * 2 * (2 * window) ** 2 * window
-    probe_block = pl.BlockSpec(
-        here.shape[:1] + (at_once,) + here.shape[2:], lambda step, *_: (0, step, 0, 0, 0)
-    )
-    spec_shape = (at_once, 2 * window, window)
     spectrum, power = call(
-        forward_kernel, "forward", (meta, scan),
-        (touched, here, there, right, left),
-        [whole(touched.shape)] + [probe_block] * 2 + [whole(right.shape), whole(left.shape)],
+        forward_kernel, "forward", (meta, scan), (touched, here, there, right, left),
         [
-            jax.ShapeDtypeStruct((STEPS,) + spec_shape, f32),
+            jax.ShapeDtypeStruct((modes, 2 * window, window), f32),
             jax.ShapeDtypeStruct((window, window), bf16),
         ],
-        [per_step(spec_shape), whole((window, window))],
-        steps=STEPS,
-        scratch=[pltpu.VMEM(window_shape, f32), pltpu.VMEM((window, window), f32)],
         flops=product_flops,
     )
     powers = lax.all_gather(power, "zr", axis=0)
-
-    slot_block = pl.BlockSpec(
-        (1, window, window), lambda step, meta_ref, *_: (meta_ref[0] * quarters + meta_ref[1], 0, 0)
-    )
     pieces = call(
         backward_kernel, "backward", (meta, scan),
-        (spectrum, powers, measured_amplitude[0], here, there, right, left),
-        [per_step(spec_shape), whole(powers.shape), slot_block]
-        + [probe_block] * 2 + [whole(right.shape), whole(left.shape)],
+        (spectrum, powers, measured_amplitude, here, there, right, left),
         jax.ShapeDtypeStruct(touched.shape, bf16),
-        whole(touched.shape),
-        steps=STEPS,
-        scratch=[pltpu.VMEM((window, window), f32), pltpu.VMEM(window_shape, f32)],
         flops=product_flops,
     )
     pieces = lax.all_to_all(pieces, "zr", 0, 0, tiled=True)
-    term = jnp.sum(pieces.astype(f32), axis=0).astype(bf16)
+    first, second, third, fourth = (pieces[sender].astype(f32) for sender in range(RUN))
+    term = ((first + second) + (third + fourth)).astype(bf16)
     partners = lax.ppermute(term, "xl", swap)
     above0 = lax.ppermute(term, axes, down_first)
     above1 = lax.ppermute(term, axes, down_second)
     half_sum = call(
         place_kernel, "place", (meta, scan, above), (term, partners, above0, above1),
-        [whole(touched_shape)] * 4,
-        jax.ShapeDtypeStruct(lane_shape, bf16), whole(lane_shape),
+        jax.ShapeDtypeStruct(lane_shape, bf16),
     )
     terms = lax.all_to_all(half_sum, "zq", 0, 0, tiled=True)
     return object_field - step_size * jnp.sum(terms.astype(f32), axis=0)

time: 153 us -> 149 us (0.974)
  Pallas kernels: 15.4 us -> 11 us
    pallas_call x5, Pallas kernels: 15.4 us -> 11 us  [call(): pl.pallas_call(kernel, grid_spec=pltpu.PrefetchScalarGridSpec(num_scalar_...]
where the time goes in v4:
time: 149 us; the launch traced here: 148 us
  starting transfers between devices  61.3 us (41%)
  blocking collectives  55.5 us (37%)
  waiting for transfers between devices  15.7 us (11%)
  Pallas kernels  11 us (7%)
  other arithmetic  2.45 us (2%)
  local copies, waits for them, and re-layouts  1.87 us (1%)
    all_to_all x1, blocking collectives, on_device(): terms = lax.all_to_all(half_sum, 'zq', 0, 0, tiled=True)  18.7 us
    all_to_all x1, starting transfers between devices, on_device(): packed = lax.all_to_all(packed, 'zq', 0, 0, tiled=True)  15.6 us
    all_gather x1, blocking collectives, on_device(): touched = lax.all_gather(touched, 'zr', axis=0)  13.8 us
    all_gather x1, blocking collectives, on_device(): powers = lax.all_gather(power, 'zr', axis=0)  13.1 us
    pallas_call x5, Pallas kernels, call(): pl.pallas_call(kernel, grid_spec=pltpu.PrefetchScalarGridSpec(num_scalar_...  11 us
    all_to_all x1, blocking collectives, on_device(): pieces = lax.all_to_all(pieces, 'zr', 0, 0, tiled=True)  9.95 us
    ppermute x3, starting transfers between devices, on_device(): lax.ppermute(part_modes, 'y', [(i, (i + d) % ups) for i in range(ups)])  9.5 us
    ppermute x1, starting transfers between devices, on_device(): below0 = lax.ppermute(upper, axes, up_first)  8.21 us
  transfers between devices with their start and end apart: 13, of which 5 were waited for; matrix products, arithmetic and copies ran while one was open for 1% of the time, Pallas kernels for 1%

profile of v4, /device:TPU:1, one launch (start us, length us, event | category | flops | bytes accessed | tf_op | source)
XLA Modules:
  0.0 148.1 jit_solution(16611550083957506093)
XLA Ops:
  0.0 0.0 copy-start
  0.0 0.0 copy-start.2
  0.0 0.0 copy-start.3
  0.0 1.0 copy-done
  1.1 0.8 convert.10
  1.9 0.7 broadcast_in_dim.2
  2.6 15.6 %all-to-all-start = ((bf16[4,2,32,512]{3,2,1,0:T(8,128)(2,1)}), bf16[4,2,32,512]{3,2,1,0:T(8,128)(2,1)S(1)}, u32[]{:S(2)}, u32[]{:S(2)}) async-start(bf16[4,2,32,512]{3,2,1,0:T(8,128)(2,1)} %broadcast_in_dim.2), calls=%async_computation | async-start | bytes 524288 | tf_op jit(solution)/shard_map/all_to_all | solution.py:286
  18.3 0.8 pad_add_fusion.scan_ref
  19.0 5.5 %collective-permute-start = (s32[32]{0:T(128)S(1)}, s32[32]{0:T(128)S(1)}, u32[]{:S(2)}, u32[]{:S(2)}) collective-permute-start(s32[32]{0:T(128)S(1)} %pad_add_fusion.scan_ref), channel_id=1, source_target_pairs={{0,32},{32,64},{64,96},{96,128},{128,160},{160,192},{192,224},{224... | collective-permute-start | bytes 392 | tf_op jit(solution)/shard_map/ppermute | solution.py:278
  24.5 0.1 stack.46.meta_ref
  24.6 0.6 collective-permute-done.above_ref
  25.2 6.8 %all-to-all-done.packed_ref = bf16[4,2,32,512]{3,2,1,0:T(8,128)(2,1)S(1)} async-done(((bf16[4,2,32,512]{3,2,1,0:T(8,128)(2,1)}), bf16[4,2,32,512]{3,2,1,0:T(8,128)(2,1)S(1)}, u32[]{:S(2)}, u32[]{:S(2)}) %all-to-all-start) | async-done | bytes 262176 | tf_op jit(solution)/shard_map/all_to_all | solution.py:286
  32.0 1.1 cut.1
  33.2 3.1 %collective-permute-start.1 = (bf16[4,2,16,512]{3,2,1,0:T(8,128)(2,1)S(1)}, bf16[4,2,16,512]{3,2,1,0:T(8,128)(2,1)S(1)}, u32[]{:S(2)}, u32[]{:S(2)}) collective-permute-start(bf16[4,2,16,512]{3,2,1,0:T(8,128)(2,1)S(1)} %get-tuple-element.25), channel_id=1, source_target_pairs={{0,16},{16,0},{1,17},{17,1},{2,18},{18,2},{3,19},{19,3},{4,20},{20... | collective-permute-start | bytes 393224 | tf_op jit(solution)/shard_map/ppermute | solution.py:293
  36.3 2.2 %collective-permute-start.2 = (bf16[2,64,256]{2,1,0:T(8,128)(2,1)S(1)}, bf16[2,64,256]{2,1,0:T(8,128)(2,1)S(1)}, u32[]{:S(2)}, u32[]{:S(2)}) collective-permute-start(bf16[2,64,256]{2,1,0:T(8,128)(2,1)S(1)} %get-tuple-element.22), channel_id=1, source_target_pairs={{0,16},{16,0},{1,17},{17,1},{2,18},{18,2},{3,19},{19,3},{4,20},{20... | collective-permute-start | bytes 196616 | tf_op jit(solution)/shard_map/ppermute | solution.py:294
  38.5 8.2 %collective-permute-start.3 = (bf16[2,64,256]{2,1,0:T(8,128)(2,1)S(1)}, bf16[2,64,256]{2,1,0:T(8,128)(2,1)S(1)}, u32[]{:S(2)}, u32[]{:S(2)}) collective-permute-start(bf16[2,64,256]{2,1,0:T(8,128)(2,1)S(1)} %get-tuple-element.23), channel_id=1, source_target_pairs={{32,0},{64,32},{96,64},{128,96},{160,128},{192,160},{224,192},{256... | collective-permute-start | bytes 196616 | tf_op jit(solution)/shard_map/ppermute | solution.py:295
  46.7 1.8 %collective-permute-start.4 = (bf16[2,64,256]{2,1,0:T(8,128)(2,1)S(1)}, bf16[2,64,256]{2,1,0:T(8,128)(2,1)S(1)}, u32[]{:S(2)}, u32[]{:S(2)}) collective-permute-start(bf16[2,64,256]{2,1,0:T(8,128)(2,1)S(1)} %get-tuple-element.24), channel_id=1, source_target_pairs={{32,16},{64,48},{96,80},{128,112},{160,144},{192,176},{224,208},{2... | collective-permute-start | bytes 196616 | tf_op jit(solution)/shard_map/ppermute | solution.py:296
  48.5 0.0 collective-permute-done.2.other_ref
  48.5 2.8 %collective-permute-done.3.below0_ref = bf16[2,64,256]{2,1,0:T(8,128)(2,1)S(1)} collective-permute-done((bf16[2,64,256]{2,1,0:T(8,128)(2,1)S(1)}, bf16[2,64,256]{2,1,0:T(8,128)(2,1)S(1)}, u32[]{:S(2)}, u32[]{:S(2)}) %collective-permute-start.3) | collective-permute-done | bytes 65568 | tf_op jit(solution)/shard_map/ppermute | solution.py:295
  51.3 0.0 collective-permute-done.4.below1_ref
  51.3 0.0 collective-permute-done.1
  51.3 4.6 %collective-permute-start.7 = (bf16[8,2,16,512]{3,2,1,0:T(8,128)(2,1)S(1)}, bf16[8,2,16,512]{3,2,1,0:T(8,128)(2,1)S(1)}, u32[]{:S(2)}, u32[]{:S(2)}) collective-permute-start(bf16[8,2,16,512]{3,2,1,0:T(8,128)(2,1)S(1)} %constant_dynamic-update-slice_fusion), channel_id=1, source_target_pairs={{0,384},{128,0},{256,128},{384,256},{1,385},{129,1},{257,129},{385... | collective-permute-start | bytes 786440 | tf_op jit(solution)/shard_map/ppermute | solution.py:302
  56.0 2.3 %collective-permute-start.6 = (bf16[8,2,16,512]{3,2,1,0:T(8,128)(2,1)S(1)}, bf16[8,2,16,512]{3,2,1,0:T(8,128)(2,1)S(1)}, u32[]{:S(2)}, u32[]{:S(2)}) collective-permute-start(bf16[8,2,16,512]{3,2,1,0:T(8,128)(2,1)S(1)} %constant_dynamic-update-slice_fusion), channel_id=1, source_target_pairs={{0,256},{128,384},{256,0},{384,128},{1,257},{129,385},{257,1},{385... | collective-permute-start | bytes 786440 | tf_op jit(solution)/shard_map/ppermute | solution.py:302
  58.2 2.6 %collective-permute-start.5 = (bf16[8,2,16,512]{3,2,1,0:T(8,128)(2,1)S(1)}, bf16[8,2,16,512]{3,2,1,0:T(8,128)(2,1)S(1)}, u32[]{:S(2)}, u32[]{:S(2)}) collective-permute-start(bf16[8,2,16,512]{3,2,1,0:T(8,128)(2,1)S(1)} %constant_dynamic-update-slice_fusion), channel_id=1, source_target_pairs={{0,128},{128,256},{256,384},{384,0},{1,129},{129,257},{257,385},{3... | collective-permute-start | bytes 786440 | tf_op jit(solution)/shard_map/ppermute | solution.py:302
  60.8 0.8 touch.1
  61.6 13.8 %all-gather = bf16[8,80,256]{2,1,0:T(8,128)(2,1)S(1)} all-gather(bf16[2,80,256]{2,1,0:T(8,128)(2,1)S(1)} %touch.1), channel_id=2, replica_groups=mesh['y'=4,'xh'=2,'c'=2,'xl'=2,'zq'=4,'zr'=4] {'zr'}, dimensions={0}, use_global_device_ids=true | all-gather | bytes 409600 | tf_op jit(solution)/shard_map/all_gather | solution.py:309
  75.4 0.0 collective-permute-done.7
  75.4 0.0 collective-permute-done.6
  75.4 0.0 collective-permute-done.5
  75.4 0.1 pad_maximum_fusion.here_ref
  75.5 0.0 copy-start.1
  75.6 4.1 %collective-permute-start.8 = (bf16[4,8,2,16,512]{4,3,2,1,0:T(8,128)(2,1)S(1)}, bf16[4,8,2,16,512]{4,3,2,1,0:T(8,128)(2,1)S(1)}, u32[]{:S(2)}, u32[]{:S(2)}) collective-permute-start(bf16[4,8,2,16,512]{4,3,2,1,0:T(8,128)(2,1)S(1)} %pad_maximum_fusion.here_ref), channel_id=1, source_target_pairs={{0,32},{32,0},{1,33},{33,1},{2,34},{34,2},{3,35},{35,3},{4,36},{36... | collective-permute-start | bytes 3145736 | tf_op jit(solution)/shard_map/ppermute | solution.py:312
  79.6 2.3 %collective-permute-done.8.there_ref = bf16[4,8,2,16,512]{4,3,2,1,0:T(8,128)(2,1)S(1)} collective-permute-done((bf16[4,8,2,16,512]{4,3,2,1,0:T(8,128)(2,1)S(1)}, bf16[4,8,2,16,512]{4,3,2,1,0:T(8,128)(2,1)S(1)}, u32[]{:S(2)}, u32[]{:S(2)}) %collective-permute-start.8) | collective-permute-done | bytes 1048608 | tf_op jit(solution)/shard_map/ppermute | solution.py:312
  81.9 0.0 copy-done.2
  81.9 0.0 copy-done.3
  81.9 3.6 %forward.1 = (f32[8,512,256]{2,1,0:T(8,128)S(1)}, bf16[256,256]{1,0:T(8,128)(2,1)S(1)}) custom-call(s32[7]{0:T(128)S(1)} %stack.46.meta_ref, s32[32]{0:T(128)S(1)} %pad_add_fusion.scan_ref, bf16[4,2,80,256]{3,2,1,0:T(8,128)(2,1)S(1)} %bitcast.20, bf16[4,8,2,16,512]{4,3,2,1,0:T(8,128)(2,1)S(1)} %pad_maximum_fusion.here_ref, ...), custom_call_target="tpu_custom_call" | custom-call | flops 2147483648 | bytes 4194304 | tf_op jit(solution)/shard_map/forward/pallas_call | solution.py:237
  85.5 13.1 %all-gather.1 = bf16[1024,256]{1,0:T(8,128)(2,1)S(1)} all-gather(bf16[256,256]{1,0:T(8,128)(2,1)S(1)} %get-tuple-element.36), channel_id=3, replica_groups=mesh['y'=4,'xh'=2,'c'=2,'xl'=2,'zq'=4,'zr'=4] {'zr'}, dimensions={0}, use_global_device_ids=true | all-gather | bytes 655360 | tf_op jit(solution)/shard_map/all_gather | solution.py:323
  98.6 0.0 copy-done.1
  98.6 0.0 copy-start.4
  98.6 4.1 %backward.1 = bf16[4,2,80,256]{3,2,1,0:T(8,128)(2,1)S(1)} custom-call(s32[7]{0:T(128)S(1)} %stack.46.meta_ref, s32[32]{0:T(128)S(1)} %pad_add_fusion.scan_ref, f32[8,512,256]{2,1,0:T(8,128)S(1)} %get-tuple-element.35.spec_ref, bf16[4,256,256]{2,1,0:T(8,128)(2,1)S(1)} %bitcast.19, f32[1,8,256,256]{3,2,1,0:T(8,128)S(1)} %copy-done.1, ...), custom_call_target="tpu_custom_call" | custom-call | flops 2147483648 | bytes 4194304 | tf_op jit(solution)/shard_map/backward/pallas_call | solution.py:237
  102.7 9.9 %all_to_all.15 = bf16[4,2,80,256]{3,2,1,0:T(8,128)(2,1)S(1)} all-to-all(bf16[4,2,80,256]{3,2,1,0:T(8,128)(2,1)S(1)} %backward.1), channel_id=1, replica_groups=mesh['y'=4,'xh'=2,'c'=2,'xl'=2,'zq'=4,'zr'=4] {'zr'}, dimensions={0} | all-to-all | bytes 655360 | tf_op jit(solution)/shard_map/all_to_all | solution.py:330
  112.7 1.3 collective-permute-start.11
  114.0 8.2 %collective-permute-start.10 = (bf16[2,80,256]{2,1,0:T(8,128)(2,1)S(1)}, bf16[2,80,256]{2,1,0:T(8,128)(2,1)S(1)}, u32[]{:S(2)}, u32[]{:S(2)}) collective-permute-start(bf16[2,80,256]{2,1,0:T(8,128)(2,1)S(1)} %fusion.own_ref), channel_id=1, source_target_pairs={{0,32},{32,64},{64,96},{96,128},{128,160},{160,192},{192,224},{224... | collective-permute-start | bytes 245768 | tf_op jit(solution)/shard_map/ppermute | solution.py:334
  122.2 1.9 %collective-permute-start.9 = (bf16[2,80,256]{2,1,0:T(8,128)(2,1)S(1)}, bf16[2,80,256]{2,1,0:T(8,128)(2,1)S(1)}, u32[]{:S(2)}, u32[]{:S(2)}) collective-permute-start(bf16[2,80,256]{2,1,0:T(8,128)(2,1)S(1)} %fusion.own_ref), channel_id=1, source_target_pairs={{0,16},{16,0},{1,17},{17,1},{2,18},{18,2},{3,19},{19,3},{4,20},{20... | collective-permute-start | bytes 245768 | tf_op jit(solution)/shard_map/ppermute | solution.py:333
  124.1 0.0 collective-permute-done.11.lower_ref
  124.1 0.0 collective-permute-done.10.upper_ref
  124.1 3.2 %collective-permute-done.9.partner_ref = bf16[2,80,256]{2,1,0:T(8,128)(2,1)S(1)} collective-permute-done((bf16[2,80,256]{2,1,0:T(8,128)(2,1)S(1)}, bf16[2,80,256]{2,1,0:T(8,128)(2,1)S(1)}, u32[]{:S(2)}, u32[]{:S(2)}) %collective-permute-start.9) | collective-permute-done | bytes 81952 | tf_op jit(solution)/shard_map/ppermute | solution.py:333
  127.4 1.3 place.1
  128.7 18.7 %all_to_all.16 = bf16[4,2,16,512]{3,2,1,0:T(8,128)(2,1)S(1)} all-to-all(bf16[4,2,16,512]{3,2,1,0:T(8,128)(2,1)S(1)} %place.1), channel_id=1, replica_groups=mesh['y'=4,'xh'=2,'c'=2,'xl'=2,'zq'=4,'zr'=4] {'zq'}, dimensions={0} | all-to-all | bytes 262144 | tf_op jit(solution)/shard_map/all_to_all | solution.py:340
  147.5 0.0 copy-done.4
  147.5 0.6 multiply_subtract_fusion
  (7 shorter events, 0.1 us)
Async XLA Ops:
  0.0 1.0 copy-start
  0.0 81.9 %copy-start.2 = (bf16[512,512]{1,0:T(8,128)(2,1)S(1)}, bf16[512,512]{1,0:T(8,128)(2,1)}, u32[]{:S(2)}) copy-start(bf16[512,512]{1,0:T(8,128)(2,1)} %constant.45.clone.left_ref) | copy-start | bytes 1572868
  0.0 81.9 %copy-start.3 = (bf16[512,512]{1,0:T(8,128)(2,1)S(1)}, bf16[512,512]{1,0:T(8,128)(2,1)}, u32[]{:S(2)}) copy-start(bf16[512,512]{1,0:T(8,128)(2,1)} %constant.44.clone.right_ref) | copy-start | bytes 1572868
  2.6 29.4 %all-to-all-start = ((bf16[4,2,32,512]{3,2,1,0:T(8,128)(2,1)}), bf16[4,2,32,512]{3,2,1,0:T(8,128)(2,1)S(1)}, u32[]{:S(2)}, u32[]{:S(2)}) async-start(bf16[4,2,32,512]{3,2,1,0:T(8,128)(2,1)} %broadcast_in_dim.2), calls=%async_computation | async-start | bytes 524288 | tf_op jit(solution)/shard_map/all_to_all | solution.py:286
  19.0 6.2 %collective-permute-start = (s32[32]{0:T(128)S(1)}, s32[32]{0:T(128)S(1)}, u32[]{:S(2)}, u32[]{:S(2)}) collective-permute-start(s32[32]{0:T(128)S(1)} %pad_add_fusion.scan_ref), channel_id=1, source_target_pairs={{0,32},{32,64},{64,96},{96,128},{128,160},{160,192},{192,224},{224... | collective-permute-start | bytes 392 | tf_op jit(solution)/shard_map/ppermute | solution.py:278
  33.2 18.1 %collective-permute-start.1 = (bf16[4,2,16,512]{3,2,1,0:T(8,128)(2,1)S(1)}, bf16[4,2,16,512]{3,2,1,0:T(8,128)(2,1)S(1)}, u32[]{:S(2)}, u32[]{:S(2)}) collective-permute-start(bf16[4,2,16,512]{3,2,1,0:T(8,128)(2,1)S(1)} %get-tuple-element.25), channel_id=1, source_target_pairs={{0,16},{16,0},{1,17},{17,1},{2,18},{18,2},{3,19},{19,3},{4,20},{20... | collective-permute-start | bytes 393224 | tf_op jit(solution)/shard_map/ppermute | solution.py:293
  36.3 12.2 %collective-permute-start.2 = (bf16[2,64,256]{2,1,0:T(8,128)(2,1)S(1)}, bf16[2,64,256]{2,1,0:T(8,128)(2,1)S(1)}, u32[]{:S(2)}, u32[]{:S(2)}) collective-permute-start(bf16[2,64,256]{2,1,0:T(8,128)(2,1)S(1)} %get-tuple-element.22), channel_id=1, source_target_pairs={{0,16},{16,0},{1,17},{17,1},{2,18},{18,2},{3,19},{19,3},{4,20},{20... | collective-permute-start | bytes 196616 | tf_op jit(solution)/shard_map/ppermute | solution.py:294
  38.5 12.8 %collective-permute-start.3 = (bf16[2,64,256]{2,1,0:T(8,128)(2,1)S(1)}, bf16[2,64,256]{2,1,0:T(8,128)(2,1)S(1)}, u32[]{:S(2)}, u32[]{:S(2)}) collective-permute-start(bf16[2,64,256]{2,1,0:T(8,128)(2,1)S(1)} %get-tuple-element.23), channel_id=1, source_target_pairs={{32,0},{64,32},{96,64},{128,96},{160,128},{192,160},{224,192},{256... | collective-permute-start | bytes 196616 | tf_op jit(solution)/shard_map/ppermute | solution.py:295
  46.7 4.6 %collective-permute-start.4 = (bf16[2,64,256]{2,1,0:T(8,128)(2,1)S(1)}, bf16[2,64,256]{2,1,0:T(8,128)(2,1)S(1)}, u32[]{:S(2)}, u32[]{:S(2)}) collective-permute-start(bf16[2,64,256]{2,1,0:T(8,128)(2,1)S(1)} %get-tuple-element.24), channel_id=1, source_target_pairs={{32,16},{64,48},{96,80},{128,112},{160,144},{192,176},{224,208},{2... | collective-permute-start | bytes 196616 | tf_op jit(solution)/shard_map/ppermute | solution.py:296
  51.3 24.1 %collective-permute-start.7 = (bf16[8,2,16,512]{3,2,1,0:T(8,128)(2,1)S(1)}, bf16[8,2,16,512]{3,2,1,0:T(8,128)(2,1)S(1)}, u32[]{:S(2)}, u32[]{:S(2)}) collective-permute-start(bf16[8,2,16,512]{3,2,1,0:T(8,128)(2,1)S(1)} %constant_dynamic-update-slice_fusion), channel_id=1, source_target_pairs={{0,384},{128,0},{256,128},{384,256},{1,385},{129,1},{257,129},{385... | collective-permute-start | bytes 786440 | tf_op jit(solution)/shard_map/ppermute | solution.py:302
  56.0 19.4 %collective-permute-start.6 = (bf16[8,2,16,512]{3,2,1,0:T(8,128)(2,1)S(1)}, bf16[8,2,16,512]{3,2,1,0:T(8,128)(2,1)S(1)}, u32[]{:S(2)}, u32[]{:S(2)}) collective-permute-start(bf16[8,2,16,512]{3,2,1,0:T(8,128)(2,1)S(1)} %constant_dynamic-update-slice_fusion), channel_id=1, source_target_pairs={{0,256},{128,384},{256,0},{384,128},{1,257},{129,385},{257,1},{385... | collective-permute-start | bytes 786440 | tf_op jit(solution)/shard_map/ppermute | solution.py:302
  58.2 17.2 %collective-permute-start.5 = (bf16[8,2,16,512]{3,2,1,0:T(8,128)(2,1)S(1)}, bf16[8,2,16,512]{3,2,1,0:T(8,128)(2,1)S(1)}, u32[]{:S(2)}, u32[]{:S(2)}) collective-permute-start(bf16[8,2,16,512]{3,2,1,0:T(8,128)(2,1)S(1)} %constant_dynamic-update-slice_fusion), channel_id=1, source_target_pairs={{0,128},{128,256},{256,384},{384,0},{1,129},{129,257},{257,385},{3... | collective-permute-start | bytes 786440 | tf_op jit(solution)/shard_map/ppermute | solution.py:302
  75.5 23.1 %copy-start.1 = (f32[1,8,256,256]{3,2,1,0:T(8,128)S(1)}, f32[1,8,256,256]{3,2,1,0:T(8,128)}, u32[]{:S(2)}) copy-start(f32[1,8,256,256]{3,2,1,0:T(8,128)} %amplitude_ref.1) | copy-start | bytes 6291460
  75.6 6.3 %collective-permute-start.8 = (bf16[4,8,2,16,512]{4,3,2,1,0:T(8,128)(2,1)S(1)}, bf16[4,8,2,16,512]{4,3,2,1,0:T(8,128)(2,1)S(1)}, u32[]{:S(2)}, u32[]{:S(2)}) collective-permute-start(bf16[4,8,2,16,512]{4,3,2,1,0:T(8,128)(2,1)S(1)} %pad_maximum_fusion.here_ref), channel_id=1, source_target_pairs={{0,32},{32,0},{1,33},{33,1},{2,34},{34,2},{3,35},{35,3},{4,36},{36... | collective-permute-start | bytes 3145736 | tf_op jit(solution)/shard_map/ppermute | solution.py:312
  98.6 48.8 %copy-start.4 = (f32[2,16,512]{2,1,0:T(8,128)S(1)}, f32[2,16,512]{2,1,0:T(8,128)}, u32[]{:S(2)}) copy-start(f32[2,16,512]{2,1,0:T(8,128)} %param.8) | copy-start | bytes 196612
  112.7 11.4 %collective-permute-start.11 = (bf16[2,80,256]{2,1,0:T(8,128)(2,1)S(1)}, bf16[2,80,256]{2,1,0:T(8,128)(2,1)S(1)}, u32[]{:S(2)}, u32[]{:S(2)}) collective-permute-start(bf16[2,80,256]{2,1,0:T(8,128)(2,1)S(1)} %fusion.own_ref), channel_id=1, source_target_pairs={{16,32},{48,64},{80,96},{112,128},{144,160},{176,192},{208,224},{2... | collective-permute-start | bytes 245768 | tf_op jit(solution)/shard_map/ppermute | solution.py:335
  114.0 10.1 %collective-permute-start.10 = (bf16[2,80,256]{2,1,0:T(8,128)(2,1)S(1)}, bf16[2,80,256]{2,1,0:T(8,128)(2,1)S(1)}, u32[]{:S(2)}, u32[]{:S(2)}) collective-permute-start(bf16[2,80,256]{2,1,0:T(8,128)(2,1)S(1)} %fusion.own_ref), channel_id=1, source_target_pairs={{0,32},{32,64},{64,96},{96,128},{128,160},{160,192},{192,224},{224... | collective-permute-start | bytes 245768 | tf_op jit(solution)/shard_map/ppermute | solution.py:334
  122.2 5.2 %collective-permute-start.9 = (bf16[2,80,256]{2,1,0:T(8,128)(2,1)S(1)}, bf16[2,80,256]{2,1,0:T(8,128)(2,1)S(1)}, u32[]{:S(2)}, u32[]{:S(2)}) collective-permute-start(bf16[2,80,256]{2,1,0:T(8,128)(2,1)S(1)} %fusion.own_ref), channel_id=1, source_target_pairs={{0,16},{16,0},{1,17},{17,1},{2,18},{18,2},{3,19},{19,3},{4,20},{20... | collective-permute-start | bytes 245768 | tf_op jit(solution)/shard_map/ppermute | solution.py:333

commit v5 on v4

--- a/solution.py
+++ b/solution.py
@@ -70,7 +70,7 @@
 
 
 def cut_kernel(
-    meta_ref, scan_ref, above_ref, packed_ref, own_ref, partner_ref, upper_ref, lower_ref, probe_ref
+    meta_ref, scan_ref, above_ref, packed_ref, own_ref, upper_ref, lower_ref, swap_ref
 ):
     chunks, _, _, width = packed_ref.shape
     window = own_ref.shape[-1]
@@ -87,17 +87,22 @@
     for part in range(2):
         rows = jnp.concatenate([packed_ref[chunk, part, :CHUNK] for chunk in range(chunks)], axis=0)
         columns = dot(rows, pick).astype(bf16)
-        for index, target in enumerate((own_ref, partner_ref, upper_ref, lower_ref)):
+        for index, target in ((0, own_ref), (2, upper_ref), (3, lower_ref)):
             target[part] = columns[:, index * window : (index + 1) * window]
         for chunk in range(chunks):
-            probe_ref[chunk, part] = packed_ref[chunk, part, CHUNK:]
+            swap_ref[chunk, part] = packed_ref[chunk, part, CHUNK:]
+        partner = columns[:, window : 2 * window]
+        for pair in range(chunks // 2):
+            swap_ref[chunks + pair, part] = jnp.concatenate(
+                [partner[(2 * pair + i) * CHUNK : (2 * pair + i + 1) * CHUNK] for i in range(2)], axis=1
+            )
 
 
 def touch_kernel(
-    meta_ref, scan_ref, own_ref, other_ref, below0_ref, below1_ref, touched_ref
+    meta_ref, scan_ref, own_ref, swapped_ref, below0_ref, below1_ref, touched_ref
 ):
     lane, quarter, member = meta_ref[0], meta_ref[1], meta_ref[5]
-    height = own_ref.shape[1]
+    height, window = own_ref.shape[1:]
     touched = touched_ref.shape[1]
     row_start = scan_ref[lane * QUARTERS + quarter]
     first = first_row(row_start, member)
@@ -111,7 +116,11 @@
     )
     for part in range(2):
         below = below0_ref[part] + below1_ref[part]
-        stack = jnp.concatenate([own_ref[part], other_ref[part], below], axis=0)
+        other = []
+        for pair in range(QUARTERS, swapped_ref.shape[0]):
+            beside = swapped_ref[pair, part]
+            other += [beside[:, :window], beside[:, window:]]
+        stack = jnp.concatenate([own_ref[part], *other, below], axis=0)
         touched_ref[part] = dot(pick, stack).astype(bf16)
 
 
@@ -286,24 +295,23 @@
     packed = lax.all_to_all(packed, "zq", 0, 0, tiled=True)
     cut_shape = (2, quarters * chunk_rows, window)
     lane_shape = (quarters, 2, chunk_rows, width)
-    own, partner, upper, lower, lane_modes = call(
+    own, upper, lower, to_swap = call(
         cut_kernel, "cut", (meta, scan, above), (packed,),
-        [jax.ShapeDtypeStruct(cut_shape, bf16)] * 4 + [jax.ShapeDtypeStruct(lane_shape, bf16)],
-    )
-    other_modes = lax.ppermute(lane_modes, "xl", swap)
-    other = lax.ppermute(partner, "xl", swap)
+        [jax.ShapeDtypeStruct(cut_shape, bf16)] * 3
+        + [jax.ShapeDtypeStruct((quarters + quarters // 2,) + lane_shape[1:], bf16)],
+    )
+    swapped = lax.ppermute(to_swap, "xl", swap)
     below0 = lax.ppermute(upper, axes, up_first)
     below1 = lax.ppermute(lower, axes, up_second)
-    lane_modes, other_modes, other, below0, below1 = lax.optimization_barrier(
-        (lane_modes, other_modes, other, below0, below1)
-    )
+    to_swap, swapped, below0, below1 = lax.optimization_barrier((to_swap, swapped, below0, below1))
+    lane_modes, other_modes = to_swap[:quarters], swapped[:quarters]
     part_modes = jnp.concatenate([lane_modes, other_modes], axis=0)
     shared = [
         lax.ppermute(part_modes, "y", [(i, (i + d) % ups) for i in range(ups)]) for d in range(1, ups)
     ]
     touched_shape = (2, window // RUN + CHUNK, window)
     touched = call(
-        touch_kernel, "touch", (meta, scan), (own, other, below0, below1),
+        touch_kernel, "touch", (meta, scan), (own, swapped, below0, below1),
         jax.ShapeDtypeStruct(touched_shape, bf16),
     )
     touched = lax.all_gather(touched, "zr", axis=0)

time: 149 us -> 146 us (0.980)
  starting transfers between devices: 61.3 us -> 58.6 us
    ppermute x2 -> x1, starting transfers between devices: 5.28 us -> 3.12 us  [on_device(): swapped = lax.ppermute(to_swap, 'xl', swap)]
  transfers between devices with their start and end apart: 13 -> 12, of which waited for: 5 -> 5; matrix products, arithmetic and copies ran while one was open for 1% -> 1% of each run, Pallas kernels for 1% -> 1%
where the time goes in v5:
time: 146 us; the launch traced here: 145 us
  starting transfers between devices  58.6 us (40%)
  blocking collectives  54.9 us (38%)
  waiting for transfers between devices  16.1 us (11%)
  Pallas kernels  11 us (8%)
  other arithmetic  2.49 us (2%)
  local copies, waits for them, and re-layouts  1.87 us (1%)
    all_to_all x1, blocking collectives, on_device(): terms = lax.all_to_all(half_sum, 'zq', 0, 0, tiled=True)  18.1 us
    all_to_all x1, starting transfers between devices, on_device(): packed = lax.all_to_all(packed, 'zq', 0, 0, tiled=True)  15.6 us
    all_gather x1, blocking collectives, on_device(): touched = lax.all_gather(touched, 'zr', axis=0)  13.9 us
    all_gather x1, blocking collectives, on_device(): powers = lax.all_gather(power, 'zr', axis=0)  13.1 us
    pallas_call x5, Pallas kernels, call(): pl.pallas_call(kernel, grid_spec=pltpu.PrefetchScalarGridSpec(num_scalar_...  11 us
    all_to_all x1, blocking collectives, on_device(): pieces = lax.all_to_all(pieces, 'zr', 0, 0, tiled=True)  9.84 us
    ppermute x3, starting transfers between devices, on_device(): lax.ppermute(part_modes, 'y', [(i, (i + d) % ups) for i in range(ups)])  9.5 us
    ppermute x1, starting transfers between devices, on_device(): above0 = lax.ppermute(term, axes, down_first)  8.35 us
  transfers between devices with their start and end apart: 12, of which 5 were waited for; matrix products, arithmetic and copies ran while one was open for 1% of the time, Pallas kernels for 1%

profile of v5, /device:TPU:1, one launch (start us, length us, event | category | flops | bytes accessed | tf_op | source)
XLA Modules:
  0.0 145.1 jit_solution(12929253678932603180)
XLA Ops:
  0.0 0.0 copy-start
  0.0 0.0 copy-start.2
  0.0 0.0 copy-start.3
  0.0 1.0 copy-done
  1.1 0.8 convert.10
  1.9 0.7 broadcast_in_dim.2
  2.6 15.6 %all-to-all-start = ((bf16[4,2,32,512]{3,2,1,0:T(8,128)(2,1)}), bf16[4,2,32,512]{3,2,1,0:T(8,128)(2,1)S(1)}, u32[]{:S(2)}, u32[]{:S(2)}) async-start(bf16[4,2,32,512]{3,2,1,0:T(8,128)(2,1)} %broadcast_in_dim.2), calls=%async_computation | async-start | bytes 524288 | tf_op jit(solution)/shard_map/all_to_all | solution.py:295
  18.3 0.8 pad_add_fusion.scan_ref
  19.0 5.5 %collective-permute-start = (s32[32]{0:T(128)S(1)}, s32[32]{0:T(128)S(1)}, u32[]{:S(2)}, u32[]{:S(2)}) collective-permute-start(s32[32]{0:T(128)S(1)} %pad_add_fusion.scan_ref), channel_id=1, source_target_pairs={{0,32},{32,64},{64,96},{96,128},{128,160},{160,192},{192,224},{224... | collective-permute-start | bytes 392 | tf_op jit(solution)/shard_map/ppermute | solution.py:287
  24.5 0.1 stack.46.meta_ref
  24.6 0.6 collective-permute-done.above_ref
  25.2 6.8 %all-to-all-done.packed_ref = bf16[4,2,32,512]{3,2,1,0:T(8,128)(2,1)S(1)} async-done(((bf16[4,2,32,512]{3,2,1,0:T(8,128)(2,1)}), bf16[4,2,32,512]{3,2,1,0:T(8,128)(2,1)S(1)}, u32[]{:S(2)}, u32[]{:S(2)}) %all-to-all-start) | async-done | bytes 262176 | tf_op jit(solution)/shard_map/all_to_all | solution.py:295
  32.0 1.1 cut.1
  33.2 3.1 %collective-permute-start.1 = (bf16[6,2,16,512]{3,2,1,0:T(8,128)(2,1)S(1)}, bf16[6,2,16,512]{3,2,1,0:T(8,128)(2,1)S(1)}, u32[]{:S(2)}, u32[]{:S(2)}) collective-permute-start(bf16[6,2,16,512]{3,2,1,0:T(8,128)(2,1)S(1)} %get-tuple-element.22), channel_id=1, source_target_pairs={{0,16},{16,0},{1,17},{17,1},{2,18},{18,2},{3,19},{19,3},{4,20},{20... | collective-permute-start | bytes 589832 | tf_op jit(solution)/shard_map/ppermute | solution.py:303
  36.3 7.9 %collective-permute-start.2 = (bf16[2,64,256]{2,1,0:T(8,128)(2,1)S(1)}, bf16[2,64,256]{2,1,0:T(8,128)(2,1)S(1)}, u32[]{:S(2)}, u32[]{:S(2)}) collective-permute-start(bf16[2,64,256]{2,1,0:T(8,128)(2,1)S(1)} %get-tuple-element.20), channel_id=1, source_target_pairs={{32,0},{64,32},{96,64},{128,96},{160,128},{192,160},{224,192},{256... | collective-permute-start | bytes 196616 | tf_op jit(solution)/shard_map/ppermute | solution.py:304
  44.2 1.3 collective-permute-start.3
  45.5 3.1 %collective-permute-done.2.below0_ref = bf16[2,64,256]{2,1,0:T(8,128)(2,1)S(1)} collective-permute-done((bf16[2,64,256]{2,1,0:T(8,128)(2,1)S(1)}, bf16[2,64,256]{2,1,0:T(8,128)(2,1)S(1)}, u32[]{:S(2)}, u32[]{:S(2)}) %collective-permute-start.2) | collective-permute-done | bytes 65568 | tf_op jit(solution)/shard_map/ppermute | solution.py:304
  48.7 0.0 collective-permute-done.3.below1_ref
  48.7 0.0 collective-permute-done.1.swapped_ref
  48.8 4.6 %collective-permute-start.6 = (bf16[8,2,16,512]{3,2,1,0:T(8,128)(2,1)S(1)}, bf16[8,2,16,512]{3,2,1,0:T(8,128)(2,1)S(1)}, u32[]{:S(2)}, u32[]{:S(2)}) collective-permute-start(bf16[8,2,16,512]{3,2,1,0:T(8,128)(2,1)S(1)} %get-tuple-element.34), channel_id=1, source_target_pairs={{0,384},{128,0},{256,128},{384,256},{1,385},{129,1},{257,129},{385... | collective-permute-start | bytes 786440 | tf_op jit(solution)/shard_map/ppermute | solution.py:310
  53.4 2.3 %collective-permute-start.5 = (bf16[8,2,16,512]{3,2,1,0:T(8,128)(2,1)S(1)}, bf16[8,2,16,512]{3,2,1,0:T(8,128)(2,1)S(1)}, u32[]{:S(2)}, u32[]{:S(2)}) collective-permute-start(bf16[8,2,16,512]{3,2,1,0:T(8,128)(2,1)S(1)} %get-tuple-element.34), channel_id=1, source_target_pairs={{0,256},{128,384},{256,0},{384,128},{1,257},{129,385},{257,1},{385... | collective-permute-start | bytes 786440 | tf_op jit(solution)/shard_map/ppermute | solution.py:310
  55.7 2.6 %collective-permute-start.4 = (bf16[8,2,16,512]{3,2,1,0:T(8,128)(2,1)S(1)}, bf16[8,2,16,512]{3,2,1,0:T(8,128)(2,1)S(1)}, u32[]{:S(2)}, u32[]{:S(2)}) collective-permute-start(bf16[8,2,16,512]{3,2,1,0:T(8,128)(2,1)S(1)} %get-tuple-element.34), channel_id=1, source_target_pairs={{0,128},{128,256},{256,384},{384,0},{1,129},{129,257},{257,385},{3... | collective-permute-start | bytes 786440 | tf_op jit(solution)/shard_map/ppermute | solution.py:310
  58.3 0.8 touch.1
  59.1 13.9 %all-gather = bf16[8,80,256]{2,1,0:T(8,128)(2,1)S(1)} all-gather(bf16[2,80,256]{2,1,0:T(8,128)(2,1)S(1)} %touch.1), channel_id=2, replica_groups=mesh['y'=4,'xh'=2,'c'=2,'xl'=2,'zq'=4,'zr'=4] {'zr'}, dimensions={0}, use_global_device_ids=true | all-gather | bytes 409600 | tf_op jit(solution)/shard_map/all_gather | solution.py:317
  73.0 0.0 collective-permute-done.6
  73.0 0.0 collective-permute-done.5
  73.0 0.0 collective-permute-done.4
  73.0 0.1 pad_maximum_fusion.here_ref
  73.1 0.0 copy-start.1
  73.1 4.1 %collective-permute-start.7 = (bf16[4,8,2,16,512]{4,3,2,1,0:T(8,128)(2,1)S(1)}, bf16[4,8,2,16,512]{4,3,2,1,0:T(8,128)(2,1)S(1)}, u32[]{:S(2)}, u32[]{:S(2)}) collective-permute-start(bf16[4,8,2,16,512]{4,3,2,1,0:T(8,128)(2,1)S(1)} %pad_maximum_fusion.here_ref), channel_id=1, source_target_pairs={{0,32},{32,0},{1,33},{33,1},{2,34},{34,2},{3,35},{35,3},{4,36},{36... | collective-permute-start | bytes 3145736 | tf_op jit(solution)/shard_map/ppermute | solution.py:320
  77.2 2.3 %collective-permute-done.7.there_ref = bf16[4,8,2,16,512]{4,3,2,1,0:T(8,128)(2,1)S(1)} collective-permute-done((bf16[4,8,2,16,512]{4,3,2,1,0:T(8,128)(2,1)S(1)}, bf16[4,8,2,16,512]{4,3,2,1,0:T(8,128)(2,1)S(1)}, u32[]{:S(2)}, u32[]{:S(2)}) %collective-permute-start.7) | collective-permute-done | bytes 1048608 | tf_op jit(solution)/shard_map/ppermute | solution.py:320
  79.5 0.0 copy-done.2
  79.5 0.0 copy-done.3
  79.5 3.6 %forward.1 = (f32[8,512,256]{2,1,0:T(8,128)S(1)}, bf16[256,256]{1,0:T(8,128)(2,1)S(1)}) custom-call(s32[7]{0:T(128)S(1)} %stack.46.meta_ref, s32[32]{0:T(128)S(1)} %pad_add_fusion.scan_ref, bf16[4,2,80,256]{3,2,1,0:T(8,128)(2,1)S(1)} %bitcast.21, bf16[4,8,2,16,512]{4,3,2,1,0:T(8,128)(2,1)S(1)} %pad_maximum_fusion.here_ref, ...), custom_call_target="tpu_custom_call" | custom-call | flops 2147483648 | bytes 4194304 | tf_op jit(solution)/shard_map/forward/pallas_call | solution.py:246
  83.1 13.1 %all-gather.1 = bf16[1024,256]{1,0:T(8,128)(2,1)S(1)} all-gather(bf16[256,256]{1,0:T(8,128)(2,1)S(1)} %get-tuple-element.32), channel_id=3, replica_groups=mesh['y'=4,'xh'=2,'c'=2,'xl'=2,'zq'=4,'zr'=4] {'zr'}, dimensions={0}, use_global_device_ids=true | all-gather | bytes 655360 | tf_op jit(solution)/shard_map/all_gather | solution.py:331
  96.2 0.0 copy-done.1
  96.2 0.0 copy-start.4
  96.2 4.1 %backward.1 = bf16[4,2,80,256]{3,2,1,0:T(8,128)(2,1)S(1)} custom-call(s32[7]{0:T(128)S(1)} %stack.46.meta_ref, s32[32]{0:T(128)S(1)} %pad_add_fusion.scan_ref, f32[8,512,256]{2,1,0:T(8,128)S(1)} %get-tuple-element.31.spec_ref, bf16[4,256,256]{2,1,0:T(8,128)(2,1)S(1)} %bitcast.20, f32[1,8,256,256]{3,2,1,0:T(8,128)S(1)} %copy-done.1, ...), custom_call_target="tpu_custom_call" | custom-call | flops 2147483648 | bytes 4194304 | tf_op jit(solution)/shard_map/backward/pallas_call | solution.py:246
  100.3 9.8 %all_to_all.15 = bf16[4,2,80,256]{3,2,1,0:T(8,128)(2,1)S(1)} all-to-all(bf16[4,2,80,256]{3,2,1,0:T(8,128)(2,1)S(1)} %backward.1), channel_id=1, replica_groups=mesh['y'=4,'xh'=2,'c'=2,'xl'=2,'zq'=4,'zr'=4] {'zr'}, dimensions={0} | all-to-all | bytes 655360 | tf_op jit(solution)/shard_map/all_to_all | solution.py:338
  110.2 1.3 collective-permute-start.10
  111.5 8.3 %collective-permute-start.9 = (bf16[2,80,256]{2,1,0:T(8,128)(2,1)S(1)}, bf16[2,80,256]{2,1,0:T(8,128)(2,1)S(1)}, u32[]{:S(2)}, u32[]{:S(2)}) collective-permute-start(bf16[2,80,256]{2,1,0:T(8,128)(2,1)S(1)} %fusion.own_ref), channel_id=1, source_target_pairs={{0,32},{32,64},{64,96},{96,128},{128,160},{160,192},{192,224},{224... | collective-permute-start | bytes 245768 | tf_op jit(solution)/shard_map/ppermute | solution.py:342
  119.8 1.9 %collective-permute-start.8 = (bf16[2,80,256]{2,1,0:T(8,128)(2,1)S(1)}, bf16[2,80,256]{2,1,0:T(8,128)(2,1)S(1)}, u32[]{:S(2)}, u32[]{:S(2)}) collective-permute-start(bf16[2,80,256]{2,1,0:T(8,128)(2,1)S(1)} %fusion.own_ref), channel_id=1, source_target_pairs={{0,16},{16,0},{1,17},{17,1},{2,18},{18,2},{3,19},{19,3},{4,20},{20... | collective-permute-start | bytes 245768 | tf_op jit(solution)/shard_map/ppermute | solution.py:341
  121.8 0.0 collective-permute-done.10.lower_ref
  121.8 0.0 collective-permute-done.9.upper_ref
  121.8 3.2 %collective-permute-done.8.partner_ref = bf16[2,80,256]{2,1,0:T(8,128)(2,1)S(1)} collective-permute-done((bf16[2,80,256]{2,1,0:T(8,128)(2,1)S(1)}, bf16[2,80,256]{2,1,0:T(8,128)(2,1)S(1)}, u32[]{:S(2)}, u32[]{:S(2)}) %collective-permute-start.8) | collective-permute-done | bytes 81952 | tf_op jit(solution)/shard_map/ppermute | solution.py:341
  125.0 1.3 place.1
  126.4 18.1 %all_to_all.16 = bf16[4,2,16,512]{3,2,1,0:T(8,128)(2,1)S(1)} all-to-all(bf16[4,2,16,512]{3,2,1,0:T(8,128)(2,1)S(1)} %place.1), channel_id=1, replica_groups=mesh['y'=4,'xh'=2,'c'=2,'xl'=2,'zq'=4,'zr'=4] {'zq'}, dimensions={0} | all-to-all | bytes 262144 | tf_op jit(solution)/shard_map/all_to_all | solution.py:348
  144.5 0.0 copy-done.4
  144.5 0.6 multiply_subtract_fusion
  (8 shorter events, 0.1 us)
Async XLA Ops:
  0.0 1.0 copy-start
  0.0 79.5 %copy-start.2 = (bf16[512,512]{1,0:T(8,128)(2,1)S(1)}, bf16[512,512]{1,0:T(8,128)(2,1)}, u32[]{:S(2)}) copy-start(bf16[512,512]{1,0:T(8,128)(2,1)} %constant.45.clone.left_ref) | copy-start | bytes 1572868
  0.0 79.5 %copy-start.3 = (bf16[512,512]{1,0:T(8,128)(2,1)S(1)}, bf16[512,512]{1,0:T(8,128)(2,1)}, u32[]{:S(2)}) copy-start(bf16[512,512]{1,0:T(8,128)(2,1)} %constant.44.clone.right_ref) | copy-start | bytes 1572868
  2.6 29.4 %all-to-all-start = ((bf16[4,2,32,512]{3,2,1,0:T(8,128)(2,1)}), bf16[4,2,32,512]{3,2,1,0:T(8,128)(2,1)S(1)}, u32[]{:S(2)}, u32[]{:S(2)}) async-start(bf16[4,2,32,512]{3,2,1,0:T(8,128)(2,1)} %broadcast_in_dim.2), calls=%async_computation | async-start | bytes 524288 | tf_op jit(solution)/shard_map/all_to_all | solution.py:295
  19.0 6.2 %collective-permute-start = (s32[32]{0:T(128)S(1)}, s32[32]{0:T(128)S(1)}, u32[]{:S(2)}, u32[]{:S(2)}) collective-permute-start(s32[32]{0:T(128)S(1)} %pad_add_fusion.scan_ref), channel_id=1, source_target_pairs={{0,32},{32,64},{64,96},{96,128},{128,160},{160,192},{192,224},{224... | collective-permute-start | bytes 392 | tf_op jit(solution)/shard_map/ppermute | solution.py:287
  33.2 15.5 %collective-permute-start.1 = (bf16[6,2,16,512]{3,2,1,0:T(8,128)(2,1)S(1)}, bf16[6,2,16,512]{3,2,1,0:T(8,128)(2,1)S(1)}, u32[]{:S(2)}, u32[]{:S(2)}) collective-permute-start(bf16[6,2,16,512]{3,2,1,0:T(8,128)(2,1)S(1)} %get-tuple-element.22), channel_id=1, source_target_pairs={{0,16},{16,0},{1,17},{17,1},{2,18},{18,2},{3,19},{19,3},{4,20},{20... | collective-permute-start | bytes 589832 | tf_op jit(solution)/shard_map/ppermute | solution.py:303
  36.3 12.4 %collective-permute-start.2 = (bf16[2,64,256]{2,1,0:T(8,128)(2,1)S(1)}, bf16[2,64,256]{2,1,0:T(8,128)(2,1)S(1)}, u32[]{:S(2)}, u32[]{:S(2)}) collective-permute-start(bf16[2,64,256]{2,1,0:T(8,128)(2,1)S(1)} %get-tuple-element.20), channel_id=1, source_target_pairs={{32,0},{64,32},{96,64},{128,96},{160,128},{192,160},{224,192},{256... | collective-permute-start | bytes 196616 | tf_op jit(solution)/shard_map/ppermute | solution.py:304
  44.2 4.4 %collective-permute-start.3 = (bf16[2,64,256]{2,1,0:T(8,128)(2,1)S(1)}, bf16[2,64,256]{2,1,0:T(8,128)(2,1)S(1)}, u32[]{:S(2)}, u32[]{:S(2)}) collective-permute-start(bf16[2,64,256]{2,1,0:T(8,128)(2,1)S(1)} %get-tuple-element.21), channel_id=1, source_target_pairs={{32,16},{64,48},{96,80},{128,112},{160,144},{192,176},{224,208},{2... | collective-permute-start | bytes 196616 | tf_op jit(solution)/shard_map/ppermute | solution.py:305
  48.8 24.2 %collective-permute-start.6 = (bf16[8,2,16,512]{3,2,1,0:T(8,128)(2,1)S(1)}, bf16[8,2,16,512]{3,2,1,0:T(8,128)(2,1)S(1)}, u32[]{:S(2)}, u32[]{:S(2)}) collective-permute-start(bf16[8,2,16,512]{3,2,1,0:T(8,128)(2,1)S(1)} %get-tuple-element.34), channel_id=1, source_target_pairs={{0,384},{128,0},{256,128},{384,256},{1,385},{129,1},{257,129},{385... | collective-permute-start | bytes 786440 | tf_op jit(solution)/shard_map/ppermute | solution.py:310
  53.4 19.5 %collective-permute-start.5 = (bf16[8,2,16,512]{3,2,1,0:T(8,128)(2,1)S(1)}, bf16[8,2,16,512]{3,2,1,0:T(8,128)(2,1)S(1)}, u32[]{:S(2)}, u32[]{:S(2)}) collective-permute-start(bf16[8,2,16,512]{3,2,1,0:T(8,128)(2,1)S(1)} %get-tuple-element.34), channel_id=1, source_target_pairs={{0,256},{128,384},{256,0},{384,128},{1,257},{129,385},{257,1},{385... | collective-permute-start | bytes 786440 | tf_op jit(solution)/shard_map/ppermute | solution.py:310
  55.7 17.3 %collective-permute-start.4 = (bf16[8,2,16,512]{3,2,1,0:T(8,128)(2,1)S(1)}, bf16[8,2,16,512]{3,2,1,0:T(8,128)(2,1)S(1)}, u32[]{:S(2)}, u32[]{:S(2)}) collective-permute-start(bf16[8,2,16,512]{3,2,1,0:T(8,128)(2,1)S(1)} %get-tuple-element.34), channel_id=1, source_target_pairs={{0,128},{128,256},{256,384},{384,0},{1,129},{129,257},{257,385},{3... | collective-permute-start | bytes 786440 | tf_op jit(solution)/shard_map/ppermute | solution.py:310
  73.1 23.1 %copy-start.1 = (f32[1,8,256,256]{3,2,1,0:T(8,128)S(1)}, f32[1,8,256,256]{3,2,1,0:T(8,128)}, u32[]{:S(2)}) copy-start(f32[1,8,256,256]{3,2,1,0:T(8,128)} %amplitude_ref.1) | copy-start | bytes 6291460
  73.1 6.3 %collective-permute-start.7 = (bf16[4,8,2,16,512]{4,3,2,1,0:T(8,128)(2,1)S(1)}, bf16[4,8,2,16,512]{4,3,2,1,0:T(8,128)(2,1)S(1)}, u32[]{:S(2)}, u32[]{:S(2)}) collective-permute-start(bf16[4,8,2,16,512]{4,3,2,1,0:T(8,128)(2,1)S(1)} %pad_maximum_fusion.here_ref), channel_id=1, source_target_pairs={{0,32},{32,0},{1,33},{33,1},{2,34},{34,2},{3,35},{35,3},{4,36},{36... | collective-permute-start | bytes 3145736 | tf_op jit(solution)/shard_map/ppermute | solution.py:320
  96.2 48.3 %copy-start.4 = (f32[2,16,512]{2,1,0:T(8,128)S(1)}, f32[2,16,512]{2,1,0:T(8,128)}, u32[]{:S(2)}) copy-start(f32[2,16,512]{2,1,0:T(8,128)} %param.8) | copy-start | bytes 196612
  110.2 11.6 %collective-permute-start.10 = (bf16[2,80,256]{2,1,0:T(8,128)(2,1)S(1)}, bf16[2,80,256]{2,1,0:T(8,128)(2,1)S(1)}, u32[]{:S(2)}, u32[]{:S(2)}) collective-permute-start(bf16[2,80,256]{2,1,0:T(8,128)(2,1)S(1)} %fusion.own_ref), channel_id=1, source_target_pairs={{16,32},{48,64},{80,96},{112,128},{144,160},{176,192},{208,224},{2... | collective-permute-start | bytes 245768 | tf_op jit(solution)/shard_map/ppermute | solution.py:343
  111.5 10.3 %collective-permute-start.9 = (bf16[2,80,256]{2,1,0:T(8,128)(2,1)S(1)}, bf16[2,80,256]{2,1,0:T(8,128)(2,1)S(1)}, u32[]{:S(2)}, u32[]{:S(2)}) collective-permute-start(bf16[2,80,256]{2,1,0:T(8,128)(2,1)S(1)} %fusion.own_ref), channel_id=1, source_target_pairs={{0,32},{32,64},{64,96},{96,128},{128,160},{160,192},{192,224},{224... | collective-permute-start | bytes 245768 | tf_op jit(solution)/shard_map/ppermute | solution.py:342
  119.8 5.2 %collective-permute-start.8 = (bf16[2,80,256]{2,1,0:T(8,128)(2,1)S(1)}, bf16[2,80,256]{2,1,0:T(8,128)(2,1)S(1)}, u32[]{:S(2)}, u32[]{:S(2)}) collective-permute-start(bf16[2,80,256]{2,1,0:T(8,128)(2,1)S(1)} %fusion.own_ref), channel_id=1, source_target_pairs={{0,16},{16,0},{1,17},{17,1},{2,18},{18,2},{3,19},{19,3},{4,20},{20... | collective-permute-start | bytes 245768 | tf_op jit(solution)/shard_map/ppermute | solution.py:341

commit v6 on v5

--- a/solution.py
+++ b/solution.py
@@ -141,28 +141,68 @@
     return rows(0), rows(1)
 
 
-def forward_kernel(
-    meta_ref, scan_ref, touched_ref, here_ref, there_ref, right_ref, left_ref,
-    spec_ref, power_ref,
-):
-    lane, quarter = meta_ref[0], meta_ref[1]
-    window = power_ref.shape[-1]
+def half_product(source_ref, patch, meta_ref, modes, right):
+    up, count = meta_ref[6], source_ref.shape[0]
+    window = source_ref.shape[-1] // 2
+    exits = []
+    for mode in modes:
+        probe = []
+        for part in range(2):
+            pieces = []
+            for row in range(count):
+                piece = source_ref[lax.rem(up - row + count, count), mode, part]
+                pieces += [piece[:, :window], piece[:, window:]]
+            probe.append(jnp.concatenate(pieces, axis=0).astype(f32))
+        exit_real = (probe[0] * patch[0] - probe[1] * patch[1]).astype(bf16)
+        exit_imag = (probe[0] * patch[1] + probe[1] * patch[0]).astype(bf16)
+        exits.append(jnp.concatenate([exit_real, exit_imag], axis=1))
+    return dot(jnp.concatenate(exits, axis=0), right).astype(bf16)
+
+
+def begin_kernel(meta_ref, scan_ref, touched_ref, here_ref, right_ref, half_ref, patch_ref):
+    lane, quarter, core = meta_ref[0], meta_ref[1], meta_ref[2]
+    window = touched_ref.shape[-1]
+    run = window // (2 * here_ref.shape[0])
     row_start = scan_ref[lane * QUARTERS + quarter]
     pick = class_rows(touched_ref.shape[2], window, row_start, True)
-    patch = [
-        dot(pick, jnp.concatenate([touched_ref[member, part] for member in range(RUN)], axis=0))
-        for part in range(2)
-    ]
+    patch = []
+    for part in range(2):
+        stack = jnp.concatenate([touched_ref[member, part] for member in range(RUN)], axis=0)
+        full = dot(pick, stack)
+        even, odd = (
+            jnp.concatenate([full[i : i + run] for i in range(first, window, 2 * run)], axis=0)
+            for first in (0, run)
+        )
+        patch.append(jnp.where(core == 0, even, odd))
+        patch_ref[part] = jnp.where(core == 0, odd, even)
+    rows = half_ref.shape[1]
+    for start in range(0, half_ref.shape[0], AT_ONCE):
+        modes = range(start, start + AT_ONCE)
+        half = half_product(here_ref, patch, meta_ref, modes, right_ref[...])
+        for i in range(AT_ONCE):
+            half_ref[start + i] = half[i * rows : (i + 1) * rows]
+
+
+def forward_kernel(
+    meta_ref, half_ref, patch_ref, there_ref, right_ref, left_ref, spec_ref, power_ref
+):
+    core = meta_ref[2]
+    window = power_ref.shape[-1]
+    rows = half_ref.shape[1]
+    run = window // (2 * there_ref.shape[0])
+    patch = [patch_ref[part] for part in range(2)]
     total = jnp.zeros((window, window), f32)
     for start in range(0, spec_ref.shape[0], AT_ONCE):
-        exits = []
-        for mode in range(start, start + AT_ONCE):
-            probe_real, probe_imag = full_probe(here_ref, there_ref, meta_ref, mode)
-            exit_real = (probe_real * patch[0] - probe_imag * patch[1]).astype(bf16)
-            exit_imag = (probe_real * patch[1] + probe_imag * patch[0]).astype(bf16)
-            exits.append(jnp.concatenate([exit_real, exit_imag], axis=1))
-        half_spectrum = dot(jnp.concatenate(exits, axis=0), right_ref[...]).astype(bf16)
-        stacks = [on_top(half_spectrum[i * window : (i + 1) * window]) for i in range(AT_ONCE)]
+        modes = range(start, start + AT_ONCE)
+        others = half_product(there_ref, patch, meta_ref, modes, right_ref[...])
+        stacks = []
+        for i in range(AT_ONCE):
+            here, there = half_ref[start + i], others[i * rows : (i + 1) * rows]
+            even, odd = jnp.where(core == 0, here, there), jnp.where(core == 0, there, here)
+            pieces = []
+            for first in range(0, rows, run):
+                pieces += [even[first : first + run], odd[first : first + run]]
+            stacks.append(on_top(jnp.concatenate(pieces, axis=0)))
         spectra = dot(left_ref[...], jnp.concatenate(stacks, axis=1))
         for i in range(AT_ONCE):
             spectrum = spectra[:, i * window : (i + 1) * window]
@@ -320,13 +360,21 @@
     there = lax.ppermute(here, "c", swap)
     modes = here.shape[1]
     product_flops = modes * 2 * 2 * (2 * window) ** 2 * window
+    half_spectra, other_patch = call(
+        begin_kernel, "begin", (meta, scan), (touched, here, right),
+        [
+            jax.ShapeDtypeStruct((modes, window // 2, 2 * window), bf16),
+            jax.ShapeDtypeStruct((2, window // 2, window), f32),
+        ],
+        flops=product_flops // 4,
+    )
     spectrum, power = call(
-        forward_kernel, "forward", (meta, scan), (touched, here, there, right, left),
+        forward_kernel, "forward", (meta,), (half_spectra, other_patch, there, right, left),
         [
             jax.ShapeDtypeStruct((modes, 2 * window, window), f32),
             jax.ShapeDtypeStruct((window, window), bf16),
         ],
-        flops=product_flops,
+        flops=product_flops * 3 // 4,
     )
     powers = lax.all_gather(power, "zr", axis=0)
     pieces = call(

time: 146 us -> 145 us (level)
  waiting for transfers between devices: 16.1 us -> 14.4 us
    ppermute x1, waiting for transfers between devices: 2.26 us -> 0.6 us  [on_device(): there = lax.ppermute(here, 'c', swap)]
    pallas_call x5 -> x6, Pallas kernels: 11 us -> 12 us  [call(): pl.pallas_call(kernel, grid_spec=pltpu.PrefetchScalarGridSpec(num_scalar_...]
  transfers between devices with their start and end apart: 12 -> 12, of which waited for: 5 -> 5; matrix products, arithmetic and copies ran while one was open for 1% -> 1% of each run, Pallas kernels for 1% -> 2%
where the time goes in v6:
time: 145 us
  starting transfers between devices  58.6 us (40%)
  blocking collectives  54.9 us (38%)
  waiting for transfers between devices  14.4 us (10%)
  Pallas kernels  12 us (8%)
  other arithmetic  2.49 us (2%)
  local copies, waits for them, and re-layouts  1.88 us (1%)
    all_to_all x1, blocking collectives, on_device(): terms = lax.all_to_all(half_sum, 'zq', 0, 0, tiled=True)  18.1 us
    all_to_all x1, starting transfers between devices, on_device(): packed = lax.all_to_all(packed, 'zq', 0, 0, tiled=True)  15.6 us
    all_gather x1, blocking collectives, on_device(): touched = lax.all_gather(touched, 'zr', axis=0)  13.9 us
    all_gather x1, blocking collectives, on_device(): powers = lax.all_gather(power, 'zr', axis=0)  13 us
    pallas_call x6, Pallas kernels, call(): pl.pallas_call(kernel, grid_spec=pltpu.PrefetchScalarGridSpec(num_scalar_...  12 us
    all_to_all x1, blocking collectives, on_device(): pieces = lax.all_to_all(pieces, 'zr', 0, 0, tiled=True)  9.86 us
    ppermute x3, starting transfers between devices, on_device(): lax.ppermute(part_modes, 'y', [(i, (i + d) % ups) for i in range(ups)])  9.5 us
    ppermute x1, starting transfers between devices, on_device(): above0 = lax.ppermute(term, axes, down_first)  8.37 us
  transfers between devices with their start and end apart: 12, of which 5 were waited for; matrix products, arithmetic and copies ran while one was open for 1% of the time, Pallas kernels for 2%

profile of v6, /device:TPU:1, one launch (start us, length us, event | category | flops | bytes accessed | tf_op | source)
XLA Modules:
  0.0 144.5 jit_solution(10748934441816083537)
XLA Ops:
  0.0 0.0 copy-start
  0.0 0.0 copy-start.2
  0.0 0.0 copy-start.3
  0.0 1.0 copy-done
  1.1 0.8 convert.10
  1.9 0.7 broadcast_in_dim.2
  2.6 15.6 %all-to-all-start = ((bf16[4,2,32,512]{3,2,1,0:T(8,128)(2,1)}), bf16[4,2,32,512]{3,2,1,0:T(8,128)(2,1)S(1)}, u32[]{:S(2)}, u32[]{:S(2)}) async-start(bf16[4,2,32,512]{3,2,1,0:T(8,128)(2,1)} %broadcast_in_dim.2), calls=%async_computation | async-start | bytes 524288 | tf_op jit(solution)/shard_map/all_to_all | solution.py:335
  18.3 0.8 pad_add_fusion.scan_ref
  19.0 5.5 %collective-permute-start = (s32[32]{0:T(128)S(1)}, s32[32]{0:T(128)S(1)}, u32[]{:S(2)}, u32[]{:S(2)}) collective-permute-start(s32[32]{0:T(128)S(1)} %pad_add_fusion.scan_ref), channel_id=1, source_target_pairs={{0,32},{32,64},{64,96},{96,128},{128,160},{160,192},{192,224},{224... | collective-permute-start | bytes 392 | tf_op jit(solution)/shard_map/ppermute | solution.py:327
  24.5 0.1 stack.46.meta_ref
  24.6 0.6 collective-permute-done.above_ref
  25.2 6.8 %all-to-all-done.packed_ref = bf16[4,2,32,512]{3,2,1,0:T(8,128)(2,1)S(1)} async-done(((bf16[4,2,32,512]{3,2,1,0:T(8,128)(2,1)}), bf16[4,2,32,512]{3,2,1,0:T(8,128)(2,1)S(1)}, u32[]{:S(2)}, u32[]{:S(2)}) %all-to-all-start) | async-done | bytes 262176 | tf_op jit(solution)/shard_map/all_to_all | solution.py:335
  32.0 1.1 cut.1
  33.2 3.1 %collective-permute-start.1 = (bf16[6,2,16,512]{3,2,1,0:T(8,128)(2,1)S(1)}, bf16[6,2,16,512]{3,2,1,0:T(8,128)(2,1)S(1)}, u32[]{:S(2)}, u32[]{:S(2)}) collective-permute-start(bf16[6,2,16,512]{3,2,1,0:T(8,128)(2,1)S(1)} %get-tuple-element.24), channel_id=1, source_target_pairs={{0,16},{16,0},{1,17},{17,1},{2,18},{18,2},{3,19},{19,3},{4,20},{20... | collective-permute-start | bytes 589832 | tf_op jit(solution)/shard_map/ppermute | solution.py:343
  36.3 7.9 %collective-permute-start.2 = (bf16[2,64,256]{2,1,0:T(8,128)(2,1)S(1)}, bf16[2,64,256]{2,1,0:T(8,128)(2,1)S(1)}, u32[]{:S(2)}, u32[]{:S(2)}) collective-permute-start(bf16[2,64,256]{2,1,0:T(8,128)(2,1)S(1)} %get-tuple-element.22), channel_id=1, source_target_pairs={{32,0},{64,32},{96,64},{128,96},{160,128},{192,160},{224,192},{256... | collective-permute-start | bytes 196616 | tf_op jit(solution)/shard_map/ppermute | solution.py:344
  44.3 1.3 collective-permute-start.3
  45.6 3.1 %collective-permute-done.2.below0_ref = bf16[2,64,256]{2,1,0:T(8,128)(2,1)S(1)} collective-permute-done((bf16[2,64,256]{2,1,0:T(8,128)(2,1)S(1)}, bf16[2,64,256]{2,1,0:T(8,128)(2,1)S(1)}, u32[]{:S(2)}, u32[]{:S(2)}) %collective-permute-start.2) | collective-permute-done | bytes 65568 | tf_op jit(solution)/shard_map/ppermute | solution.py:344
  48.7 0.0 collective-permute-done.3.below1_ref
  48.7 0.0 collective-permute-done.1.swapped_ref
  48.8 4.6 %collective-permute-start.6 = (bf16[8,2,16,512]{3,2,1,0:T(8,128)(2,1)S(1)}, bf16[8,2,16,512]{3,2,1,0:T(8,128)(2,1)S(1)}, u32[]{:S(2)}, u32[]{:S(2)}) collective-permute-start(bf16[8,2,16,512]{3,2,1,0:T(8,128)(2,1)S(1)} %get-tuple-element.38), channel_id=1, source_target_pairs={{0,384},{128,0},{256,128},{384,256},{1,385},{129,1},{257,129},{385... | collective-permute-start | bytes 786440 | tf_op jit(solution)/shard_map/ppermute | solution.py:350
  53.4 2.3 %collective-permute-start.5 = (bf16[8,2,16,512]{3,2,1,0:T(8,128)(2,1)S(1)}, bf16[8,2,16,512]{3,2,1,0:T(8,128)(2,1)S(1)}, u32[]{:S(2)}, u32[]{:S(2)}) collective-permute-start(bf16[8,2,16,512]{3,2,1,0:T(8,128)(2,1)S(1)} %get-tuple-element.38), channel_id=1, source_target_pairs={{0,256},{128,384},{256,0},{384,128},{1,257},{129,385},{257,1},{385... | collective-permute-start | bytes 786440 | tf_op jit(solution)/shard_map/ppermute | solution.py:350
  55.7 2.6 %collective-permute-start.4 = (bf16[8,2,16,512]{3,2,1,0:T(8,128)(2,1)S(1)}, bf16[8,2,16,512]{3,2,1,0:T(8,128)(2,1)S(1)}, u32[]{:S(2)}, u32[]{:S(2)}) collective-permute-start(bf16[8,2,16,512]{3,2,1,0:T(8,128)(2,1)S(1)} %get-tuple-element.38), channel_id=1, source_target_pairs={{0,128},{128,256},{256,384},{384,0},{1,129},{129,257},{257,385},{3... | collective-permute-start | bytes 786440 | tf_op jit(solution)/shard_map/ppermute | solution.py:350
  58.3 0.8 touch.1
  59.1 13.9 %all-gather = bf16[8,80,256]{2,1,0:T(8,128)(2,1)S(1)} all-gather(bf16[2,80,256]{2,1,0:T(8,128)(2,1)S(1)} %touch.1), channel_id=2, replica_groups=mesh['y'=4,'xh'=2,'c'=2,'xl'=2,'zq'=4,'zr'=4] {'zr'}, dimensions={0}, use_global_device_ids=true | all-gather | bytes 409600 | tf_op jit(solution)/shard_map/all_gather | solution.py:357
  73.0 0.0 collective-permute-done.6
  73.0 0.0 collective-permute-done.5
  73.0 0.0 collective-permute-done.4
  73.0 0.1 pad_maximum_fusion.here_ref
  73.1 0.0 copy-start.1
  73.1 4.0 %collective-permute-start.7 = (bf16[4,8,2,16,512]{4,3,2,1,0:T(8,128)(2,1)S(1)}, bf16[4,8,2,16,512]{4,3,2,1,0:T(8,128)(2,1)S(1)}, u32[]{:S(2)}, u32[]{:S(2)}) collective-permute-start(bf16[4,8,2,16,512]{4,3,2,1,0:T(8,128)(2,1)S(1)} %pad_maximum_fusion.here_ref), channel_id=1, source_target_pairs={{0,32},{32,0},{1,33},{33,1},{2,34},{34,2},{3,35},{35,3},{4,36},{36... | collective-permute-start | bytes 3145736 | tf_op jit(solution)/shard_map/ppermute | solution.py:360
  77.2 0.0 copy-done.2
  77.2 1.7 %begin.1 = (bf16[8,128,512]{2,1,0:T(8,128)(2,1)S(1)}, f32[2,128,256]{2,1,0:T(8,128)S(1)}) custom-call(s32[7]{0:T(128)S(1)} %stack.46.meta_ref, s32[32]{0:T(128)S(1)} %pad_add_fusion.scan_ref, bf16[4,2,80,256]{3,2,1,0:T(8,128)(2,1)S(1)} %bitcast.21, bf16[4,8,2,16,512]{4,3,2,1,0:T(8,128)(2,1)S(1)} %pad_maximum_fusion.here_ref, bf16[512,512]{1,0:T(8,128)(2,1)S(1)} %copy-done.2), custom_call_target="tpu_custom_call" | custom-call | flops 536870912 | bytes 4194304 | tf_op jit(solution)/shard_map/begin/pallas_call | solution.py:286
  78.9 0.6 collective-permute-done.7.there_ref
  79.5 0.0 copy-done.3
  79.5 3.0 %forward.1 = (f32[8,512,256]{2,1,0:T(8,128)S(1)}, bf16[256,256]{1,0:T(8,128)(2,1)S(1)}) custom-call(s32[7]{0:T(128)S(1)} %stack.46.meta_ref, bf16[8,128,512]{2,1,0:T(8,128)(2,1)S(1)} %get-tuple-element.33.half_ref, f32[2,128,256]{2,1,0:T(8,128)S(1)} %get-tuple-element.34.patch_ref, bf16[4,8,2,16,512]{4,3,2,1,0:T(8,128)(2,1)S(1)} %collective-permute-done.7.there_ref, ...), custom_call_target="tpu_custom_call" | custom-call | flops 1610612736 | bytes 4194304 | tf_op jit(solution)/shard_map/forward/pallas_call | solution.py:286
  82.4 13.0 %all-gather.1 = bf16[1024,256]{1,0:T(8,128)(2,1)S(1)} all-gather(bf16[256,256]{1,0:T(8,128)(2,1)S(1)} %get-tuple-element.36), channel_id=3, replica_groups=mesh['y'=4,'xh'=2,'c'=2,'xl'=2,'zq'=4,'zr'=4] {'zr'}, dimensions={0}, use_global_device_ids=true | all-gather | bytes 655360 | tf_op jit(solution)/shard_map/all_gather | solution.py:379
  95.5 0.0 copy-done.1
  95.5 0.0 copy-start.4
  95.5 4.1 %backward.1 = bf16[4,2,80,256]{3,2,1,0:T(8,128)(2,1)S(1)} custom-call(s32[7]{0:T(128)S(1)} %stack.46.meta_ref, s32[32]{0:T(128)S(1)} %pad_add_fusion.scan_ref, f32[8,512,256]{2,1,0:T(8,128)S(1)} %get-tuple-element.35.spec_ref, bf16[4,256,256]{2,1,0:T(8,128)(2,1)S(1)} %bitcast.20, f32[1,8,256,256]{3,2,1,0:T(8,128)S(1)} %copy-done.1, ...), custom_call_target="tpu_custom_call" | custom-call | flops 2147483648 | bytes 4194304 | tf_op jit(solution)/shard_map/backward/pallas_call | solution.py:286
  99.6 9.9 %all_to_all.15 = bf16[4,2,80,256]{3,2,1,0:T(8,128)(2,1)S(1)} all-to-all(bf16[4,2,80,256]{3,2,1,0:T(8,128)(2,1)S(1)} %backward.1), channel_id=1, replica_groups=mesh['y'=4,'xh'=2,'c'=2,'xl'=2,'zq'=4,'zr'=4] {'zr'}, dimensions={0} | all-to-all | bytes 655360 | tf_op jit(solution)/shard_map/all_to_all | solution.py:386
  109.5 1.3 collective-permute-start.10
  110.8 8.4 %collective-permute-start.9 = (bf16[2,80,256]{2,1,0:T(8,128)(2,1)S(1)}, bf16[2,80,256]{2,1,0:T(8,128)(2,1)S(1)}, u32[]{:S(2)}, u32[]{:S(2)}) collective-permute-start(bf16[2,80,256]{2,1,0:T(8,128)(2,1)S(1)} %fusion.own_ref), channel_id=1, source_target_pairs={{0,32},{32,64},{64,96},{96,128},{128,160},{160,192},{192,224},{224... | collective-permute-start | bytes 245768 | tf_op jit(solution)/shard_map/ppermute | solution.py:390
  119.2 1.9 %collective-permute-start.8 = (bf16[2,80,256]{2,1,0:T(8,128)(2,1)S(1)}, bf16[2,80,256]{2,1,0:T(8,128)(2,1)S(1)}, u32[]{:S(2)}, u32[]{:S(2)}) collective-permute-start(bf16[2,80,256]{2,1,0:T(8,128)(2,1)S(1)} %fusion.own_ref), channel_id=1, source_target_pairs={{0,16},{16,0},{1,17},{17,1},{2,18},{18,2},{3,19},{19,3},{4,20},{20... | collective-permute-start | bytes 245768 | tf_op jit(solution)/shard_map/ppermute | solution.py:389
  121.1 0.0 collective-permute-done.10.lower_ref
  121.2 0.0 collective-permute-done.9.upper_ref
  121.2 3.2 %collective-permute-done.8.partner_ref = bf16[2,80,256]{2,1,0:T(8,128)(2,1)S(1)} collective-permute-done((bf16[2,80,256]{2,1,0:T(8,128)(2,1)S(1)}, bf16[2,80,256]{2,1,0:T(8,128)(2,1)S(1)}, u32[]{:S(2)}, u32[]{:S(2)}) %collective-permute-start.8) | collective-permute-done | bytes 81952 | tf_op jit(solution)/shard_map/ppermute | solution.py:389
  124.4 1.3 place.1
  125.7 18.1 %all_to_all.16 = bf16[4,2,16,512]{3,2,1,0:T(8,128)(2,1)S(1)} all-to-all(bf16[4,2,16,512]{3,2,1,0:T(8,128)(2,1)S(1)} %place.1), channel_id=1, replica_groups=mesh['y'=4,'xh'=2,'c'=2,'xl'=2,'zq'=4,'zr'=4] {'zq'}, dimensions={0} | all-to-all | bytes 262144 | tf_op jit(solution)/shard_map/all_to_all | solution.py:396
  143.9 0.0 copy-done.4
  143.9 0.6 multiply_subtract_fusion
  (8 shorter events, 0.1 us)
Async XLA Ops:
  0.0 1.0 copy-start
  0.0 77.2 %copy-start.2 = (bf16[512,512]{1,0:T(8,128)(2,1)S(1)}, bf16[512,512]{1,0:T(8,128)(2,1)}, u32[]{:S(2)}) copy-start(bf16[512,512]{1,0:T(8,128)(2,1)} %constant.44.clone.right_ref) | copy-start | bytes 1572868
  0.0 79.5 %copy-start.3 = (bf16[512,512]{1,0:T(8,128)(2,1)S(1)}, bf16[512,512]{1,0:T(8,128)(2,1)}, u32[]{:S(2)}) copy-start(bf16[512,512]{1,0:T(8,128)(2,1)} %constant.45.clone.left_ref) | copy-start | bytes 1572868
  2.6 29.4 %all-to-all-start = ((bf16[4,2,32,512]{3,2,1,0:T(8,128)(2,1)}), bf16[4,2,32,512]{3,2,1,0:T(8,128)(2,1)S(1)}, u32[]{:S(2)}, u32[]{:S(2)}) async-start(bf16[4,2,32,512]{3,2,1,0:T(8,128)(2,1)} %broadcast_in_dim.2), calls=%async_computation | async-start | bytes 524288 | tf_op jit(solution)/shard_map/all_to_all | solution.py:335
  19.0 6.2 %collective-permute-start = (s32[32]{0:T(128)S(1)}, s32[32]{0:T(128)S(1)}, u32[]{:S(2)}, u32[]{:S(2)}) collective-permute-start(s32[32]{0:T(128)S(1)} %pad_add_fusion.scan_ref), channel_id=1, source_target_pairs={{0,32},{32,64},{64,96},{96,128},{128,160},{160,192},{192,224},{224... | collective-permute-start | bytes 392 | tf_op jit(solution)/shard_map/ppermute | solution.py:327
  33.2 15.5 %collective-permute-start.1 = (bf16[6,2,16,512]{3,2,1,0:T(8,128)(2,1)S(1)}, bf16[6,2,16,512]{3,2,1,0:T(8,128)(2,1)S(1)}, u32[]{:S(2)}, u32[]{:S(2)}) collective-permute-start(bf16[6,2,16,512]{3,2,1,0:T(8,128)(2,1)S(1)} %get-tuple-element.24), channel_id=1, source_target_pairs={{0,16},{16,0},{1,17},{17,1},{2,18},{18,2},{3,19},{19,3},{4,20},{20... | collective-permute-start | bytes 589832 | tf_op jit(solution)/shard_map/ppermute | solution.py:343
  36.3 12.4 %collective-permute-start.2 = (bf16[2,64,256]{2,1,0:T(8,128)(2,1)S(1)}, bf16[2,64,256]{2,1,0:T(8,128)(2,1)S(1)}, u32[]{:S(2)}, u32[]{:S(2)}) collective-permute-start(bf16[2,64,256]{2,1,0:T(8,128)(2,1)S(1)} %get-tuple-element.22), channel_id=1, source_target_pairs={{32,0},{64,32},{96,64},{128,96},{160,128},{192,160},{224,192},{256... | collective-permute-start | bytes 196616 | tf_op jit(solution)/shard_map/ppermute | solution.py:344
  44.3 4.5 %collective-permute-start.3 = (bf16[2,64,256]{2,1,0:T(8,128)(2,1)S(1)}, bf16[2,64,256]{2,1,0:T(8,128)(2,1)S(1)}, u32[]{:S(2)}, u32[]{:S(2)}) collective-permute-start(bf16[2,64,256]{2,1,0:T(8,128)(2,1)S(1)} %get-tuple-element.23), channel_id=1, source_target_pairs={{32,16},{64,48},{96,80},{128,112},{160,144},{192,176},{224,208},{2... | collective-permute-start | bytes 196616 | tf_op jit(solution)/shard_map/ppermute | solution.py:345
  48.8 24.2 %collective-permute-start.6 = (bf16[8,2,16,512]{3,2,1,0:T(8,128)(2,1)S(1)}, bf16[8,2,16,512]{3,2,1,0:T(8,128)(2,1)S(1)}, u32[]{:S(2)}, u32[]{:S(2)}) collective-permute-start(bf16[8,2,16,512]{3,2,1,0:T(8,128)(2,1)S(1)} %get-tuple-element.38), channel_id=1, source_target_pairs={{0,384},{128,0},{256,128},{384,256},{1,385},{129,1},{257,129},{385... | collective-permute-start | bytes 786440 | tf_op jit(solution)/shard_map/ppermute | solution.py:350
  53.4 19.6 %collective-permute-start.5 = (bf16[8,2,16,512]{3,2,1,0:T(8,128)(2,1)S(1)}, bf16[8,2,16,512]{3,2,1,0:T(8,128)(2,1)S(1)}, u32[]{:S(2)}, u32[]{:S(2)}) collective-permute-start(bf16[8,2,16,512]{3,2,1,0:T(8,128)(2,1)S(1)} %get-tuple-element.38), channel_id=1, source_target_pairs={{0,256},{128,384},{256,0},{384,128},{1,257},{129,385},{257,1},{385... | collective-permute-start | bytes 786440 | tf_op jit(solution)/shard_map/ppermute | solution.py:350
  55.7 17.3 %collective-permute-start.4 = (bf16[8,2,16,512]{3,2,1,0:T(8,128)(2,1)S(1)}, bf16[8,2,16,512]{3,2,1,0:T(8,128)(2,1)S(1)}, u32[]{:S(2)}, u32[]{:S(2)}) collective-permute-start(bf16[8,2,16,512]{3,2,1,0:T(8,128)(2,1)S(1)} %get-tuple-element.38), channel_id=1, source_target_pairs={{0,128},{128,256},{256,384},{384,0},{1,129},{129,257},{257,385},{3... | collective-permute-start | bytes 786440 | tf_op jit(solution)/shard_map/ppermute | solution.py:350
  73.1 22.3 %copy-start.1 = (f32[1,8,256,256]{3,2,1,0:T(8,128)S(1)}, f32[1,8,256,256]{3,2,1,0:T(8,128)}, u32[]{:S(2)}) copy-start(f32[1,8,256,256]{3,2,1,0:T(8,128)} %amplitude_ref.1) | copy-start | bytes 6291460
  73.1 6.3 %collective-permute-start.7 = (bf16[4,8,2,16,512]{4,3,2,1,0:T(8,128)(2,1)S(1)}, bf16[4,8,2,16,512]{4,3,2,1,0:T(8,128)(2,1)S(1)}, u32[]{:S(2)}, u32[]{:S(2)}) collective-permute-start(bf16[4,8,2,16,512]{4,3,2,1,0:T(8,128)(2,1)S(1)} %pad_maximum_fusion.here_ref), channel_id=1, source_target_pairs={{0,32},{32,0},{1,33},{33,1},{2,34},{34,2},{3,35},{35,3},{4,36},{36... | collective-permute-start | bytes 3145736 | tf_op jit(solution)/shard_map/ppermute | solution.py:360
  95.5 48.4 %copy-start.4 = (f32[2,16,512]{2,1,0:T(8,128)S(1)}, f32[2,16,512]{2,1,0:T(8,128)}, u32[]{:S(2)}) copy-start(f32[2,16,512]{2,1,0:T(8,128)} %param.8) | copy-start | bytes 196612
  109.5 11.6 %collective-permute-start.10 = (bf16[2,80,256]{2,1,0:T(8,128)(2,1)S(1)}, bf16[2,80,256]{2,1,0:T(8,128)(2,1)S(1)}, u32[]{:S(2)}, u32[]{:S(2)}) collective-permute-start(bf16[2,80,256]{2,1,0:T(8,128)(2,1)S(1)} %fusion.own_ref), channel_id=1, source_target_pairs={{16,32},{48,64},{80,96},{112,128},{144,160},{176,192},{208,224},{2... | collective-permute-start | bytes 245768 | tf_op jit(solution)/shard_map/ppermute | solution.py:391
  110.8 10.3 %collective-permute-start.9 = (bf16[2,80,256]{2,1,0:T(8,128)(2,1)S(1)}, bf16[2,80,256]{2,1,0:T(8,128)(2,1)S(1)}, u32[]{:S(2)}, u32[]{:S(2)}) collective-permute-start(bf16[2,80,256]{2,1,0:T(8,128)(2,1)S(1)} %fusion.own_ref), channel_id=1, source_target_pairs={{0,32},{32,64},{64,96},{96,128},{128,160},{160,192},{192,224},{224... | collective-permute-start | bytes 245768 | tf_op jit(solution)/shard_map/ppermute | solution.py:390
  119.2 5.2 %collective-permute-start.8 = (bf16[2,80,256]{2,1,0:T(8,128)(2,1)S(1)}, bf16[2,80,256]{2,1,0:T(8,128)(2,1)S(1)}, u32[]{:S(2)}, u32[]{:S(2)}) collective-permute-start(bf16[2,80,256]{2,1,0:T(8,128)(2,1)S(1)} %fusion.own_ref), channel_id=1, source_target_pairs={{0,16},{16,0},{1,17},{17,1},{2,18},{18,2},{3,19},{19,3},{4,20},{20... | collective-permute-start | bytes 245768 | tf_op jit(solution)/shard_map/ppermute | solution.py:389

commit v7 on v6

--- a/solution.py
+++ b/solution.py
@@ -343,7 +343,6 @@
     swapped = lax.ppermute(to_swap, "xl", swap)
     below0 = lax.ppermute(upper, axes, up_first)
     below1 = lax.ppermute(lower, axes, up_second)
-    to_swap, swapped, below0, below1 = lax.optimization_barrier((to_swap, swapped, below0, below1))
     lane_modes, other_modes = to_swap[:quarters], swapped[:quarters]
     part_modes = jnp.concatenate([lane_modes, other_modes], axis=0)
     shared = [
@@ -353,6 +352,7 @@
     touched = call(
         touch_kernel, "touch", (meta, scan), (own, swapped, below0, below1),
         jax.ShapeDtypeStruct(touched_shape, bf16),
+        flops=5 * 10**9,
     )
     touched = lax.all_gather(touched, "zr", axis=0)
     *shared, touched = lax.optimization_barrier((*shared, touched))

time: 145 us -> 145 us (level); the launches traced: 145 us -> 143 us
  starting transfers between devices: 58.6 us -> 61.9 us
  waiting for transfers between devices: 14.4 us -> 11.2 us
  blocking collectives: 54.9 us -> 52.6 us
    ppermute x1, waiting for transfers between devices: 3.15 us -> 0.01 us  [on_device(): below0 = lax.ppermute(upper, axes, up_first)]
    all_to_all x1, blocking collectives: 18.1 us -> 15.8 us  [on_device(): terms = lax.all_to_all(half_sum, 'zq', 0, 0, tiled=True)]
    ppermute x1, starting transfers between devices: 4.05 us -> 6.18 us  [on_device(): there = lax.ppermute(here, 'c', swap)]
  transfers between devices with their start and end apart: 12 -> 12, of which waited for: 5 -> 4; matrix products, arithmetic and copies ran while one was open for 1% -> 1% of each run, Pallas kernels for 2% -> 2%
where the time goes in v7:
time: 145 us; the launch traced here: 143 us
  starting transfers between devices  61.9 us (43%)
  blocking collectives  52.6 us (36%)
  Pallas kernels  12.1 us (8%)
  waiting for transfers between devices  11.2 us (8%)
  other arithmetic  2.49 us (2%)
  local copies, waits for them, and re-layouts  1.9 us (1%)
    all_to_all x1, blocking collectives, on_device(): terms = lax.all_to_all(half_sum, 'zq', 0, 0, tiled=True)  15.8 us
    all_to_all x1, starting transfers between devices, on_device(): packed = lax.all_to_all(packed, 'zq', 0, 0, tiled=True)  15.6 us
    all_gather x1, blocking collectives, on_device(): touched = lax.all_gather(touched, 'zr', axis=0)  14.2 us
    all_gather x1, blocking collectives, on_device(): powers = lax.all_gather(power, 'zr', axis=0)  13 us
    pallas_call x6, Pallas kernels, call(): pl.pallas_call(kernel, grid_spec=pltpu.PrefetchScalarGridSpec(num_scalar_...  12.1 us
    all_to_all x1, blocking collectives, on_device(): pieces = lax.all_to_all(pieces, 'zr', 0, 0, tiled=True)  9.65 us
    ppermute x1, starting transfers between devices, on_device(): above0 = lax.ppermute(term, axes, down_first)  9.52 us
    ppermute x3, starting transfers between devices, on_device(): lax.ppermute(part_modes, 'y', [(i, (i + d) % ups) for i in range(ups)])  9.5 us
  transfers between devices with their start and end apart: 12, of which 4 were waited for; matrix products, arithmetic and copies ran while one was open for 1% of the time, Pallas kernels for 2%

profile of v7, /device:TPU:1, one launch (start us, length us, event | category | flops | bytes accessed | tf_op | source)
XLA Modules:
  0.0 142.6 jit_solution(8538856333581481896)
XLA Ops:
  0.0 0.0 copy-start
  0.0 1.0 copy-done
  1.1 0.8 convert.10
  1.9 0.7 broadcast_in_dim.2
  2.6 15.6 %all-to-all-start = ((bf16[4,2,32,512]{3,2,1,0:T(8,128)(2,1)}), bf16[4,2,32,512]{3,2,1,0:T(8,128)(2,1)S(1)}, u32[]{:S(2)}, u32[]{:S(2)}) async-start(bf16[4,2,32,512]{3,2,1,0:T(8,128)(2,1)} %broadcast_in_dim.2), calls=%async_computation | async-start | bytes 524288 | tf_op jit(solution)/shard_map/all_to_all | solution.py:335
  18.3 0.8 pad_add_fusion.scan_ref
  19.0 5.5 %collective-permute-start = (s32[32]{0:T(128)S(1)}, s32[32]{0:T(128)S(1)}, u32[]{:S(2)}, u32[]{:S(2)}) collective-permute-start(s32[32]{0:T(128)S(1)} %pad_add_fusion.scan_ref), channel_id=1, source_target_pairs={{0,32},{32,64},{64,96},{96,128},{128,160},{160,192},{192,224},{224... | collective-permute-start | bytes 392 | tf_op jit(solution)/shard_map/ppermute | solution.py:327
  24.5 0.1 stack.46.meta_ref
  24.6 0.6 collective-permute-done.above_ref
  25.2 6.8 %all-to-all-done.packed_ref = bf16[4,2,32,512]{3,2,1,0:T(8,128)(2,1)S(1)} async-done(((bf16[4,2,32,512]{3,2,1,0:T(8,128)(2,1)}), bf16[4,2,32,512]{3,2,1,0:T(8,128)(2,1)S(1)}, u32[]{:S(2)}, u32[]{:S(2)}) %all-to-all-start) | async-done | bytes 262176 | tf_op jit(solution)/shard_map/all_to_all | solution.py:335
  32.0 1.1 cut.1
  33.2 3.1 %collective-permute-start.1 = (bf16[6,2,16,512]{3,2,1,0:T(8,128)(2,1)S(1)}, bf16[6,2,16,512]{3,2,1,0:T(8,128)(2,1)S(1)}, u32[]{:S(2)}, u32[]{:S(2)}) collective-permute-start(bf16[6,2,16,512]{3,2,1,0:T(8,128)(2,1)S(1)} %get-tuple-element.17), channel_id=1, source_target_pairs={{0,16},{16,0},{1,17},{17,1},{2,18},{18,2},{3,19},{19,3},{4,20},{20... | collective-permute-start | bytes 589832 | tf_op jit(solution)/shard_map/ppermute | solution.py:343
  36.3 7.9 %collective-permute-start.5 = (bf16[2,64,256]{2,1,0:T(8,128)(2,1)S(1)}, bf16[2,64,256]{2,1,0:T(8,128)(2,1)S(1)}, u32[]{:S(2)}, u32[]{:S(2)}) collective-permute-start(bf16[2,64,256]{2,1,0:T(8,128)(2,1)S(1)} %get-tuple-element.19), channel_id=1, source_target_pairs={{32,0},{64,32},{96,64},{128,96},{160,128},{192,160},{224,192},{256... | collective-permute-start | bytes 196616 | tf_op jit(solution)/shard_map/ppermute | solution.py:344
  44.3 1.3 collective-permute-start.6
  45.6 0.0 collective-permute-done.1.swapped_ref
  45.6 4.6 %collective-permute-start.4 = (bf16[8,2,16,512]{3,2,1,0:T(8,128)(2,1)S(1)}, bf16[8,2,16,512]{3,2,1,0:T(8,128)(2,1)S(1)}, u32[]{:S(2)}, u32[]{:S(2)}) collective-permute-start(bf16[8,2,16,512]{3,2,1,0:T(8,128)(2,1)S(1)} %get-tuple-element.30), channel_id=1, source_target_pairs={{0,384},{128,0},{256,128},{384,256},{1,385},{129,1},{257,129},{385... | collective-permute-start | bytes 786440 | tf_op jit(solution)/shard_map/ppermute | solution.py:349
  50.3 2.3 %collective-permute-start.3 = (bf16[8,2,16,512]{3,2,1,0:T(8,128)(2,1)S(1)}, bf16[8,2,16,512]{3,2,1,0:T(8,128)(2,1)S(1)}, u32[]{:S(2)}, u32[]{:S(2)}) collective-permute-start(bf16[8,2,16,512]{3,2,1,0:T(8,128)(2,1)S(1)} %get-tuple-element.30), channel_id=1, source_target_pairs={{0,256},{128,384},{256,0},{384,128},{1,257},{129,385},{257,1},{385... | collective-permute-start | bytes 786440 | tf_op jit(solution)/shard_map/ppermute | solution.py:349
  52.6 2.6 %collective-permute-start.2 = (bf16[8,2,16,512]{3,2,1,0:T(8,128)(2,1)S(1)}, bf16[8,2,16,512]{3,2,1,0:T(8,128)(2,1)S(1)}, u32[]{:S(2)}, u32[]{:S(2)}) collective-permute-start(bf16[8,2,16,512]{3,2,1,0:T(8,128)(2,1)S(1)} %get-tuple-element.30), channel_id=1, source_target_pairs={{0,128},{128,256},{256,384},{384,0},{1,129},{129,257},{257,385},{3... | collective-permute-start | bytes 786440 | tf_op jit(solution)/shard_map/ppermute | solution.py:349
  55.2 0.0 collective-permute-done.5.below0_ref
  55.2 0.0 collective-permute-done.6.below1_ref
  55.2 0.0 copy-start.2
  55.2 0.8 touch.1
  56.0 0.0 copy-start.3
  56.0 14.2 %all-gather = bf16[8,80,256]{2,1,0:T(8,128)(2,1)S(1)} all-gather(bf16[2,80,256]{2,1,0:T(8,128)(2,1)S(1)} %touch.1), channel_id=2, replica_groups=mesh['y'=4,'xh'=2,'c'=2,'xl'=2,'zq'=4,'zr'=4] {'zr'}, dimensions={0}, use_global_device_ids=true | all-gather | bytes 409600 | tf_op jit(solution)/shard_map/all_gather | solution.py:357
  70.2 0.0 collective-permute-done.4
  70.2 0.0 collective-permute-done.3
  70.2 0.0 collective-permute-done.2
  70.2 0.1 pad_maximum_fusion.here_ref
  70.3 0.0 copy-start.1
  70.4 6.2 %collective-permute-start.7 = (bf16[4,8,2,16,512]{4,3,2,1,0:T(8,128)(2,1)S(1)}, bf16[4,8,2,16,512]{4,3,2,1,0:T(8,128)(2,1)S(1)}, u32[]{:S(2)}, u32[]{:S(2)}) collective-permute-start(bf16[4,8,2,16,512]{4,3,2,1,0:T(8,128)(2,1)S(1)} %pad_maximum_fusion.here_ref), channel_id=1, source_target_pairs={{0,32},{32,0},{1,33},{33,1},{2,34},{34,2},{3,35},{35,3},{4,36},{36... | collective-permute-start | bytes 3145736 | tf_op jit(solution)/shard_map/ppermute | solution.py:360
  76.5 0.0 copy-done.2
  76.6 1.7 %begin.1 = (bf16[8,128,512]{2,1,0:T(8,128)(2,1)S(1)}, f32[2,128,256]{2,1,0:T(8,128)S(1)}) custom-call(s32[7]{0:T(128)S(1)} %stack.46.meta_ref, s32[32]{0:T(128)S(1)} %pad_add_fusion.scan_ref, bf16[4,2,80,256]{3,2,1,0:T(8,128)(2,1)S(1)} %bitcast.21, bf16[4,8,2,16,512]{4,3,2,1,0:T(8,128)(2,1)S(1)} %pad_maximum_fusion.here_ref, bf16[512,512]{1,0:T(8,128)(2,1)S(1)} %copy-done.2), custom_call_target="tpu_custom_call" | custom-call | flops 536870912 | bytes 4194304 | tf_op jit(solution)/shard_map/begin/pallas_call | solution.py:286
  78.3 0.6 collective-permute-done.7.there_ref
  78.8 0.0 copy-done.3
  78.8 3.0 %forward.1 = (f32[8,512,256]{2,1,0:T(8,128)S(1)}, bf16[256,256]{1,0:T(8,128)(2,1)S(1)}) custom-call(s32[7]{0:T(128)S(1)} %stack.46.meta_ref, bf16[8,128,512]{2,1,0:T(8,128)(2,1)S(1)} %get-tuple-element.25.half_ref, f32[2,128,256]{2,1,0:T(8,128)S(1)} %get-tuple-element.26.patch_ref, bf16[4,8,2,16,512]{4,3,2,1,0:T(8,128)(2,1)S(1)} %collective-permute-done.7.there_ref, ...), custom_call_target="tpu_custom_call" | custom-call | flops 1610612736 | bytes 4194304 | tf_op jit(solution)/shard_map/forward/pallas_call | solution.py:286
  81.8 13.0 %all-gather.1 = bf16[1024,256]{1,0:T(8,128)(2,1)S(1)} all-gather(bf16[256,256]{1,0:T(8,128)(2,1)S(1)} %get-tuple-element.28), channel_id=3, replica_groups=mesh['y'=4,'xh'=2,'c'=2,'xl'=2,'zq'=4,'zr'=4] {'zr'}, dimensions={0}, use_global_device_ids=true | all-gather | bytes 655360 | tf_op jit(solution)/shard_map/all_gather | solution.py:379
  94.8 0.0 copy-done.1
  94.8 0.0 copy-start.4
  94.8 4.2 %backward.1 = bf16[4,2,80,256]{3,2,1,0:T(8,128)(2,1)S(1)} custom-call(s32[7]{0:T(128)S(1)} %stack.46.meta_ref, s32[32]{0:T(128)S(1)} %pad_add_fusion.scan_ref, f32[8,512,256]{2,1,0:T(8,128)S(1)} %get-tuple-element.27.spec_ref, bf16[4,256,256]{2,1,0:T(8,128)(2,1)S(1)} %bitcast.20, f32[1,8,256,256]{3,2,1,0:T(8,128)S(1)} %copy-done.1, ...), custom_call_target="tpu_custom_call" | custom-call | flops 2147483648 | bytes 4194304 | tf_op jit(solution)/shard_map/backward/pallas_call | solution.py:286
  99.0 9.6 %all_to_all.15 = bf16[4,2,80,256]{3,2,1,0:T(8,128)(2,1)S(1)} all-to-all(bf16[4,2,80,256]{3,2,1,0:T(8,128)(2,1)S(1)} %backward.1), channel_id=1, replica_groups=mesh['y'=4,'xh'=2,'c'=2,'xl'=2,'zq'=4,'zr'=4] {'zr'}, dimensions={0} | all-to-all | bytes 655360 | tf_op jit(solution)/shard_map/all_to_all | solution.py:386
  108.7 1.3 collective-permute-start.10
  110.0 9.5 %collective-permute-start.9 = (bf16[2,80,256]{2,1,0:T(8,128)(2,1)S(1)}, bf16[2,80,256]{2,1,0:T(8,128)(2,1)S(1)}, u32[]{:S(2)}, u32[]{:S(2)}) collective-permute-start(bf16[2,80,256]{2,1,0:T(8,128)(2,1)S(1)} %fusion.own_ref), channel_id=1, source_target_pairs={{0,32},{32,64},{64,96},{96,128},{128,160},{160,192},{192,224},{224... | collective-permute-start | bytes 245768 | tf_op jit(solution)/shard_map/ppermute | solution.py:390
  119.5 1.9 %collective-permute-start.8 = (bf16[2,80,256]{2,1,0:T(8,128)(2,1)S(1)}, bf16[2,80,256]{2,1,0:T(8,128)(2,1)S(1)}, u32[]{:S(2)}, u32[]{:S(2)}) collective-permute-start(bf16[2,80,256]{2,1,0:T(8,128)(2,1)S(1)} %fusion.own_ref), channel_id=1, source_target_pairs={{0,16},{16,0},{1,17},{17,1},{2,18},{18,2},{3,19},{19,3},{4,20},{20... | collective-permute-start | bytes 245768 | tf_op jit(solution)/shard_map/ppermute | solution.py:389
  121.5 0.0 collective-permute-done.10.lower_ref
  121.5 0.0 collective-permute-done.9.upper_ref
  121.5 3.2 %collective-permute-done.8.partner_ref = bf16[2,80,256]{2,1,0:T(8,128)(2,1)S(1)} collective-permute-done((bf16[2,80,256]{2,1,0:T(8,128)(2,1)S(1)}, bf16[2,80,256]{2,1,0:T(8,128)(2,1)S(1)}, u32[]{:S(2)}, u32[]{:S(2)}) %collective-permute-start.8) | collective-permute-done | bytes 81952 | tf_op jit(solution)/shard_map/ppermute | solution.py:389
  124.7 1.3 place.1
  126.1 15.8 %all_to_all.16 = bf16[4,2,16,512]{3,2,1,0:T(8,128)(2,1)S(1)} all-to-all(bf16[4,2,16,512]{3,2,1,0:T(8,128)(2,1)S(1)} %place.1), channel_id=1, replica_groups=mesh['y'=4,'xh'=2,'c'=2,'xl'=2,'zq'=4,'zr'=4] {'zq'}, dimensions={0} | all-to-all | bytes 262144 | tf_op jit(solution)/shard_map/all_to_all | solution.py:396
  141.9 0.0 copy-done.4
  141.9 0.6 multiply_subtract_fusion
  (8 shorter events, 0.1 us)
Async XLA Ops:
  0.0 1.0 copy-start
  2.6 29.4 %all-to-all-start = ((bf16[4,2,32,512]{3,2,1,0:T(8,128)(2,1)}), bf16[4,2,32,512]{3,2,1,0:T(8,128)(2,1)S(1)}, u32[]{:S(2)}, u32[]{:S(2)}) async-start(bf16[4,2,32,512]{3,2,1,0:T(8,128)(2,1)} %broadcast_in_dim.2), calls=%async_computation | async-start | bytes 524288 | tf_op jit(solution)/shard_map/all_to_all | solution.py:335
  19.0 6.2 %collective-permute-start = (s32[32]{0:T(128)S(1)}, s32[32]{0:T(128)S(1)}, u32[]{:S(2)}, u32[]{:S(2)}) collective-permute-start(s32[32]{0:T(128)S(1)} %pad_add_fusion.scan_ref), channel_id=1, source_target_pairs={{0,32},{32,64},{64,96},{96,128},{128,160},{160,192},{192,224},{224... | collective-permute-start | bytes 392 | tf_op jit(solution)/shard_map/ppermute | solution.py:327
  33.2 12.4 %collective-permute-start.1 = (bf16[6,2,16,512]{3,2,1,0:T(8,128)(2,1)S(1)}, bf16[6,2,16,512]{3,2,1,0:T(8,128)(2,1)S(1)}, u32[]{:S(2)}, u32[]{:S(2)}) collective-permute-start(bf16[6,2,16,512]{3,2,1,0:T(8,128)(2,1)S(1)} %get-tuple-element.17), channel_id=1, source_target_pairs={{0,16},{16,0},{1,17},{17,1},{2,18},{18,2},{3,19},{19,3},{4,20},{20... | collective-permute-start | bytes 589832 | tf_op jit(solution)/shard_map/ppermute | solution.py:343
  36.3 18.8 %collective-permute-start.5 = (bf16[2,64,256]{2,1,0:T(8,128)(2,1)S(1)}, bf16[2,64,256]{2,1,0:T(8,128)(2,1)S(1)}, u32[]{:S(2)}, u32[]{:S(2)}) collective-permute-start(bf16[2,64,256]{2,1,0:T(8,128)(2,1)S(1)} %get-tuple-element.19), channel_id=1, source_target_pairs={{32,0},{64,32},{96,64},{128,96},{160,128},{192,160},{224,192},{256... | collective-permute-start | bytes 196616 | tf_op jit(solution)/shard_map/ppermute | solution.py:344
  44.3 10.9 %collective-permute-start.6 = (bf16[2,64,256]{2,1,0:T(8,128)(2,1)S(1)}, bf16[2,64,256]{2,1,0:T(8,128)(2,1)S(1)}, u32[]{:S(2)}, u32[]{:S(2)}) collective-permute-start(bf16[2,64,256]{2,1,0:T(8,128)(2,1)S(1)} %get-tuple-element.20), channel_id=1, source_target_pairs={{32,16},{64,48},{96,80},{128,112},{160,144},{192,176},{224,208},{2... | collective-permute-start | bytes 196616 | tf_op jit(solution)/shard_map/ppermute | solution.py:345
  45.6 24.5 %collective-permute-start.4 = (bf16[8,2,16,512]{3,2,1,0:T(8,128)(2,1)S(1)}, bf16[8,2,16,512]{3,2,1,0:T(8,128)(2,1)S(1)}, u32[]{:S(2)}, u32[]{:S(2)}) collective-permute-start(bf16[8,2,16,512]{3,2,1,0:T(8,128)(2,1)S(1)} %get-tuple-element.30), channel_id=1, source_target_pairs={{0,384},{128,0},{256,128},{384,256},{1,385},{129,1},{257,129},{385... | collective-permute-start | bytes 786440 | tf_op jit(solution)/shard_map/ppermute | solution.py:349
  50.3 19.9 %collective-permute-start.3 = (bf16[8,2,16,512]{3,2,1,0:T(8,128)(2,1)S(1)}, bf16[8,2,16,512]{3,2,1,0:T(8,128)(2,1)S(1)}, u32[]{:S(2)}, u32[]{:S(2)}) collective-permute-start(bf16[8,2,16,512]{3,2,1,0:T(8,128)(2,1)S(1)} %get-tuple-element.30), channel_id=1, source_target_pairs={{0,256},{128,384},{256,0},{384,128},{1,257},{129,385},{257,1},{385... | collective-permute-start | bytes 786440 | tf_op jit(solution)/shard_map/ppermute | solution.py:349
  52.6 17.6 %collective-permute-start.2 = (bf16[8,2,16,512]{3,2,1,0:T(8,128)(2,1)S(1)}, bf16[8,2,16,512]{3,2,1,0:T(8,128)(2,1)S(1)}, u32[]{:S(2)}, u32[]{:S(2)}) collective-permute-start(bf16[8,2,16,512]{3,2,1,0:T(8,128)(2,1)S(1)} %get-tuple-element.30), channel_id=1, source_target_pairs={{0,128},{128,256},{256,384},{384,0},{1,129},{129,257},{257,385},{3... | collective-permute-start | bytes 786440 | tf_op jit(solution)/shard_map/ppermute | solution.py:349
  55.2 21.4 %copy-start.2 = (bf16[512,512]{1,0:T(8,128)(2,1)S(1)}, bf16[512,512]{1,0:T(8,128)(2,1)}, u32[]{:S(2)}) copy-start(bf16[512,512]{1,0:T(8,128)(2,1)} %constant.44.clone.right_ref) | copy-start | bytes 1572868
  56.0 22.8 %copy-start.3 = (bf16[512,512]{1,0:T(8,128)(2,1)S(1)}, bf16[512,512]{1,0:T(8,128)(2,1)}, u32[]{:S(2)}) copy-start(bf16[512,512]{1,0:T(8,128)(2,1)} %constant.45.clone.left_ref) | copy-start | bytes 1572868
  70.3 24.4 %copy-start.1 = (f32[1,8,256,256]{3,2,1,0:T(8,128)S(1)}, f32[1,8,256,256]{3,2,1,0:T(8,128)}, u32[]{:S(2)}) copy-start(f32[1,8,256,256]{3,2,1,0:T(8,128)} %amplitude_ref.1) | copy-start | bytes 6291460
  70.4 8.5 %collective-permute-start.7 = (bf16[4,8,2,16,512]{4,3,2,1,0:T(8,128)(2,1)S(1)}, bf16[4,8,2,16,512]{4,3,2,1,0:T(8,128)(2,1)S(1)}, u32[]{:S(2)}, u32[]{:S(2)}) collective-permute-start(bf16[4,8,2,16,512]{4,3,2,1,0:T(8,128)(2,1)S(1)} %pad_maximum_fusion.here_ref), channel_id=1, source_target_pairs={{0,32},{32,0},{1,33},{33,1},{2,34},{34,2},{3,35},{35,3},{4,36},{36... | collective-permute-start | bytes 3145736 | tf_op jit(solution)/shard_map/ppermute | solution.py:360
  94.8 47.1 %copy-start.4 = (f32[2,16,512]{2,1,0:T(8,128)S(1)}, f32[2,16,512]{2,1,0:T(8,128)}, u32[]{:S(2)}) copy-start(f32[2,16,512]{2,1,0:T(8,128)} %param.8) | copy-start | bytes 196612
  108.7 12.8 %collective-permute-start.10 = (bf16[2,80,256]{2,1,0:T(8,128)(2,1)S(1)}, bf16[2,80,256]{2,1,0:T(8,128)(2,1)S(1)}, u32[]{:S(2)}, u32[]{:S(2)}) collective-permute-start(bf16[2,80,256]{2,1,0:T(8,128)(2,1)S(1)} %fusion.own_ref), channel_id=1, source_target_pairs={{16,32},{48,64},{80,96},{112,128},{144,160},{176,192},{208,224},{2... | collective-permute-start | bytes 245768 | tf_op jit(solution)/shard_map/ppermute | solution.py:391
  110.0 11.5 %collective-permute-start.9 = (bf16[2,80,256]{2,1,0:T(8,128)(2,1)S(1)}, bf16[2,80,256]{2,1,0:T(8,128)(2,1)S(1)}, u32[]{:S(2)}, u32[]{:S(2)}) collective-permute-start(bf16[2,80,256]{2,1,0:T(8,128)(2,1)S(1)} %fusion.own_ref), channel_id=1, source_target_pairs={{0,32},{32,64},{64,96},{96,128},{128,160},{160,192},{192,224},{224... | collective-permute-start | bytes 245768 | tf_op jit(solution)/shard_map/ppermute | solution.py:390
  119.5 5.2 %collective-permute-start.8 = (bf16[2,80,256]{2,1,0:T(8,128)(2,1)S(1)}, bf16[2,80,256]{2,1,0:T(8,128)(2,1)S(1)}, u32[]{:S(2)}, u32[]{:S(2)}) collective-permute-start(bf16[2,80,256]{2,1,0:T(8,128)(2,1)S(1)} %fusion.own_ref), channel_id=1, source_target_pairs={{0,16},{16,0},{1,17},{17,1},{2,18},{18,2},{3,19},{19,3},{4,20},{20... | collective-permute-start | bytes 245768 | tf_op jit(solution)/shard_map/ppermute | solution.py:389

commit v8 on v6

--- a/solution.py
+++ b/solution.py
@@ -14,7 +14,7 @@
 TILE_AXES = ("y", "xh", "c")
 DEPTH_AXES = ("zq", "zr")
 CHUNK = 16
-AT_ONCE = 2
+AT_ONCE = 4
 QUARTERS = 4
 RUN = 4
 VMEM_LIMIT = 20 * 1024 * 1024

time: 145 us -> 145 us (level)
  no operation moved by 1% of the time
where the time goes in v8:
time: 145 us; the launch traced here: 144 us
  starting transfers between devices  58.6 us (40%)
  blocking collectives  54.9 us (38%)
  waiting for transfers between devices  14.5 us (10%)
  Pallas kernels  11.4 us (8%)
  other arithmetic  2.49 us (2%)
  local copies, waits for them, and re-layouts  1.88 us (1%)
    all_to_all x1, blocking collectives, on_device(): terms = lax.all_to_all(half_sum, 'zq', 0, 0, tiled=True)  18.1 us
    all_to_all x1, starting transfers between devices, on_device(): packed = lax.all_to_all(packed, 'zq', 0, 0, tiled=True)  15.6 us
    all_gather x1, blocking collectives, on_device(): touched = lax.all_gather(touched, 'zr', axis=0)  13.9 us
    all_gather x1, blocking collectives, on_device(): powers = lax.all_gather(power, 'zr', axis=0)  13 us
    pallas_call x6, Pallas kernels, call(): pl.pallas_call(kernel, grid_spec=pltpu.PrefetchScalarGridSpec(num_scalar_...  11.4 us
    all_to_all x1, blocking collectives, on_device(): pieces = lax.all_to_all(pieces, 'zr', 0, 0, tiled=True)  9.86 us
    ppermute x3, starting transfers between devices, on_device(): lax.ppermute(part_modes, 'y', [(i, (i + d) % ups) for i in range(ups)])  9.5 us
    ppermute x1, starting transfers between devices, on_device(): above0 = lax.ppermute(term, axes, down_first)  8.38 us
  transfers between devices with their start and end apart: 12, of which 5 were waited for; matrix products, arithmetic and copies ran while one was open for 1% of the time, Pallas kernels for 2%

profile of v8, /device:TPU:1, one launch (start us, length us, event | category | flops | bytes accessed | tf_op | source)
XLA Modules:
  0.0 144.0 jit_solution(1185078758898006216)
XLA Ops:
  0.0 0.0 copy-start
  0.0 0.0 copy-start.2
  0.0 0.0 copy-start.3
  0.0 1.0 copy-done
  1.1 0.8 convert.10
  1.9 0.7 broadcast_in_dim.2
  2.6 15.6 %all-to-all-start = ((bf16[4,2,32,512]{3,2,1,0:T(8,128)(2,1)}), bf16[4,2,32,512]{3,2,1,0:T(8,128)(2,1)S(1)}, u32[]{:S(2)}, u32[]{:S(2)}) async-start(bf16[4,2,32,512]{3,2,1,0:T(8,128)(2,1)} %broadcast_in_dim.2), calls=%async_computation | async-start | bytes 524288 | tf_op jit(solution)/shard_map/all_to_all | solution.py:335
  18.3 0.8 pad_add_fusion.scan_ref
  19.0 5.5 %collective-permute-start = (s32[32]{0:T(128)S(1)}, s32[32]{0:T(128)S(1)}, u32[]{:S(2)}, u32[]{:S(2)}) collective-permute-start(s32[32]{0:T(128)S(1)} %pad_add_fusion.scan_ref), channel_id=1, source_target_pairs={{0,32},{32,64},{64,96},{96,128},{128,160},{160,192},{192,224},{224... | collective-permute-start | bytes 392 | tf_op jit(solution)/shard_map/ppermute | solution.py:327
  24.5 0.1 stack.46.meta_ref
  24.6 0.6 collective-permute-done.above_ref
  25.2 6.8 %all-to-all-done.packed_ref = bf16[4,2,32,512]{3,2,1,0:T(8,128)(2,1)S(1)} async-done(((bf16[4,2,32,512]{3,2,1,0:T(8,128)(2,1)}), bf16[4,2,32,512]{3,2,1,0:T(8,128)(2,1)S(1)}, u32[]{:S(2)}, u32[]{:S(2)}) %all-to-all-start) | async-done | bytes 262176 | tf_op jit(solution)/shard_map/all_to_all | solution.py:335
  32.0 1.1 cut.1
  33.2 3.1 %collective-permute-start.1 = (bf16[6,2,16,512]{3,2,1,0:T(8,128)(2,1)S(1)}, bf16[6,2,16,512]{3,2,1,0:T(8,128)(2,1)S(1)}, u32[]{:S(2)}, u32[]{:S(2)}) collective-permute-start(bf16[6,2,16,512]{3,2,1,0:T(8,128)(2,1)S(1)} %get-tuple-element.24), channel_id=1, source_target_pairs={{0,16},{16,0},{1,17},{17,1},{2,18},{18,2},{3,19},{19,3},{4,20},{20... | collective-permute-start | bytes 589832 | tf_op jit(solution)/shard_map/ppermute | solution.py:343
  36.3 7.9 %collective-permute-start.2 = (bf16[2,64,256]{2,1,0:T(8,128)(2,1)S(1)}, bf16[2,64,256]{2,1,0:T(8,128)(2,1)S(1)}, u32[]{:S(2)}, u32[]{:S(2)}) collective-permute-start(bf16[2,64,256]{2,1,0:T(8,128)(2,1)S(1)} %get-tuple-element.22), channel_id=1, source_target_pairs={{32,0},{64,32},{96,64},{128,96},{160,128},{192,160},{224,192},{256... | collective-permute-start | bytes 196616 | tf_op jit(solution)/shard_map/ppermute | solution.py:344
  44.3 1.3 collective-permute-start.3
  45.6 3.1 %collective-permute-done.2.below0_ref = bf16[2,64,256]{2,1,0:T(8,128)(2,1)S(1)} collective-permute-done((bf16[2,64,256]{2,1,0:T(8,128)(2,1)S(1)}, bf16[2,64,256]{2,1,0:T(8,128)(2,1)S(1)}, u32[]{:S(2)}, u32[]{:S(2)}) %collective-permute-start.2) | collective-permute-done | bytes 65568 | tf_op jit(solution)/shard_map/ppermute | solution.py:344
  48.7 0.0 collective-permute-done.3.below1_ref
  48.7 0.0 collective-permute-done.1.swapped_ref
  48.8 4.6 %collective-permute-start.6 = (bf16[8,2,16,512]{3,2,1,0:T(8,128)(2,1)S(1)}, bf16[8,2,16,512]{3,2,1,0:T(8,128)(2,1)S(1)}, u32[]{:S(2)}, u32[]{:S(2)}) collective-permute-start(bf16[8,2,16,512]{3,2,1,0:T(8,128)(2,1)S(1)} %get-tuple-element.38), channel_id=1, source_target_pairs={{0,384},{128,0},{256,128},{384,256},{1,385},{129,1},{257,129},{385... | collective-permute-start | bytes 786440 | tf_op jit(solution)/shard_map/ppermute | solution.py:350
  53.4 2.3 %collective-permute-start.5 = (bf16[8,2,16,512]{3,2,1,0:T(8,128)(2,1)S(1)}, bf16[8,2,16,512]{3,2,1,0:T(8,128)(2,1)S(1)}, u32[]{:S(2)}, u32[]{:S(2)}) collective-permute-start(bf16[8,2,16,512]{3,2,1,0:T(8,128)(2,1)S(1)} %get-tuple-element.38), channel_id=1, source_target_pairs={{0,256},{128,384},{256,0},{384,128},{1,257},{129,385},{257,1},{385... | collective-permute-start | bytes 786440 | tf_op jit(solution)/shard_map/ppermute | solution.py:350
  55.7 2.6 %collective-permute-start.4 = (bf16[8,2,16,512]{3,2,1,0:T(8,128)(2,1)S(1)}, bf16[8,2,16,512]{3,2,1,0:T(8,128)(2,1)S(1)}, u32[]{:S(2)}, u32[]{:S(2)}) collective-permute-start(bf16[8,2,16,512]{3,2,1,0:T(8,128)(2,1)S(1)} %get-tuple-element.38), channel_id=1, source_target_pairs={{0,128},{128,256},{256,384},{384,0},{1,129},{129,257},{257,385},{3... | collective-permute-start | bytes 786440 | tf_op jit(solution)/shard_map/ppermute | solution.py:350
  58.3 0.8 touch.1
  59.1 13.9 %all-gather = bf16[8,80,256]{2,1,0:T(8,128)(2,1)S(1)} all-gather(bf16[2,80,256]{2,1,0:T(8,128)(2,1)S(1)} %touch.1), channel_id=2, replica_groups=mesh['y'=4,'xh'=2,'c'=2,'xl'=2,'zq'=4,'zr'=4] {'zr'}, dimensions={0}, use_global_device_ids=true | all-gather | bytes 409600 | tf_op jit(solution)/shard_map/all_gather | solution.py:357
  73.0 0.0 collective-permute-done.6
  73.0 0.0 collective-permute-done.5
  73.0 0.0 collective-permute-done.4
  73.0 0.1 pad_maximum_fusion.here_ref
  73.1 0.0 copy-start.1
  73.1 4.0 %collective-permute-start.7 = (bf16[4,8,2,16,512]{4,3,2,1,0:T(8,128)(2,1)S(1)}, bf16[4,8,2,16,512]{4,3,2,1,0:T(8,128)(2,1)S(1)}, u32[]{:S(2)}, u32[]{:S(2)}) collective-permute-start(bf16[4,8,2,16,512]{4,3,2,1,0:T(8,128)(2,1)S(1)} %pad_maximum_fusion.here_ref), channel_id=1, source_target_pairs={{0,32},{32,0},{1,33},{33,1},{2,34},{34,2},{3,35},{35,3},{4,36},{36... | collective-permute-start | bytes 3145736 | tf_op jit(solution)/shard_map/ppermute | solution.py:360
  77.2 0.0 copy-done.2
  77.2 1.6 %begin.1 = (bf16[8,128,512]{2,1,0:T(8,128)(2,1)S(1)}, f32[2,128,256]{2,1,0:T(8,128)S(1)}) custom-call(s32[7]{0:T(128)S(1)} %stack.46.meta_ref, s32[32]{0:T(128)S(1)} %pad_add_fusion.scan_ref, bf16[4,2,80,256]{3,2,1,0:T(8,128)(2,1)S(1)} %bitcast.21, bf16[4,8,2,16,512]{4,3,2,1,0:T(8,128)(2,1)S(1)} %pad_maximum_fusion.here_ref, bf16[512,512]{1,0:T(8,128)(2,1)S(1)} %copy-done.2), custom_call_target="tpu_custom_call" | custom-call | flops 536870912 | bytes 4194304 | tf_op jit(solution)/shard_map/begin/pallas_call | solution.py:286
  78.8 0.6 collective-permute-done.7.there_ref
  79.5 0.0 copy-done.3
  79.5 2.7 %forward.1 = (f32[8,512,256]{2,1,0:T(8,128)S(1)}, bf16[256,256]{1,0:T(8,128)(2,1)S(1)}) custom-call(s32[7]{0:T(128)S(1)} %stack.46.meta_ref, bf16[8,128,512]{2,1,0:T(8,128)(2,1)S(1)} %get-tuple-element.33.half_ref, f32[2,128,256]{2,1,0:T(8,128)S(1)} %get-tuple-element.34.patch_ref, bf16[4,8,2,16,512]{4,3,2,1,0:T(8,128)(2,1)S(1)} %collective-permute-done.7.there_ref, ...), custom_call_target="tpu_custom_call" | custom-call | flops 1610612736 | bytes 4194304 | tf_op jit(solution)/shard_map/forward/pallas_call | solution.py:286
  82.1 13.0 %all-gather.1 = bf16[1024,256]{1,0:T(8,128)(2,1)S(1)} all-gather(bf16[256,256]{1,0:T(8,128)(2,1)S(1)} %get-tuple-element.36), channel_id=3, replica_groups=mesh['y'=4,'xh'=2,'c'=2,'xl'=2,'zq'=4,'zr'=4] {'zr'}, dimensions={0}, use_global_device_ids=true | all-gather | bytes 655360 | tf_op jit(solution)/shard_map/all_gather | solution.py:379
  95.2 0.0 copy-done.1
  95.2 0.0 copy-start.4
  95.2 3.9 %backward.1 = bf16[4,2,80,256]{3,2,1,0:T(8,128)(2,1)S(1)} custom-call(s32[7]{0:T(128)S(1)} %stack.46.meta_ref, s32[32]{0:T(128)S(1)} %pad_add_fusion.scan_ref, f32[8,512,256]{2,1,0:T(8,128)S(1)} %get-tuple-element.35.spec_ref, bf16[4,256,256]{2,1,0:T(8,128)(2,1)S(1)} %bitcast.20, f32[1,8,256,256]{3,2,1,0:T(8,128)S(1)} %copy-done.1, ...), custom_call_target="tpu_custom_call" | custom-call | flops 2147483648 | bytes 4194304 | tf_op jit(solution)/shard_map/backward/pallas_call | solution.py:286
  99.1 9.9 %all_to_all.15 = bf16[4,2,80,256]{3,2,1,0:T(8,128)(2,1)S(1)} all-to-all(bf16[4,2,80,256]{3,2,1,0:T(8,128)(2,1)S(1)} %backward.1), channel_id=1, replica_groups=mesh['y'=4,'xh'=2,'c'=2,'xl'=2,'zq'=4,'zr'=4] {'zr'}, dimensions={0} | all-to-all | bytes 655360 | tf_op jit(solution)/shard_map/all_to_all | solution.py:386
  109.0 1.3 collective-permute-start.10
  110.3 8.4 %collective-permute-start.9 = (bf16[2,80,256]{2,1,0:T(8,128)(2,1)S(1)}, bf16[2,80,256]{2,1,0:T(8,128)(2,1)S(1)}, u32[]{:S(2)}, u32[]{:S(2)}) collective-permute-start(bf16[2,80,256]{2,1,0:T(8,128)(2,1)S(1)} %fusion.own_ref), channel_id=1, source_target_pairs={{0,32},{32,64},{64,96},{96,128},{128,160},{160,192},{192,224},{224... | collective-permute-start | bytes 245768 | tf_op jit(solution)/shard_map/ppermute | solution.py:390
  118.7 1.9 %collective-permute-start.8 = (bf16[2,80,256]{2,1,0:T(8,128)(2,1)S(1)}, bf16[2,80,256]{2,1,0:T(8,128)(2,1)S(1)}, u32[]{:S(2)}, u32[]{:S(2)}) collective-permute-start(bf16[2,80,256]{2,1,0:T(8,128)(2,1)S(1)} %fusion.own_ref), channel_id=1, source_target_pairs={{0,16},{16,0},{1,17},{17,1},{2,18},{18,2},{3,19},{19,3},{4,20},{20... | collective-permute-start | bytes 245768 | tf_op jit(solution)/shard_map/ppermute | solution.py:389
  120.6 0.0 collective-permute-done.10.lower_ref
  120.6 0.0 collective-permute-done.9.upper_ref
  120.6 3.2 %collective-permute-done.8.partner_ref = bf16[2,80,256]{2,1,0:T(8,128)(2,1)S(1)} collective-permute-done((bf16[2,80,256]{2,1,0:T(8,128)(2,1)S(1)}, bf16[2,80,256]{2,1,0:T(8,128)(2,1)S(1)}, u32[]{:S(2)}, u32[]{:S(2)}) %collective-permute-start.8) | collective-permute-done | bytes 81952 | tf_op jit(solution)/shard_map/ppermute | solution.py:389
  123.9 1.3 place.1
  125.2 18.1 %all_to_all.16 = bf16[4,2,16,512]{3,2,1,0:T(8,128)(2,1)S(1)} all-to-all(bf16[4,2,16,512]{3,2,1,0:T(8,128)(2,1)S(1)} %place.1), channel_id=1, replica_groups=mesh['y'=4,'xh'=2,'c'=2,'xl'=2,'zq'=4,'zr'=4] {'zq'}, dimensions={0} | all-to-all | bytes 262144 | tf_op jit(solution)/shard_map/all_to_all | solution.py:396
  143.3 0.0 copy-done.4
  143.3 0.6 multiply_subtract_fusion
  (8 shorter events, 0.1 us)
Async XLA Ops:
  0.0 1.0 copy-start
  0.0 77.2 %copy-start.2 = (bf16[512,512]{1,0:T(8,128)(2,1)S(1)}, bf16[512,512]{1,0:T(8,128)(2,1)}, u32[]{:S(2)}) copy-start(bf16[512,512]{1,0:T(8,128)(2,1)} %constant.44.clone.right_ref) | copy-start | bytes 1572868
  0.0 79.5 %copy-start.3 = (bf16[512,512]{1,0:T(8,128)(2,1)S(1)}, bf16[512,512]{1,0:T(8,128)(2,1)}, u32[]{:S(2)}) copy-start(bf16[512,512]{1,0:T(8,128)(2,1)} %constant.45.clone.left_ref) | copy-start | bytes 1572868
  2.6 29.4 %all-to-all-start = ((bf16[4,2,32,512]{3,2,1,0:T(8,128)(2,1)}), bf16[4,2,32,512]{3,2,1,0:T(8,128)(2,1)S(1)}, u32[]{:S(2)}, u32[]{:S(2)}) async-start(bf16[4,2,32,512]{3,2,1,0:T(8,128)(2,1)} %broadcast_in_dim.2), calls=%async_computation | async-start | bytes 524288 | tf_op jit(solution)/shard_map/all_to_all | solution.py:335
  19.0 6.2 %collective-permute-start = (s32[32]{0:T(128)S(1)}, s32[32]{0:T(128)S(1)}, u32[]{:S(2)}, u32[]{:S(2)}) collective-permute-start(s32[32]{0:T(128)S(1)} %pad_add_fusion.scan_ref), channel_id=1, source_target_pairs={{0,32},{32,64},{64,96},{96,128},{128,160},{160,192},{192,224},{224... | collective-permute-start | bytes 392 | tf_op jit(solution)/shard_map/ppermute | solution.py:327
  33.2 15.5 %collective-permute-start.1 = (bf16[6,2,16,512]{3,2,1,0:T(8,128)(2,1)S(1)}, bf16[6,2,16,512]{3,2,1,0:T(8,128)(2,1)S(1)}, u32[]{:S(2)}, u32[]{:S(2)}) collective-permute-start(bf16[6,2,16,512]{3,2,1,0:T(8,128)(2,1)S(1)} %get-tuple-element.24), channel_id=1, source_target_pairs={{0,16},{16,0},{1,17},{17,1},{2,18},{18,2},{3,19},{19,3},{4,20},{20... | collective-permute-start | bytes 589832 | tf_op jit(solution)/shard_map/ppermute | solution.py:343
  36.3 12.4 %collective-permute-start.2 = (bf16[2,64,256]{2,1,0:T(8,128)(2,1)S(1)}, bf16[2,64,256]{2,1,0:T(8,128)(2,1)S(1)}, u32[]{:S(2)}, u32[]{:S(2)}) collective-permute-start(bf16[2,64,256]{2,1,0:T(8,128)(2,1)S(1)} %get-tuple-element.22), channel_id=1, source_target_pairs={{32,0},{64,32},{96,64},{128,96},{160,128},{192,160},{224,192},{256... | collective-permute-start | bytes 196616 | tf_op jit(solution)/shard_map/ppermute | solution.py:344
  44.3 4.5 %collective-permute-start.3 = (bf16[2,64,256]{2,1,0:T(8,128)(2,1)S(1)}, bf16[2,64,256]{2,1,0:T(8,128)(2,1)S(1)}, u32[]{:S(2)}, u32[]{:S(2)}) collective-permute-start(bf16[2,64,256]{2,1,0:T(8,128)(2,1)S(1)} %get-tuple-element.23), channel_id=1, source_target_pairs={{32,16},{64,48},{96,80},{128,112},{160,144},{192,176},{224,208},{2... | collective-permute-start | bytes 196616 | tf_op jit(solution)/shard_map/ppermute | solution.py:345
  48.8 24.2 %collective-permute-start.6 = (bf16[8,2,16,512]{3,2,1,0:T(8,128)(2,1)S(1)}, bf16[8,2,16,512]{3,2,1,0:T(8,128)(2,1)S(1)}, u32[]{:S(2)}, u32[]{:S(2)}) collective-permute-start(bf16[8,2,16,512]{3,2,1,0:T(8,128)(2,1)S(1)} %get-tuple-element.38), channel_id=1, source_target_pairs={{0,384},{128,0},{256,128},{384,256},{1,385},{129,1},{257,129},{385... | collective-permute-start | bytes 786440 | tf_op jit(solution)/shard_map/ppermute | solution.py:350
  53.4 19.6 %collective-permute-start.5 = (bf16[8,2,16,512]{3,2,1,0:T(8,128)(2,1)S(1)}, bf16[8,2,16,512]{3,2,1,0:T(8,128)(2,1)S(1)}, u32[]{:S(2)}, u32[]{:S(2)}) collective-permute-start(bf16[8,2,16,512]{3,2,1,0:T(8,128)(2,1)S(1)} %get-tuple-element.38), channel_id=1, source_target_pairs={{0,256},{128,384},{256,0},{384,128},{1,257},{129,385},{257,1},{385... | collective-permute-start | bytes 786440 | tf_op jit(solution)/shard_map/ppermute | solution.py:350
  55.7 17.3 %collective-permute-start.4 = (bf16[8,2,16,512]{3,2,1,0:T(8,128)(2,1)S(1)}, bf16[8,2,16,512]{3,2,1,0:T(8,128)(2,1)S(1)}, u32[]{:S(2)}, u32[]{:S(2)}) collective-permute-start(bf16[8,2,16,512]{3,2,1,0:T(8,128)(2,1)S(1)} %get-tuple-element.38), channel_id=1, source_target_pairs={{0,128},{128,256},{256,384},{384,0},{1,129},{129,257},{257,385},{3... | collective-permute-start | bytes 786440 | tf_op jit(solution)/shard_map/ppermute | solution.py:350
  73.1 22.0 %copy-start.1 = (f32[1,8,256,256]{3,2,1,0:T(8,128)S(1)}, f32[1,8,256,256]{3,2,1,0:T(8,128)}, u32[]{:S(2)}) copy-start(f32[1,8,256,256]{3,2,1,0:T(8,128)} %amplitude_ref.1) | copy-start | bytes 6291460
  73.1 6.3 %collective-permute-start.7 = (bf16[4,8,2,16,512]{4,3,2,1,0:T(8,128)(2,1)S(1)}, bf16[4,8,2,16,512]{4,3,2,1,0:T(8,128)(2,1)S(1)}, u32[]{:S(2)}, u32[]{:S(2)}) collective-permute-start(bf16[4,8,2,16,512]{4,3,2,1,0:T(8,128)(2,1)S(1)} %pad_maximum_fusion.here_ref), channel_id=1, source_target_pairs={{0,32},{32,0},{1,33},{33,1},{2,34},{34,2},{3,35},{35,3},{4,36},{36... | collective-permute-start | bytes 3145736 | tf_op jit(solution)/shard_map/ppermute | solution.py:360
  95.2 48.1 %copy-start.4 = (f32[2,16,512]{2,1,0:T(8,128)S(1)}, f32[2,16,512]{2,1,0:T(8,128)}, u32[]{:S(2)}) copy-start(f32[2,16,512]{2,1,0:T(8,128)} %param.8) | copy-start | bytes 196612
  109.0 11.6 %collective-permute-start.10 = (bf16[2,80,256]{2,1,0:T(8,128)(2,1)S(1)}, bf16[2,80,256]{2,1,0:T(8,128)(2,1)S(1)}, u32[]{:S(2)}, u32[]{:S(2)}) collective-permute-start(bf16[2,80,256]{2,1,0:T(8,128)(2,1)S(1)} %fusion.own_ref), channel_id=1, source_target_pairs={{16,32},{48,64},{80,96},{112,128},{144,160},{176,192},{208,224},{2... | collective-permute-start | bytes 245768 | tf_op jit(solution)/shard_map/ppermute | solution.py:391
  110.3 10.3 %collective-permute-start.9 = (bf16[2,80,256]{2,1,0:T(8,128)(2,1)S(1)}, bf16[2,80,256]{2,1,0:T(8,128)(2,1)S(1)}, u32[]{:S(2)}, u32[]{:S(2)}) collective-permute-start(bf16[2,80,256]{2,1,0:T(8,128)(2,1)S(1)} %fusion.own_ref), channel_id=1, source_target_pairs={{0,32},{32,64},{64,96},{96,128},{128,160},{160,192},{192,224},{224... | collective-permute-start | bytes 245768 | tf_op jit(solution)/shard_map/ppermute | solution.py:390
  118.7 5.2 %collective-permute-start.8 = (bf16[2,80,256]{2,1,0:T(8,128)(2,1)S(1)}, bf16[2,80,256]{2,1,0:T(8,128)(2,1)S(1)}, u32[]{:S(2)}, u32[]{:S(2)}) collective-permute-start(bf16[2,80,256]{2,1,0:T(8,128)(2,1)S(1)} %fusion.own_ref), channel_id=1, source_target_pairs={{0,16},{16,0},{1,17},{17,1},{2,18},{18,2},{3,19},{19,3},{4,20},{20... | collective-permute-start | bytes 245768 | tf_op jit(solution)/shard_map/ppermute | solution.py:389

commit v9 on v8

--- a/solution.py
+++ b/solution.py
@@ -176,11 +176,10 @@
         patch.append(jnp.where(core == 0, even, odd))
         patch_ref[part] = jnp.where(core == 0, odd, even)
     rows = half_ref.shape[1]
-    for start in range(0, half_ref.shape[0], AT_ONCE):
-        modes = range(start, start + AT_ONCE)
-        half = half_product(here_ref, patch, meta_ref, modes, right_ref[...])
-        for i in range(AT_ONCE):
-            half_ref[start + i] = half[i * rows : (i + 1) * rows]
+    modes = range(half_ref.shape[0])
+    half = half_product(here_ref, patch, meta_ref, modes, right_ref[...])
+    for mode in modes:
+        half_ref[mode] = half[mode * rows : (mode + 1) * rows]
 
 
 def forward_kernel(

time: 145 us -> 145 us (level)
  no operation moved by 1% of the time
where the time goes in v9:
time: 145 us; the launch traced here: 144 us
  starting transfers between devices  58.6 us (40%)
  blocking collectives  54.9 us (38%)
  waiting for transfers between devices  14.5 us (10%)
  Pallas kernels  11.4 us (8%)
  other arithmetic  2.49 us (2%)
  local copies, waits for them, and re-layouts  1.88 us (1%)
    all_to_all x1, blocking collectives, on_device(): terms = lax.all_to_all(half_sum, 'zq', 0, 0, tiled=True)  18.1 us
    all_to_all x1, starting transfers between devices, on_device(): packed = lax.all_to_all(packed, 'zq', 0, 0, tiled=True)  15.6 us
    all_gather x1, blocking collectives, on_device(): touched = lax.all_gather(touched, 'zr', axis=0)  13.9 us
    all_gather x1, blocking collectives, on_device(): powers = lax.all_gather(power, 'zr', axis=0)  13 us
    pallas_call x6, Pallas kernels, call(): pl.pallas_call(kernel, grid_spec=pltpu.PrefetchScalarGridSpec(num_scalar_...  11.4 us
    all_to_all x1, blocking collectives, on_device(): pieces = lax.all_to_all(pieces, 'zr', 0, 0, tiled=True)  9.86 us
    ppermute x3, starting transfers between devices, on_device(): lax.ppermute(part_modes, 'y', [(i, (i + d) % ups) for i in range(ups)])  9.5 us
    ppermute x1, starting transfers between devices, on_device(): above0 = lax.ppermute(term, axes, down_first)  8.38 us
  transfers between devices with their start and end apart: 12, of which 5 were waited for; matrix products, arithmetic and copies ran while one was open for 1% of the time, Pallas kernels for 2%

profile of v9, /device:TPU:1, one launch (start us, length us, event | category | flops | bytes accessed | tf_op | source)
XLA Modules:
  0.0 144.0 jit_solution(13015321415877785847)
XLA Ops:
  0.0 0.0 copy-start
  0.0 0.0 copy-start.2
  0.0 0.0 copy-start.3
  0.0 1.0 copy-done
  1.1 0.8 convert.10
  1.9 0.7 broadcast_in_dim.2
  2.6 15.6 %all-to-all-start = ((bf16[4,2,32,512]{3,2,1,0:T(8,128)(2,1)}), bf16[4,2,32,512]{3,2,1,0:T(8,128)(2,1)S(1)}, u32[]{:S(2)}, u32[]{:S(2)}) async-start(bf16[4,2,32,512]{3,2,1,0:T(8,128)(2,1)} %broadcast_in_dim.2), calls=%async_computation | async-start | bytes 524288 | tf_op jit(solution)/shard_map/all_to_all | solution.py:334
  18.3 0.8 pad_add_fusion.scan_ref
  19.0 5.5 %collective-permute-start = (s32[32]{0:T(128)S(1)}, s32[32]{0:T(128)S(1)}, u32[]{:S(2)}, u32[]{:S(2)}) collective-permute-start(s32[32]{0:T(128)S(1)} %pad_add_fusion.scan_ref), channel_id=1, source_target_pairs={{0,32},{32,64},{64,96},{96,128},{128,160},{160,192},{192,224},{224... | collective-permute-start | bytes 392 | tf_op jit(solution)/shard_map/ppermute | solution.py:326
  24.5 0.1 stack.46.meta_ref
  24.6 0.6 collective-permute-done.above_ref
  25.2 6.8 %all-to-all-done.packed_ref = bf16[4,2,32,512]{3,2,1,0:T(8,128)(2,1)S(1)} async-done(((bf16[4,2,32,512]{3,2,1,0:T(8,128)(2,1)}), bf16[4,2,32,512]{3,2,1,0:T(8,128)(2,1)S(1)}, u32[]{:S(2)}, u32[]{:S(2)}) %all-to-all-start) | async-done | bytes 262176 | tf_op jit(solution)/shard_map/all_to_all | solution.py:334
  32.0 1.1 cut.1
  33.2 3.1 %collective-permute-start.1 = (bf16[6,2,16,512]{3,2,1,0:T(8,128)(2,1)S(1)}, bf16[6,2,16,512]{3,2,1,0:T(8,128)(2,1)S(1)}, u32[]{:S(2)}, u32[]{:S(2)}) collective-permute-start(bf16[6,2,16,512]{3,2,1,0:T(8,128)(2,1)S(1)} %get-tuple-element.24), channel_id=1, source_target_pairs={{0,16},{16,0},{1,17},{17,1},{2,18},{18,2},{3,19},{19,3},{4,20},{20... | collective-permute-start | bytes 589832 | tf_op jit(solution)/shard_map/ppermute | solution.py:342
  36.3 7.9 %collective-permute-start.2 = (bf16[2,64,256]{2,1,0:T(8,128)(2,1)S(1)}, bf16[2,64,256]{2,1,0:T(8,128)(2,1)S(1)}, u32[]{:S(2)}, u32[]{:S(2)}) collective-permute-start(bf16[2,64,256]{2,1,0:T(8,128)(2,1)S(1)} %get-tuple-element.22), channel_id=1, source_target_pairs={{32,0},{64,32},{96,64},{128,96},{160,128},{192,160},{224,192},{256... | collective-permute-start | bytes 196616 | tf_op jit(solution)/shard_map/ppermute | solution.py:343
  44.3 1.3 collective-permute-start.3
  45.6 3.1 %collective-permute-done.2.below0_ref = bf16[2,64,256]{2,1,0:T(8,128)(2,1)S(1)} collective-permute-done((bf16[2,64,256]{2,1,0:T(8,128)(2,1)S(1)}, bf16[2,64,256]{2,1,0:T(8,128)(2,1)S(1)}, u32[]{:S(2)}, u32[]{:S(2)}) %collective-permute-start.2) | collective-permute-done | bytes 65568 | tf_op jit(solution)/shard_map/ppermute | solution.py:343
  48.7 0.0 collective-permute-done.3.below1_ref
  48.7 0.0 collective-permute-done.1.swapped_ref
  48.8 4.6 %collective-permute-start.6 = (bf16[8,2,16,512]{3,2,1,0:T(8,128)(2,1)S(1)}, bf16[8,2,16,512]{3,2,1,0:T(8,128)(2,1)S(1)}, u32[]{:S(2)}, u32[]{:S(2)}) collective-permute-start(bf16[8,2,16,512]{3,2,1,0:T(8,128)(2,1)S(1)} %get-tuple-element.38), channel_id=1, source_target_pairs={{0,384},{128,0},{256,128},{384,256},{1,385},{129,1},{257,129},{385... | collective-permute-start | bytes 786440 | tf_op jit(solution)/shard_map/ppermute | solution.py:349
  53.4 2.3 %collective-permute-start.5 = (bf16[8,2,16,512]{3,2,1,0:T(8,128)(2,1)S(1)}, bf16[8,2,16,512]{3,2,1,0:T(8,128)(2,1)S(1)}, u32[]{:S(2)}, u32[]{:S(2)}) collective-permute-start(bf16[8,2,16,512]{3,2,1,0:T(8,128)(2,1)S(1)} %get-tuple-element.38), channel_id=1, source_target_pairs={{0,256},{128,384},{256,0},{384,128},{1,257},{129,385},{257,1},{385... | collective-permute-start | bytes 786440 | tf_op jit(solution)/shard_map/ppermute | solution.py:349
  55.7 2.6 %collective-permute-start.4 = (bf16[8,2,16,512]{3,2,1,0:T(8,128)(2,1)S(1)}, bf16[8,2,16,512]{3,2,1,0:T(8,128)(2,1)S(1)}, u32[]{:S(2)}, u32[]{:S(2)}) collective-permute-start(bf16[8,2,16,512]{3,2,1,0:T(8,128)(2,1)S(1)} %get-tuple-element.38), channel_id=1, source_target_pairs={{0,128},{128,256},{256,384},{384,0},{1,129},{129,257},{257,385},{3... | collective-permute-start | bytes 786440 | tf_op jit(solution)/shard_map/ppermute | solution.py:349
  58.3 0.8 touch.1
  59.1 13.9 %all-gather = bf16[8,80,256]{2,1,0:T(8,128)(2,1)S(1)} all-gather(bf16[2,80,256]{2,1,0:T(8,128)(2,1)S(1)} %touch.1), channel_id=2, replica_groups=mesh['y'=4,'xh'=2,'c'=2,'xl'=2,'zq'=4,'zr'=4] {'zr'}, dimensions={0}, use_global_device_ids=true | all-gather | bytes 409600 | tf_op jit(solution)/shard_map/all_gather | solution.py:356
  73.0 0.0 collective-permute-done.6
  73.0 0.0 collective-permute-done.5
  73.0 0.0 collective-permute-done.4
  73.0 0.1 pad_maximum_fusion.here_ref
  73.1 0.0 copy-start.1
  73.1 4.0 %collective-permute-start.7 = (bf16[4,8,2,16,512]{4,3,2,1,0:T(8,128)(2,1)S(1)}, bf16[4,8,2,16,512]{4,3,2,1,0:T(8,128)(2,1)S(1)}, u32[]{:S(2)}, u32[]{:S(2)}) collective-permute-start(bf16[4,8,2,16,512]{4,3,2,1,0:T(8,128)(2,1)S(1)} %pad_maximum_fusion.here_ref), channel_id=1, source_target_pairs={{0,32},{32,0},{1,33},{33,1},{2,34},{34,2},{3,35},{35,3},{4,36},{36... | collective-permute-start | bytes 3145736 | tf_op jit(solution)/shard_map/ppermute | solution.py:359
  77.2 0.0 copy-done.2
  77.2 1.6 %begin.1 = (bf16[8,128,512]{2,1,0:T(8,128)(2,1)S(1)}, f32[2,128,256]{2,1,0:T(8,128)S(1)}) custom-call(s32[7]{0:T(128)S(1)} %stack.46.meta_ref, s32[32]{0:T(128)S(1)} %pad_add_fusion.scan_ref, bf16[4,2,80,256]{3,2,1,0:T(8,128)(2,1)S(1)} %bitcast.21, bf16[4,8,2,16,512]{4,3,2,1,0:T(8,128)(2,1)S(1)} %pad_maximum_fusion.here_ref, bf16[512,512]{1,0:T(8,128)(2,1)S(1)} %copy-done.2), custom_call_target="tpu_custom_call" | custom-call | flops 536870912 | bytes 4194304 | tf_op jit(solution)/shard_map/begin/pallas_call | solution.py:285
  78.8 0.6 collective-permute-done.7.there_ref
  79.5 0.0 copy-done.3
  79.5 2.7 %forward.1 = (f32[8,512,256]{2,1,0:T(8,128)S(1)}, bf16[256,256]{1,0:T(8,128)(2,1)S(1)}) custom-call(s32[7]{0:T(128)S(1)} %stack.46.meta_ref, bf16[8,128,512]{2,1,0:T(8,128)(2,1)S(1)} %get-tuple-element.33.half_ref, f32[2,128,256]{2,1,0:T(8,128)S(1)} %get-tuple-element.34.patch_ref, bf16[4,8,2,16,512]{4,3,2,1,0:T(8,128)(2,1)S(1)} %collective-permute-done.7.there_ref, ...), custom_call_target="tpu_custom_call" | custom-call | flops 1610612736 | bytes 4194304 | tf_op jit(solution)/shard_map/forward/pallas_call | solution.py:285
  82.1 13.0 %all-gather.1 = bf16[1024,256]{1,0:T(8,128)(2,1)S(1)} all-gather(bf16[256,256]{1,0:T(8,128)(2,1)S(1)} %get-tuple-element.36), channel_id=3, replica_groups=mesh['y'=4,'xh'=2,'c'=2,'xl'=2,'zq'=4,'zr'=4] {'zr'}, dimensions={0}, use_global_device_ids=true | all-gather | bytes 655360 | tf_op jit(solution)/shard_map/all_gather | solution.py:378
  95.2 0.0 copy-done.1
  95.2 0.0 copy-start.4
  95.2 3.9 %backward.1 = bf16[4,2,80,256]{3,2,1,0:T(8,128)(2,1)S(1)} custom-call(s32[7]{0:T(128)S(1)} %stack.46.meta_ref, s32[32]{0:T(128)S(1)} %pad_add_fusion.scan_ref, f32[8,512,256]{2,1,0:T(8,128)S(1)} %get-tuple-element.35.spec_ref, bf16[4,256,256]{2,1,0:T(8,128)(2,1)S(1)} %bitcast.20, f32[1,8,256,256]{3,2,1,0:T(8,128)S(1)} %copy-done.1, ...), custom_call_target="tpu_custom_call" | custom-call | flops 2147483648 | bytes 4194304 | tf_op jit(solution)/shard_map/backward/pallas_call | solution.py:285
  99.1 9.9 %all_to_all.15 = bf16[4,2,80,256]{3,2,1,0:T(8,128)(2,1)S(1)} all-to-all(bf16[4,2,80,256]{3,2,1,0:T(8,128)(2,1)S(1)} %backward.1), channel_id=1, replica_groups=mesh['y'=4,'xh'=2,'c'=2,'xl'=2,'zq'=4,'zr'=4] {'zr'}, dimensions={0} | all-to-all | bytes 655360 | tf_op jit(solution)/shard_map/all_to_all | solution.py:385
  109.0 1.3 collective-permute-start.10
  110.3 8.4 %collective-permute-start.9 = (bf16[2,80,256]{2,1,0:T(8,128)(2,1)S(1)}, bf16[2,80,256]{2,1,0:T(8,128)(2,1)S(1)}, u32[]{:S(2)}, u32[]{:S(2)}) collective-permute-start(bf16[2,80,256]{2,1,0:T(8,128)(2,1)S(1)} %fusion.own_ref), channel_id=1, source_target_pairs={{0,32},{32,64},{64,96},{96,128},{128,160},{160,192},{192,224},{224... | collective-permute-start | bytes 245768 | tf_op jit(solution)/shard_map/ppermute | solution.py:389
  118.7 1.9 %collective-permute-start.8 = (bf16[2,80,256]{2,1,0:T(8,128)(2,1)S(1)}, bf16[2,80,256]{2,1,0:T(8,128)(2,1)S(1)}, u32[]{:S(2)}, u32[]{:S(2)}) collective-permute-start(bf16[2,80,256]{2,1,0:T(8,128)(2,1)S(1)} %fusion.own_ref), channel_id=1, source_target_pairs={{0,16},{16,0},{1,17},{17,1},{2,18},{18,2},{3,19},{19,3},{4,20},{20... | collective-permute-start | bytes 245768 | tf_op jit(solution)/shard_map/ppermute | solution.py:388
  120.6 0.0 collective-permute-done.10.lower_ref
  120.6 0.0 collective-permute-done.9.upper_ref
  120.6 3.2 %collective-permute-done.8.partner_ref = bf16[2,80,256]{2,1,0:T(8,128)(2,1)S(1)} collective-permute-done((bf16[2,80,256]{2,1,0:T(8,128)(2,1)S(1)}, bf16[2,80,256]{2,1,0:T(8,128)(2,1)S(1)}, u32[]{:S(2)}, u32[]{:S(2)}) %collective-permute-start.8) | collective-permute-done | bytes 81952 | tf_op jit(solution)/shard_map/ppermute | solution.py:388
  123.9 1.3 place.1
  125.2 18.1 %all_to_all.16 = bf16[4,2,16,512]{3,2,1,0:T(8,128)(2,1)S(1)} all-to-all(bf16[4,2,16,512]{3,2,1,0:T(8,128)(2,1)S(1)} %place.1), channel_id=1, replica_groups=mesh['y'=4,'xh'=2,'c'=2,'xl'=2,'zq'=4,'zr'=4] {'zq'}, dimensions={0} | all-to-all | bytes 262144 | tf_op jit(solution)/shard_map/all_to_all | solution.py:395
  143.3 0.0 copy-done.4
  143.3 0.6 multiply_subtract_fusion
  (8 shorter events, 0.1 us)
Async XLA Ops:
  0.0 1.0 copy-start
  0.0 77.2 %copy-start.2 = (bf16[512,512]{1,0:T(8,128)(2,1)S(1)}, bf16[512,512]{1,0:T(8,128)(2,1)}, u32[]{:S(2)}) copy-start(bf16[512,512]{1,0:T(8,128)(2,1)} %constant.44.clone.right_ref) | copy-start | bytes 1572868
  0.0 79.5 %copy-start.3 = (bf16[512,512]{1,0:T(8,128)(2,1)S(1)}, bf16[512,512]{1,0:T(8,128)(2,1)}, u32[]{:S(2)}) copy-start(bf16[512,512]{1,0:T(8,128)(2,1)} %constant.45.clone.left_ref) | copy-start | bytes 1572868
  2.6 29.4 %all-to-all-start = ((bf16[4,2,32,512]{3,2,1,0:T(8,128)(2,1)}), bf16[4,2,32,512]{3,2,1,0:T(8,128)(2,1)S(1)}, u32[]{:S(2)}, u32[]{:S(2)}) async-start(bf16[4,2,32,512]{3,2,1,0:T(8,128)(2,1)} %broadcast_in_dim.2), calls=%async_computation | async-start | bytes 524288 | tf_op jit(solution)/shard_map/all_to_all | solution.py:334
  19.0 6.2 %collective-permute-start = (s32[32]{0:T(128)S(1)}, s32[32]{0:T(128)S(1)}, u32[]{:S(2)}, u32[]{:S(2)}) collective-permute-start(s32[32]{0:T(128)S(1)} %pad_add_fusion.scan_ref), channel_id=1, source_target_pairs={{0,32},{32,64},{64,96},{96,128},{128,160},{160,192},{192,224},{224... | collective-permute-start | bytes 392 | tf_op jit(solution)/shard_map/ppermute | solution.py:326
  33.2 15.5 %collective-permute-start.1 = (bf16[6,2,16,512]{3,2,1,0:T(8,128)(2,1)S(1)}, bf16[6,2,16,512]{3,2,1,0:T(8,128)(2,1)S(1)}, u32[]{:S(2)}, u32[]{:S(2)}) collective-permute-start(bf16[6,2,16,512]{3,2,1,0:T(8,128)(2,1)S(1)} %get-tuple-element.24), channel_id=1, source_target_pairs={{0,16},{16,0},{1,17},{17,1},{2,18},{18,2},{3,19},{19,3},{4,20},{20... | collective-permute-start | bytes 589832 | tf_op jit(solution)/shard_map/ppermute | solution.py:342
  36.3 12.4 %collective-permute-start.2 = (bf16[2,64,256]{2,1,0:T(8,128)(2,1)S(1)}, bf16[2,64,256]{2,1,0:T(8,128)(2,1)S(1)}, u32[]{:S(2)}, u32[]{:S(2)}) collective-permute-start(bf16[2,64,256]{2,1,0:T(8,128)(2,1)S(1)} %get-tuple-element.22), channel_id=1, source_target_pairs={{32,0},{64,32},{96,64},{128,96},{160,128},{192,160},{224,192},{256... | collective-permute-start | bytes 196616 | tf_op jit(solution)/shard_map/ppermute | solution.py:343
  44.3 4.5 %collective-permute-start.3 = (bf16[2,64,256]{2,1,0:T(8,128)(2,1)S(1)}, bf16[2,64,256]{2,1,0:T(8,128)(2,1)S(1)}, u32[]{:S(2)}, u32[]{:S(2)}) collective-permute-start(bf16[2,64,256]{2,1,0:T(8,128)(2,1)S(1)} %get-tuple-element.23), channel_id=1, source_target_pairs={{32,16},{64,48},{96,80},{128,112},{160,144},{192,176},{224,208},{2... | collective-permute-start | bytes 196616 | tf_op jit(solution)/shard_map/ppermute | solution.py:344
  48.8 24.2 %collective-permute-start.6 = (bf16[8,2,16,512]{3,2,1,0:T(8,128)(2,1)S(1)}, bf16[8,2,16,512]{3,2,1,0:T(8,128)(2,1)S(1)}, u32[]{:S(2)}, u32[]{:S(2)}) collective-permute-start(bf16[8,2,16,512]{3,2,1,0:T(8,128)(2,1)S(1)} %get-tuple-element.38), channel_id=1, source_target_pairs={{0,384},{128,0},{256,128},{384,256},{1,385},{129,1},{257,129},{385... | collective-permute-start | bytes 786440 | tf_op jit(solution)/shard_map/ppermute | solution.py:349
  53.4 19.6 %collective-permute-start.5 = (bf16[8,2,16,512]{3,2,1,0:T(8,128)(2,1)S(1)}, bf16[8,2,16,512]{3,2,1,0:T(8,128)(2,1)S(1)}, u32[]{:S(2)}, u32[]{:S(2)}) collective-permute-start(bf16[8,2,16,512]{3,2,1,0:T(8,128)(2,1)S(1)} %get-tuple-element.38), channel_id=1, source_target_pairs={{0,256},{128,384},{256,0},{384,128},{1,257},{129,385},{257,1},{385... | collective-permute-start | bytes 786440 | tf_op jit(solution)/shard_map/ppermute | solution.py:349
  55.7 17.3 %collective-permute-start.4 = (bf16[8,2,16,512]{3,2,1,0:T(8,128)(2,1)S(1)}, bf16[8,2,16,512]{3,2,1,0:T(8,128)(2,1)S(1)}, u32[]{:S(2)}, u32[]{:S(2)}) collective-permute-start(bf16[8,2,16,512]{3,2,1,0:T(8,128)(2,1)S(1)} %get-tuple-element.38), channel_id=1, source_target_pairs={{0,128},{128,256},{256,384},{384,0},{1,129},{129,257},{257,385},{3... | collective-permute-start | bytes 786440 | tf_op jit(solution)/shard_map/ppermute | solution.py:349
  73.1 22.0 %copy-start.1 = (f32[1,8,256,256]{3,2,1,0:T(8,128)S(1)}, f32[1,8,256,256]{3,2,1,0:T(8,128)}, u32[]{:S(2)}) copy-start(f32[1,8,256,256]{3,2,1,0:T(8,128)} %amplitude_ref.1) | copy-start | bytes 6291460
  73.1 6.3 %collective-permute-start.7 = (bf16[4,8,2,16,512]{4,3,2,1,0:T(8,128)(2,1)S(1)}, bf16[4,8,2,16,512]{4,3,2,1,0:T(8,128)(2,1)S(1)}, u32[]{:S(2)}, u32[]{:S(2)}) collective-permute-start(bf16[4,8,2,16,512]{4,3,2,1,0:T(8,128)(2,1)S(1)} %pad_maximum_fusion.here_ref), channel_id=1, source_target_pairs={{0,32},{32,0},{1,33},{33,1},{2,34},{34,2},{3,35},{35,3},{4,36},{36... | collective-permute-start | bytes 3145736 | tf_op jit(solution)/shard_map/ppermute | solution.py:359
  95.2 48.1 %copy-start.4 = (f32[2,16,512]{2,1,0:T(8,128)S(1)}, f32[2,16,512]{2,1,0:T(8,128)}, u32[]{:S(2)}) copy-start(f32[2,16,512]{2,1,0:T(8,128)} %param.8) | copy-start | bytes 196612
  109.0 11.6 %collective-permute-start.10 = (bf16[2,80,256]{2,1,0:T(8,128)(2,1)S(1)}, bf16[2,80,256]{2,1,0:T(8,128)(2,1)S(1)}, u32[]{:S(2)}, u32[]{:S(2)}) collective-permute-start(bf16[2,80,256]{2,1,0:T(8,128)(2,1)S(1)} %fusion.own_ref), channel_id=1, source_target_pairs={{16,32},{48,64},{80,96},{112,128},{144,160},{176,192},{208,224},{2... | collective-permute-start | bytes 245768 | tf_op jit(solution)/shard_map/ppermute | solution.py:390
  110.3 10.3 %collective-permute-start.9 = (bf16[2,80,256]{2,1,0:T(8,128)(2,1)S(1)}, bf16[2,80,256]{2,1,0:T(8,128)(2,1)S(1)}, u32[]{:S(2)}, u32[]{:S(2)}) collective-permute-start(bf16[2,80,256]{2,1,0:T(8,128)(2,1)S(1)} %fusion.own_ref), channel_id=1, source_target_pairs={{0,32},{32,64},{64,96},{96,128},{128,160},{160,192},{192,224},{224... | collective-permute-start | bytes 245768 | tf_op jit(solution)/shard_map/ppermute | solution.py:389
  118.7 5.2 %collective-permute-start.8 = (bf16[2,80,256]{2,1,0:T(8,128)(2,1)S(1)}, bf16[2,80,256]{2,1,0:T(8,128)(2,1)S(1)}, u32[]{:S(2)}, u32[]{:S(2)}) collective-permute-start(bf16[2,80,256]{2,1,0:T(8,128)(2,1)S(1)} %fusion.own_ref), channel_id=1, source_target_pairs={{0,16},{16,0},{1,17},{17,1},{2,18},{18,2},{3,19},{19,3},{4,20},{20... | collective-permute-start | bytes 245768 | tf_op jit(solution)/shard_map/ppermute | solution.py:388
